TPU v7x, 32 devices: a whole 2x2x4 slice. The times are simulated.
32 devices in a mesh: pipe: 4 (over y, x), ctx: 8 (over z, core).
Axes of the slice: x: 2, y: 2, z: 4, core: 2. Of those that a mesh axis runs over, the one named last changes fastest.
Arguments:
- x_in: bfloat16 [4, 512, 8192], P('pipe', 'ctx'), may hold values from -6 to 6
- z_in: bfloat16 [4, 512, 8192], P('pipe', 'ctx'), may hold values from -6 to 6
- bc_in: bfloat16 [4, 512, 1024], P('pipe', 'ctx'), may hold values from -6 to 6
- dt_raw: bfloat16 [4, 512, 128], P('pipe', 'ctx'), may hold values from -3.2 to 3.2
- a_log: float32 [4, 128], P('pipe'), may hold values from -12 to 3
- dt_bias: float32 [4, 128], P('pipe'), may hold values from -3.8 to -3
- d_skip: float32 [4, 128], P('pipe'), may hold values from 0.5 to 1.5
- conv_x: bfloat16 [4, 4, 8192], P('pipe'), may hold values from -3 to 3
- conv_bc: bfloat16 [4, 4, 1024], P('pipe'), may hold values from -3 to 3
- norm_gain: float32 [4, 8192], P('pipe'), may hold values from 0.5 to 1.5
- seg_ids: int32 [4, 512], P('pipe', 'ctx'), may hold values from 0 to 3, never falling along the last dimension, each value on 1 to 256 neighbouring positions
- query: bfloat16 [4, 512, 2048], P('pipe', 'ctx'), may hold values from -192 to 192
- keys: bfloat16 [4, 512, 256], P('pipe', 'ctx'), may hold values from -6 to 6
- values: bfloat16 [4, 512, 256], P('pipe', 'ctx'), may hold values from -6 to 6
Outputs:
- mamba_out: bfloat16 [4, 512, 8192], P('pipe', 'ctx')
- handoff: bfloat16 [4, 512, 2048], P('pipe', 'ctx')
Inputs may be any that keep to these rules, and one draw needn't show every extreme that they name: `seg_ids`: segment numbers never fall along a section's sequence; no segment is longer than 256 positions, and one has exactly that many.
All inputs are finite; a program needn't handle non-finite values.
Results may differ from a plain program's by a relative error of at most 0.0044.
The roundings to bfloat16 on the way count: a program that leaves them out, or rounds other values in their place, can miss the bound.
Values may be sent and summed in bfloat16 or wider, within the bound.
No kernel may reach another device: no remote copies, remote signals or barrier semaphores. Data moves between devices by JAX's collectives and lax.ppermute only.
A program may use at most 128 MiB of HBM per device.

v0:
```python
import math

import jax
import jax.numpy as jnp
from jax import lax
from jax.sharding import PartitionSpec as P

G = 4
AH = 32
KVH = 4
HD = 64


norm_eps = 1e-05


def from_behind(value, axis, steps):
    count = lax.axis_size(axis)
    pairs = [(source, (source + steps) % count) for source in range(count)]
    return lax.ppermute(value, axis, pairs)


def causal_taps(rim, inputs, rim_ids, ids, weights):
    lag = rim.shape[0]
    length = inputs.shape[0]
    padded = jnp.concatenate([rim, inputs], axis=0)
    padded_ids = jnp.concatenate([rim_ids, ids])
    layout = (length,) + (1,) * (inputs.ndim - 1)
    summed = jnp.zeros(inputs.shape, jnp.float32)
    for tap in range(lag + 1):
        same = (padded_ids[tap : tap + length] == ids).reshape(layout)
        summed = summed + jnp.where(
            same,
            weights[tap].astype(jnp.float32) * padded[tap : tap + length].astype(jnp.float32),
            0.0,
        )
    return jax.nn.silu(summed).astype(jnp.bfloat16)


def per_head(grouped, heads):
    leading = grouped.shape[:-3]
    groups = grouped.shape[-2]
    states = grouped.shape[-1]
    moved = jnp.swapaxes(grouped, -3, -2)
    spread = jnp.repeat(moved, heads // groups, axis=-3)
    return spread.reshape(leading + (heads, 2 * states))


def state_space(x_conv, bc_conv, step_size, rates, skip, ids):
    length, local_heads, head_dim = x_conv.shape
    states = bc_conv.shape[2] // 2
    span = min(256, length)
    blocks = length // span
    lower = jnp.arange(span)[:, None] >= jnp.arange(span)[None, :]

    def advance(carry, item):
        memory, last_id = carry
        x_block, bc_block, step_block, id_block = item
        b_part = bc_block[:, :, :states]
        c_part = bc_block[:, :, states:]
        logs = jnp.cumsum(step_block * rates[None, :], axis=0)
        allowed = lower & (id_block[:, None] == id_block[None, :])
        gaps = logs[:, None, :] - logs[None, :, :]
        weights = (
            jnp.where(allowed[:, :, None], jnp.exp(jnp.minimum(gaps, 0.0)), 0.0)
            * step_block[None, :, :]
        )
        inner = jnp.einsum("thn,shn->tsh", c_part, b_part, preferred_element_type=jnp.float32)
        mixing = (inner * weights).astype(jnp.bfloat16)
        local_part = jnp.einsum("tsh,shp->thp", mixing, x_block, preferred_element_type=jnp.float32)
        keep = jnp.where((id_block == last_id)[:, None], jnp.exp(logs), 0.0)
        carried = (
            jnp.einsum(
                "thn,hpn->thp", c_part.astype(jnp.float32), memory, precision=lax.Precision.HIGHEST
            )
            * keep[:, :, None]
        )
        result = local_part + carried + skip[None, :, None] * x_block.astype(jnp.float32)
        tail = logs[span - 1]
        writes = (
            jnp.where((id_block == id_block[span - 1])[:, None], jnp.exp(tail[None, :] - logs), 0.0)
            * step_block
        )
        scaled = (x_block.astype(jnp.float32) * writes[:, :, None]).astype(jnp.bfloat16)
        added = jnp.einsum("shp,shn->hpn", scaled, b_part, preferred_element_type=jnp.float32)
        kept = jnp.where(id_block[span - 1] == last_id, jnp.exp(tail), 0.0)
        memory = memory * kept[:, None, None] + added
        return ((memory, id_block[span - 1]), result)

    start = (jnp.zeros((local_heads, head_dim, states), jnp.float32), jnp.array(-1, jnp.int32))
    items = (
        x_conv.reshape(blocks, span, local_heads, head_dim),
        bc_conv.reshape(blocks, span, local_heads, 2 * states),
        step_size.reshape(blocks, span, local_heads),
        ids.reshape(blocks, span),
    )
    (memory, _), outputs = lax.scan(advance, start, items)
    return (memory, outputs.reshape(length, local_heads, head_dim))


def on_device(
    x_in,
    z_in,
    bc_in,
    dt_raw,
    a_log,
    dt_bias,
    d_skip,
    conv_x,
    conv_bc,
    norm_gain,
    seg_ids,
    query,
    keys,
    values,
):
    ranks = lax.axis_size("ctx")
    place = lax.axis_index("ctx")
    tokens_here = x_in.shape[1]
    heads = dt_raw.shape[2]
    head_dim = x_in.shape[2] // heads
    states = bc_in.shape[2] // (2 * G)
    lag = conv_x.shape[1] - 1
    own_ids = seg_ids[0]
    all_ids = lax.all_gather(own_ids, "ctx", axis=0, tiled=True)
    local_heads = heads // ranks
    first_head = place * local_heads
    x_send = x_in[0].reshape(tokens_here, heads, head_dim)
    bc_send = per_head(bc_in[0].reshape(tokens_here, 2, G, states), heads)
    x_heads, raw_heads, bc_heads = (
        lax.all_to_all(x_send, "ctx", split_axis=1, concat_axis=0, tiled=True),
        lax.all_to_all(dt_raw[0], "ctx", split_axis=1, concat_axis=0, tiled=True),
        lax.all_to_all(bc_send, "ctx", split_axis=1, concat_axis=0, tiled=True),
    )
    empty_ids = jnp.full((lag,), -1, jnp.int32)
    taps_x = lax.dynamic_slice_in_dim(
        conv_x[0].reshape(lag + 1, heads, head_dim), first_head, local_heads, 1
    )
    taps_bc = lax.dynamic_slice_in_dim(
        per_head(conv_bc[0].reshape(lag + 1, 2, G, states), heads), first_head, local_heads, 1
    )
    x_conv = causal_taps(
        jnp.zeros((lag,) + x_heads.shape[1:], jnp.bfloat16), x_heads, empty_ids, all_ids, taps_x
    )
    bc_conv = causal_taps(
        jnp.zeros((lag,) + bc_heads.shape[1:], jnp.bfloat16), bc_heads, empty_ids, all_ids, taps_bc
    )
    bias_heads = lax.dynamic_slice_in_dim(dt_bias[0], first_head, local_heads)
    rates = -jnp.exp(lax.dynamic_slice_in_dim(a_log[0], first_head, local_heads))
    skip = lax.dynamic_slice_in_dim(d_skip[0], first_head, local_heads)
    step_size = jax.nn.softplus(raw_heads.astype(jnp.float32) + bias_heads[None, :])
    _, local = state_space(x_conv, bc_conv, step_size, rates, skip, all_ids)
    attention_mixture = local.astype(jnp.bfloat16)
    mixed_tokens = lax.all_to_all(
        attention_mixture, "ctx", split_axis=0, concat_axis=1, tiled=True
    ).reshape(tokens_here, heads * head_dim)
    gated = mixed_tokens.astype(jnp.float32) * jax.nn.silu(z_in[0].astype(jnp.float32))
    grouped = gated.reshape(tokens_here, G, heads * head_dim // G)
    factor = lax.rsqrt(jnp.mean(grouped * grouped, axis=-1, keepdims=True) + norm_eps)
    mamba_out = (
        (grouped * factor).reshape(tokens_here, heads * head_dim) * norm_gain[0][None, :]
    ).astype(jnp.bfloat16)
    ratio = AH // KVH
    queries = query[0].reshape(tokens_here, KVH, ratio, HD)
    query_pos = place * tokens_here + jnp.arange(tokens_here)
    logit_scale = 1.0 / math.sqrt(HD)
    initial = (
        jnp.full((KVH, ratio, tokens_here), -1e30, jnp.float32),
        jnp.zeros((KVH, ratio, tokens_here), jnp.float32),
        jnp.zeros((KVH, ratio, tokens_here, HD), jnp.float32),
    )
    carry = initial
    key_piece = lax.all_gather(keys[0], "ctx", axis=0, tiled=True)
    value_piece = lax.all_gather(values[0], "ctx", axis=0, tiled=True)
    count = key_piece.shape[0]
    width = math.gcd(count, 512)
    key_blocks = key_piece.reshape(count // width, width, KVH, HD)
    value_blocks = value_piece.reshape(count // width, width, KVH, HD)

    def visit(running, item):
        key_block, value_block, order = item
        first = order * width
        key_ids = lax.dynamic_slice_in_dim(all_ids, first, width)
        key_pos = first + jnp.arange(width)
        allowed = (query_pos[:, None] >= key_pos[None, :]) & (own_ids[:, None] == key_ids[None, :])
        largest, totals, accum = running
        attention_logits = (
            jnp.einsum("tgrd,mgd->grtm", queries, key_block, preferred_element_type=jnp.float32)
            * logit_scale
        )
        masked = jnp.where(allowed, attention_logits, -1e30)
        newest = jnp.maximum(largest, jnp.max(masked, axis=-1))
        weight = jnp.where(allowed, jnp.exp(masked - newest[..., None]), 0.0)
        correct = jnp.exp(largest - newest)
        totals = totals * correct + jnp.sum(weight, axis=-1)
        accum = accum * correct[..., None] + jnp.einsum(
            "grtm,mgd->grtd",
            weight.astype(jnp.bfloat16),
            value_block,
            preferred_element_type=jnp.float32,
        )
        running = (newest, totals, accum)
        return (running, None)

    carry, _ = lax.scan(
        visit, carry, (key_blocks, value_blocks, jnp.arange(count // width, dtype=jnp.int32))
    )
    largest, totals, accum = carry
    attended = accum / totals[..., None]
    attended = (
        jnp.transpose(attended, (2, 0, 1, 3)).reshape(tokens_here, AH * HD).astype(jnp.bfloat16)
    )
    handoff = from_behind(attended, "pipe", 1)
    return (mamba_out[None], handoff[None])


def solution(mesh):
    in_specs = (
        P("pipe", "ctx", None),
        P("pipe", "ctx", None),
        P("pipe", "ctx", None),
        P("pipe", "ctx", None),
        P("pipe", None),
        P("pipe", None),
        P("pipe", None),
        P("pipe", None, None),
        P("pipe", None, None),
        P("pipe", None),
        P("pipe", "ctx"),
        P("pipe", "ctx", None),
        P("pipe", "ctx", None),
        P("pipe", "ctx", None),
    )
    out_specs = (P("pipe", "ctx", None), P("pipe", "ctx", None))
    return jax.shard_map(
        on_device, mesh=mesh, in_specs=in_specs, out_specs=out_specs, check_vma=False
    )
```

profile of v0, /device:TPU:0, one launch (start us, length us, event | category | flops | bytes accessed | tf_op | source)
XLA Modules:
  0.0 315.3 jit_solution(9040418585861244815)
XLA Ops:
  2.2 6.3 %all-to-all-start = ((bf16[8,2,512]{2,1,0:T(2,128)(2,1)}), bf16[8,2,512]{2,1,0:T(2,128)(2,1)S(1)}, u32[]{:S(2)}, u32[]{:S(2)}) async-start(bf16[8,2,512]{2,1,0:T(2,128)(2,1)} %reshape.218), calls=%async_computation | async-start | bytes 32768 | tf_op jit(solution)/shard_map/all_to_all | solution.py:132
  8.5 4.3 %reshape_squeeze.16 = bf16[64,128,64]{2,1,0:T(8,128)(2,1)} reshape(bf16[1,64,8192]{2,1,0:T(8,128)(2,1)} %param.16) | data formatting | bytes 2097152 | tf_op jit(solution)/shard_map/reshape;squeeze | solution.py:128
  12.7 3.0 copy.144
  18.4 5.1 %all-to-all-start.1 = ((bf16[8,2,32768]{2,1,0:T(2,128)(2,1)}), bf16[8,2,32768]{2,1,0:T(2,128)(2,1)S(1)}, u32[]{:S(2)}, u32[]{:S(2)}) async-start(bf16[8,2,32768]{2,1,0:T(2,128)(2,1)} %reshape.220), calls=%async_computation.1 | async-start | bytes 2097152 | tf_op jit(solution)/shard_map/all_to_all | solution.py:131
  23.7 6.1 %broadcast_in_dim.176 = bf16[64,4,32,2,128]{4,3,0,2,1:T(2,128)(2,1)} broadcast(bf16[64,4,2,128]{3,2,0,1:T(2,128)(2,1)S(1)} %copy.94), dimensions={0,1,3,4} | broadcast | bytes 4325376 | tf_op jit(solution)/shard_map/broadcast_in_dim | solution.py:45
  29.8 7.6 %reshape_reshape.7 = bf16[64,128,256]{2,0,1:T(8,128)(2,1)} reshape(bf16[64,4,32,2,128]{4,3,0,2,1:T(2,128)(2,1)} %broadcast_in_dim.176) | data formatting | bytes 8388608 | tf_op jit(solution)/shard_map/reshape;reshape | solution.py:46
  37.5 12.6 %all-to-all-done.1 = bf16[8,2,32768]{2,1,0:T(2,128)(2,1)S(1)} async-done(((bf16[8,2,32768]{2,1,0:T(2,128)(2,1)}), bf16[8,2,32768]{2,1,0:T(2,128)(2,1)S(1)}, u32[]{:S(2)}, u32[]{:S(2)}) %all-to-all-start.1) | async-done | bytes 1048608 | tf_op jit(solution)/shard_map/all_to_all | solution.py:131
  50.1 4.6 %all-to-all-start.2 = ((bf16[64,128,256]{2,0,1:T(8,128)(2,1)}), bf16[64,128,256]{2,0,1:T(8,128)(2,1)}, u32[]{:S(2)}, u32[]{:S(2)}) async-start(bf16[64,128,256]{2,0,1:T(8,128)(2,1)} %reshape_reshape.7), calls=%async_computation.2 | async-start | bytes 8388608 | tf_op jit(solution)/shard_map/all_to_all | solution.py:133
  56.6 92.2 %all-reduce.3 = s32[512]{0:T(512)S(1)} all-reduce(s32[512]{0:T(512)S(1)} %bitcast_dynamic-update-slice_fusion), channel_id=2, replica_groups=mesh['pipe'=4,'ctx'=8] {'ctx'}, use_global_device_ids=true, to_apply=%add.3 | all-reduce | flops 512 | bytes 4096 | tf_op jit(solution)/shard_map/all_gather | solution.py:125
  148.8 14.2 %all-gather.1 = bf16[1,512,256]{2,1,0:T(8,128)(2,1)S(1)} all-gather(bf16[1,64,256]{2,1,0:T(8,128)(2,1)S(1)} %copy-done.11), channel_id=3, replica_groups=mesh['pipe'=4,'ctx'=8] {'ctx'}, dimensions={1}, use_global_device_ids=true | all-gather | bytes 294912 | tf_op jit(solution)/shard_map/all_gather | solution.py:173
  167.4 3.1 reshape.221
  170.5 2.9 copy.92
  173.5 3.2 %all_to_all.48 = bf16[512,16,64]{0,2,1:T(8,128)(2,1)S(1)} reshape(bf16[8,64,16,64]{1,0,3,2:T(8,128)(2,1)} %bitcast.252) | data formatting | bytes 2097152 | tf_op jit(solution)/shard_map/all_to_all | solution.py:131
  180.2 4.7 %copy.96 = bf16[8,64,16,256]{3,2,1,0:T(8,128)(2,1)S(1)} copy(bf16[8,64,16,256]{3,1,2,0:T(8,128)(2,1)} %bitcast.17) | data formatting | bytes 8388608 | tf_op jit(solution)/shard_map/all_to_all | solution.py:133
  184.9 7.8 %multiply_convert_fusion = bf16[512,16,256]{2,1,0:T(8,128)(2,1)} fusion(bf16[512,16,256]{2,1,0:T(8,128)(2,1)S(1)} %bitcast.248, f32[16,256]{1,0:T(8,128)S(1)} %get-tuple-element.192, f32[16,256]{1,0:T(8,128)S(1)} %get-tuple-element.190, f32[16,256]{1,0:T(8,128)S(1)} %get-tuple-element.191, f32[16,256]{1,0:T(8,128)S(1)} %get-tuple-element.189, ...), kind=kLoop, calls=%fused_computation.49 | loop fusion | flops 39845888 | bytes 8455680 | tf_op jit(solution)/shard_map/convert_element_type | solution.py:37
  192.7 31.1 %while.3 = (s32[]{:T(128)}, f32[16,64,128]{2,1,0:T(8,128)S(1)}, s32[]{:T(128)}, bf16[2,256,16,64]{1,3,2,0:T(8,128)(2,1)}, s32[2,256]{1,0:T(2,128)S(1)}, /*index=...) while((s32[]{:T(128)}, f32[16,64,128]{2,1,0:T(8,128)S(1)}, ...), condition=%wide.region_3.4_spmd.clone, body=%wide.region_0.3_spmd.clone.sunk | while | flops 882074176 | bytes 19326392 | solution.py:97
  197.0 3.6 %fusion.87 = f32[256,16,64]{0,2,1:T(8,128)} fusion(f32[256,16]{0,1:T(8,128)S(1)} %bitcast.258, f32[256,16]{0,1:T(8,128)S(1)} %bitcast_bitcast_fusion.2, pred[256,256]{0,1:T(8,128)(4,1)S(1)} %fusion.86, bf16[256,16,256]{2,0,1:T(8,128)(2,1)S(1)} %bitcast.242, bf16[2,256,16,64]{1,3,2,0:T(8,128)(2,1)} %get-tuple-element.310, s32[]{:T(128)} %get-tuple-element.289), kind=kOutput, calls=%fused_computation.5.clone.1 | convolution fusion | flops 408944640 | bytes 3785216 | tf_op jit(solution)/shard_map/while/body/eval_jaxpr/tsh,shp->thp/dot_general | solution.py:70
  202.2 3.4 %fusion.88 = bf16[2,256,16,64]{1,3,2,0:T(8,128)(2,1)} fusion(bf16[2,256,16,64]{1,3,2,0:T(8,128)(2,1)} %get-tuple-element.292, s32[]{:T(128)} %get-tuple-element.289, f32[256,16,64]{0,2,1:T(8,128)} %fusion.87, bf16[256,16,256]{2,0,1:T(8,128)(2,1)S(1)} %bitcast.243, f32[16]{0:T(128)S(1)} %get-tuple-element.312, f32[256,16]{0,1:T(8,128)S(1)} %get-tuple-element.274, ...), kind=kOutput, calls=%fused_computation.11.clone.1 | convolution fusion | flops 404094976 | bytes 4211713 | tf_op jit(solution)/shard_map/while/body/eval_jaxpr/thn,hpn->thp/dot_general | solution.py:73
  212.6 3.6 %fusion.87 = f32[256,16,64]{0,2,1:T(8,128)} fusion(f32[256,16]{0,1:T(8,128)S(1)} %bitcast.258, f32[256,16]{0,1:T(8,128)S(1)} %bitcast_bitcast_fusion.2, pred[256,256]{0,1:T(8,128)(4,1)S(1)} %fusion.86, bf16[256,16,256]{2,0,1:T(8,128)(2,1)S(1)} %bitcast.242, bf16[2,256,16,64]{1,3,2,0:T(8,128)(2,1)} %get-tuple-element.310, s32[]{:T(128)} %get-tuple-element.289), kind=kOutput, calls=%fused_computation.5.clone.1 | convolution fusion | flops 408944640 | bytes 3785216 | tf_op jit(solution)/shard_map/while/body/eval_jaxpr/tsh,shp->thp/dot_general | solution.py:70
  217.8 3.4 %fusion.88 = bf16[2,256,16,64]{1,3,2,0:T(8,128)(2,1)} fusion(bf16[2,256,16,64]{1,3,2,0:T(8,128)(2,1)} %get-tuple-element.292, s32[]{:T(128)} %get-tuple-element.289, f32[256,16,64]{0,2,1:T(8,128)} %fusion.87, bf16[256,16,256]{2,0,1:T(8,128)(2,1)S(1)} %bitcast.243, f32[16]{0:T(128)S(1)} %get-tuple-element.312, f32[256,16]{0,1:T(8,128)S(1)} %get-tuple-element.274, ...), kind=kOutput, calls=%fused_computation.11.clone.1 | convolution fusion | flops 404094976 | bytes 4211713 | tf_op jit(solution)/shard_map/while/body/eval_jaxpr/thn,hpn->thp/dot_general | solution.py:73
  223.8 3.0 copy.115
  229.5 4.6 %all-to-all-start.3 = ((bf16[8,2,32768]{2,1,0:T(2,128)(2,1)}), bf16[8,2,32768]{2,1,0:T(2,128)(2,1)}, u32[]{:S(2)}, u32[]{:S(2)}) async-start(bf16[8,2,32768]{2,1,0:T(2,128)(2,1)} %reshape.222), calls=%async_computation.3 | async-start | bytes 2097152 | tf_op jit(solution)/shard_map/all_to_all | solution.py:154
  236.8 30.7 %all-gather.2 = bf16[1,512,256]{2,1,0:T(8,128)(2,1)S(1)} all-gather(bf16[1,64,256]{2,1,0:T(8,128)(2,1)S(1)} %copy-done.12), channel_id=4, replica_groups=mesh['pipe'=4,'ctx'=8] {'ctx'}, dimensions={1}, use_global_device_ids=true | all-gather | bytes 294912 | tf_op jit(solution)/shard_map/all_gather | solution.py:174
  267.7 3.6 %fusion.32 = f32[4,8,64]{2,1,0:T(8,128)S(1)} fusion(f32[4,512,64,8]{1,2,3,0:T(8,128)} %get-tuple-element.203, f32[4,8,64]{2,1,0:T(8,128)S(1)} %get-tuple-element.198, pred[64,512]{1,0:T(8,128)(4,1)S(1)} %copy-done.3), kind=kLoop, calls=%fused_computation.55 | loop fusion | flops 5240832 | bytes 4243456 | tf_op jit(solution)/shard_map/while/body/eval_jaxpr/reduce_sum | solution.py:195
  275.1 3.2 %reshape.196 = f32[64,8,16,64]{3,2,1,0:T(8,128)} reshape(bf16[1,64,8192]{2,1,0:T(8,128)(2,1)S(1)} %copy-done.2) | data formatting | bytes 3145728 | tf_op jit(solution)/shard_map/convert_element_type | solution.py:157
  278.3 5.5 %copy.105 = f32[64,8,16,64]{0,1,3,2:T(8,128)} copy(f32[64,8,16,64]{3,2,1,0:T(8,128)} %reshape.196) | data formatting | bytes 4194304 | tf_op jit(solution)/shard_map/convert_element_type | solution.py:157
  283.8 3.1 reshape.223
  289.4 4.0 %reshape.198 = f32[8,64,16,64]{1,0,3,2:T(8,128)} reshape(bf16[512,16,64]{0,2,1:T(8,128)(2,1)} %copy.102) | data formatting | bytes 3145728 | tf_op jit(solution)/shard_map/convert_element_type | solution.py:157
  293.4 4.9 %multiply_reduce_fusion = f32[64,8]{0,1:T(8,128)S(1)} fusion(f32[64,8,16,64]{0,1,3,2:T(8,128)} %copy.105, f32[8,64,16,64]{1,0,3,2:T(8,128)} %reshape.198), kind=kLoop, calls=%fused_computation.52 | loop fusion | flops 3669504 | bytes 4196352 | tf_op jit(solution)/shard_map/reduce_sum | solution.py:159
  301.2 6.3 %copy.103 = f32[64,8,16,64]{3,2,1,0:T(8,128)} copy(f32[64,8,16,64]{0,1,3,2:T(8,128)} %bitcast.246) | data formatting | bytes 4194304 | tf_op jit(solution)/shard_map/convert_element_type | solution.py:157
  307.5 3.5 %reshape.195 = f32[1,64,8192]{2,1,0:T(8,128)S(1)} reshape(f32[64,8,16,64]{3,2,1,0:T(8,128)} %copy.103) | data formatting | bytes 4194304 | tf_op jit(solution)/shard_map/convert_element_type | solution.py:157
  311.1 3.5 %multiply_convert_fusion.1 = bf16[1,64,8192]{2,1,0:T(8,128)(2,1)} fusion(f32[1,64,8192]{2,1,0:T(8,128)} %mul.292, f32[1,64,8192]{2,1,0:T(8,128)S(1)} %reshape.195, f32[8192]{0:T(1024)S(1)} %bitcast.262, bf16[1,64,8192]{2,1,0:T(8,128)(2,1)} %param.17), kind=kLoop, calls=%fused_computation.57 | loop fusion | flops 4718592 | bytes 6324224 | tf_op jit(solution)/shard_map/convert_element_type | solution.py:162
  (138 shorter events, 43.3 us)
Async XLA Ops:
  2.2 16.2 %all-to-all-start = ((bf16[8,2,512]{2,1,0:T(2,128)(2,1)}), bf16[8,2,512]{2,1,0:T(2,128)(2,1)S(1)}, u32[]{:S(2)}, u32[]{:S(2)}) async-start(bf16[8,2,512]{2,1,0:T(2,128)(2,1)} %reshape.218), calls=%async_computation | async-start | bytes 32768 | tf_op jit(solution)/shard_map/all_to_all | solution.py:132
  12.7 10.7 %copy-start.5 = (bf16[1,64,1024]{2,1,0:T(8,128)(2,1)S(1)}, bf16[1,64,1024]{2,1,0:T(8,128)(2,1)}, u32[]{:S(2)}) copy-start(bf16[1,64,1024]{2,1,0:T(8,128)(2,1)} %param.18) | copy-start | bytes 393220
  18.4 31.7 %all-to-all-start.1 = ((bf16[8,2,32768]{2,1,0:T(2,128)(2,1)}), bf16[8,2,32768]{2,1,0:T(2,128)(2,1)S(1)}, u32[]{:S(2)}, u32[]{:S(2)}) async-start(bf16[8,2,32768]{2,1,0:T(2,128)(2,1)} %reshape.220), calls=%async_computation.1 | async-start | bytes 2097152 | tf_op jit(solution)/shard_map/all_to_all | solution.py:131
  37.4 17.3 %copy-start.15 = (bf16[1,4,1024]{2,1,0:T(4,128)(2,1)S(1)}, bf16[1,4,1024]{2,1,0:T(4,128)(2,1)}, u32[]{:S(2)}) copy-start(bf16[1,4,1024]{2,1,0:T(4,128)(2,1)} %param.24) | copy-start | bytes 24580
  37.4 17.7 %copy-start.6 = (bf16[1,4,8192]{2,1,0:T(4,128)(2,1)S(1)}, bf16[1,4,8192]{2,1,0:T(4,128)(2,1)}, u32[]{:S(2)}) copy-start(bf16[1,4,8192]{2,1,0:T(4,128)(2,1)} %param.23) | copy-start | bytes 196612
  37.4 17.8 %copy-start.23 = (u32[32]{0:T(128)S(1)}, u32[32]{0:T(128)}, u32[]{:S(2)}) copy-start(u32[32]{0:T(128)} %constant.111) | copy-start | bytes 388
  37.4 19.1 %copy-start.19 = (s32[1,64]{1,0:T(1,128)S(1)}, s32[1,64]{1,0:T(1,128)}, u32[]{:S(2)}) copy-start(s32[1,64]{1,0:T(1,128)} %param.26) | copy-start | bytes 772
  37.4 111.4 %copy-start.11 = (bf16[1,64,256]{2,1,0:T(8,128)(2,1)S(1)}, bf16[1,64,256]{2,1,0:T(8,128)(2,1)}, u32[]{:S(2)}) copy-start(bf16[1,64,256]{2,1,0:T(8,128)(2,1)} %param.28) | copy-start | bytes 98308
  37.4 125.7 %copy-start.4 = (bf16[1,64,2048]{2,1,0:T(8,128)(2,1)S(1)}, bf16[1,64,2048]{2,1,0:T(8,128)(2,1)}, u32[]{:S(2)}) copy-start(bf16[1,64,2048]{2,1,0:T(8,128)(2,1)} %param.27) | copy-start | bytes 786436
  37.4 126.2 %copy-start.22 = (f32[1,128]{1,0:T(1,128)S(1)}, f32[1,128]{1,0:T(1,128)}, u32[]{:S(2)}) copy-start(f32[1,128]{1,0:T(1,128)} %param.20) | copy-start | bytes 1540
  37.5 126.8 %copy-start.20 = (f32[1,128]{1,0:T(1,128)S(1)}, f32[1,128]{1,0:T(1,128)}, u32[]{:S(2)}) copy-start(f32[1,128]{1,0:T(1,128)} %param.21) | copy-start | bytes 1540
  37.5 126.8 %copy-start.21 = (f32[1,128]{1,0:T(1,128)S(1)}, f32[1,128]{1,0:T(1,128)}, u32[]{:S(2)}) copy-start(f32[1,128]{1,0:T(1,128)} %param.22) | copy-start | bytes 1540
  50.1 4.6 %copy-start.1 = (bf16[8,2,32768]{2,1,0:T(2,128)(2,1)}, bf16[8,2,32768]{2,1,0:T(2,128)(2,1)S(1)}, u32[]{:S(2)}) copy-start(bf16[8,2,32768]{2,1,0:T(2,128)(2,1)S(1)} %all-to-all-done.1) | copy-start | bytes 3145732
  50.1 130.1 %all-to-all-start.2 = ((bf16[64,128,256]{2,0,1:T(8,128)(2,1)}), bf16[64,128,256]{2,0,1:T(8,128)(2,1)}, u32[]{:S(2)}, u32[]{:S(2)}) async-start(bf16[64,128,256]{2,0,1:T(8,128)(2,1)} %reshape_reshape.7), calls=%async_computation.2 | async-start | bytes 8388608 | tf_op jit(solution)/shard_map/all_to_all | solution.py:133
  170.5 6.2 %copy-start.8 = (f32[16,64]{1,0:T(8,128)S(1)}, f32[16,64]{1,0:T(8,128)}, u32[]{:S(2)}) copy-start(f32[16,64]{1,0:T(8,128)} %get-tuple-element.194) | copy-start | bytes 12292
  170.5 6.2 %copy-start.9 = (f32[16,64]{1,0:T(8,128)S(1)}, f32[16,64]{1,0:T(8,128)}, u32[]{:S(2)}) copy-start(f32[16,64]{1,0:T(8,128)} %get-tuple-element.195) | copy-start | bytes 12292
  170.5 6.2 %copy-start.10 = (f32[16,64]{1,0:T(8,128)S(1)}, f32[16,64]{1,0:T(8,128)}, u32[]{:S(2)}) copy-start(f32[16,64]{1,0:T(8,128)} %get-tuple-element.196) | copy-start | bytes 12292
  170.5 6.2 %copy-start.16 = (pred[512]{0:T(512)(128)(4,1)S(1)}, pred[512]{0:T(512)(128)(4,1)}, u32[]{:S(2)}) copy-start(pred[512]{0:T(512)(128)(4,1)} %get-tuple-element.199) | copy-start | bytes 1540
  170.5 6.2 %copy-start.17 = (pred[512]{0:T(512)(128)(4,1)S(1)}, pred[512]{0:T(512)(128)(4,1)}, u32[]{:S(2)}) copy-start(pred[512]{0:T(512)(128)(4,1)} %get-tuple-element.200) | copy-start | bytes 1540
  170.5 6.2 %copy-start.18 = (pred[512]{0:T(512)(128)(4,1)S(1)}, pred[512]{0:T(512)(128)(4,1)}, u32[]{:S(2)}) copy-start(pred[512]{0:T(512)(128)(4,1)} %get-tuple-element.201) | copy-start | bytes 1540
  184.9 7.8 %copy-start.13 = (f32[16]{0:T(128)S(1)}, f32[16]{0:T(128)}, u32[]{:S(2)}) copy-start(f32[16]{0:T(128)} %fusion.63) | copy-start | bytes 196
  200.6 7.0 %copy-start.14 = (f32[16]{0:T(128)S(1)}, f32[16]{0:T(128)}, u32[]{:S(2)}) copy-start(f32[16]{0:T(128)} %get-tuple-element.345) | copy-start | bytes 196 | tf_op jit(solution)/shard_map/while
  216.2 7.0 %copy-start.14 = (f32[16]{0:T(128)S(1)}, f32[16]{0:T(128)}, u32[]{:S(2)}) copy-start(f32[16]{0:T(128)} %get-tuple-element.345) | copy-start | bytes 196 | tf_op jit(solution)/shard_map/while
  223.8 10.3 %copy-start.3 = (pred[64,512]{1,0:T(8,128)(4,1)S(1)}, pred[64,512]{1,0:T(8,128)(4,1)}, u32[]{:S(2)}) copy-start(pred[64,512]{1,0:T(8,128)(4,1)} %fusion.47) | copy-start | bytes 98308
  229.5 7.3 %copy-start.12 = (bf16[1,64,256]{2,1,0:T(8,128)(2,1)S(1)}, bf16[1,64,256]{2,1,0:T(8,128)(2,1)}, u32[]{:S(2)}) copy-start(bf16[1,64,256]{2,1,0:T(8,128)(2,1)} %param.29) | copy-start | bytes 98308
  229.5 54.3 %all-to-all-start.3 = ((bf16[8,2,32768]{2,1,0:T(2,128)(2,1)}), bf16[8,2,32768]{2,1,0:T(2,128)(2,1)}, u32[]{:S(2)}, u32[]{:S(2)}) async-start(bf16[8,2,32768]{2,1,0:T(2,128)(2,1)} %reshape.222), calls=%async_computation.3 | async-start | bytes 2097152 | tf_op jit(solution)/shard_map/all_to_all | solution.py:154
  267.6 3.6 %copy-start = (f32[4,512,64,8]{1,2,3,0:T(8,128)S(1)}, f32[4,512,64,8]{1,2,3,0:T(8,128)}, u32[]{:S(2)}) copy-start(f32[4,512,64,8]{1,2,3,0:T(8,128)} %get-tuple-element.203) | copy-start | bytes 12582916
  271.3 3.8 %copy-start.2 = (bf16[1,64,8192]{2,1,0:T(8,128)(2,1)S(1)}, bf16[1,64,8192]{2,1,0:T(8,128)(2,1)}, u32[]{:S(2)}) copy-start(bf16[1,64,8192]{2,1,0:T(8,128)(2,1)} %param.17) | copy-start | bytes 3145732
  273.5 10.3 %collective-permute-start = (bf16[64,2048]{1,0:T(8,128)(2,1)S(1)}, bf16[64,2048]{1,0:T(8,128)(2,1)S(1)}, u32[]{:S(2)}, u32[]{:S(2)}) collective-permute-start(bf16[64,2048]{1,0:T(8,128)(2,1)S(1)} %convert_element_type.151), channel_id=1, source_target_pairs={{0,8},{8,16},{16,24},{24,0},{1,9},{9,17},{17,25},{25,1},{2,10},{10... | collective-permute-start | bytes 786440 | tf_op jit(solution)/shard_map/ppermute | solution.py:20
  307.5 3.5 %copy-start.7 = (f32[1,8192]{1,0:T(1,128)S(1)}, f32[1,8192]{1,0:T(1,128)}, u32[]{:S(2)}) copy-start(f32[1,8192]{1,0:T(1,128)} %param.25) | copy-start | bytes 98308
where the time goes:
time: 317 us; the launch traced here: 315 us
  blocking collectives  137 us (43%)
  local copies, waits for them, and re-layouts  89.4 us (28%)
  other arithmetic  28.6 us (9%)
  starting transfers between devices  22.1 us (7%)
  matrix products  21.1 us (7%)
  waiting for transfers between devices  12.6 us (4%)
    all_gather x1, blocking collectives, on_device(): all_ids = lax.all_gather(own_ids, 'ctx', axis=0, tiled=True)  92.2 us
    all_gather x1, blocking collectives, on_device(): value_piece = lax.all_gather(values[0], 'ctx', axis=0, tiled=True)  30.7 us
    unnamed x57, local copies, waits for them, and re-layouts  14.6 us
    all_gather x1, blocking collectives, on_device(): key_piece = lax.all_gather(keys[0], 'ctx', axis=0, tiled=True)  14.2 us
    convert_element_type x3, local copies, waits for them, and re-layouts, on_device(): mixed_tokens.astype(jnp.float32) * jax.nn.silu(z_in[0].astype(jnp.float32))  13.9 us
    all_to_all x1, waiting for transfers between devices, on_device(): lax.all_to_all(x_send, 'ctx', split_axis=1, concat_axis=0, tiled=True)  12.6 us
    convert_element_type x2, other arithmetic, causal_taps(): return jax.nn.silu(summed).astype(jnp.bfloat16)  10 us
    convert_element_type x2, local copies, waits for them, and re-layouts, on_device(): z_in[0].astype(jnp.float32)  8.7 us
  transfers between devices with their start and end apart: 5, of which 1 were waited for; matrix products, arithmetic and copies ran while one was open for 18% of the time, Pallas kernels for 0%

commit v1 on v0

v1 whole, which is shorter than its diff:
```python
import functools
import math

import jax
import jax.numpy as jnp
from jax import lax
from jax.experimental import pallas as pl
from jax.experimental.pallas import tpu as pltpu
from jax.sharding import PartitionSpec as P

G = 4
AH = 32
KVH = 4
HD = 64
BLK = 256
LANES = 128
LOCAL_HEADS = 32
CHUNKS = 2

norm_eps = 1e-05
bf16 = jnp.bfloat16
f32 = jnp.float32


def shifted(value, axis, steps):
    count = lax.axis_size(axis)
    return lax.ppermute(value, axis, [(i, i + steps) for i in range(count - steps)])


def crossed(value, axis, mask):
    count = lax.axis_size(axis)
    return lax.ppermute(value, axis, [(i, i ^ mask) for i in range(count)])


def from_behind(value, axis, steps):
    count = lax.axis_size(axis)
    return lax.ppermute(value, axis, [(i, (i + steps) % count) for i in range(count)])


def iota(shape, dim):
    return lax.broadcasted_iota(jnp.int32, shape, dim)


def call(body, outs, scratch=(), flops=0, bytes_accessed=0):
    return pl.pallas_call(
        body,
        out_shape=outs,
        scratch_shapes=list(scratch),
        compiler_params=pltpu.CompilerParams(vmem_limit_bytes=48 * 2**20),
        cost_estimate=pl.CostEstimate(
            flops=flops, bytes_accessed=bytes_accessed, transcendentals=0
        ),
    )


def pack_body(share, chunk, x_ref, bc_ref, dt_ref, ids_ref, k_ref, v_ref, *outs):
    me = lax.rem(lax.axis_index("ctx"), share)
    rows, width = x_ref.shape
    piece = width // share
    states = bc_ref.shape[1] // (2 * G)
    a_refs, b_refs, kv_refs = outs[:share], outs[share : 2 * share], outs[2 * share :]
    number = ids_ref[...].astype(f32) + 1.0
    square = iota((rows, rows), 0) == iota((rows, rows), 1)
    column = jnp.sum(
        jnp.where(square, jnp.broadcast_to(number, (rows, rows)), 0.0), axis=1, keepdims=True
    )
    spread_ids = jnp.broadcast_to(column, (rows, LANES)).astype(bf16)
    steps = dt_ref[...]
    for m in range(share):
        s = me ^ m
        base = pl.multiple_of(s * piece, LANES)
        b_at = pl.multiple_of(s * states, LANES)
        c_at = pl.multiple_of(G * states + s * states, LANES)
        a_refs[m][:, :chunk] = x_ref[:, pl.ds(base, chunk)]
        a_refs[m][:, chunk : chunk + states] = bc_ref[:, pl.ds(b_at, states)]
        a_refs[m][:, chunk + states : chunk + 2 * states] = bc_ref[:, pl.ds(c_at, states)]
        a_refs[m][:, chunk + 2 * states : chunk + 3 * states] = steps
        a_refs[m][:, chunk + 3 * states :] = spread_ids
        b_refs[m][...] = x_ref[:, pl.ds(pl.multiple_of(base + chunk, LANES), chunk)]
    wide = 4 * LANES
    lane = iota((rows, wide), 1)
    row = iota((rows, wide), 0)
    which = iota((16, wide), 0)
    for r, kv in enumerate(kv_refs):
        kv[:rows, : wide // 2] = k_ref[...]
        kv[:rows, wide // 2 :] = v_ref[...]
        id_row = jnp.sum(jnp.where(lane == row + rows * r, column, 0.0), axis=0, keepdims=True)
        block = jnp.where(which == 15, id_row, 0.0)
        if r > 0:
            s = lax.rem(me + r, share)
            base = pl.multiple_of(s * piece, LANES)
            b_at = pl.multiple_of(s * states, LANES)
            c_at = pl.multiple_of(G * states + s * states, LANES)
            last = pl.ds(rows - 16, 16)
            parts = [
                x_ref[last, pl.ds(pl.multiple_of(base + p * wide, LANES), wide)].astype(f32)
                for p in range(piece // wide)
            ]
            parts.append(
                jnp.concatenate(
                    [
                        bc_ref[last, pl.ds(b_at, states)],
                        bc_ref[last, pl.ds(c_at, states)],
                        dt_ref[last, :],
                        spread_ids[rows - 16 :],
                    ],
                    axis=1,
                ).astype(f32)
            )
            for i in range(3):
                for p, part in enumerate(parts):
                    block = jnp.where(which == 5 * i + p, part[13 + i : 14 + i, :], block)
        kv[rows:, :] = block.astype(bf16)


def place_halo(scratch, halos, pieces, me):
    rows = halos[0].shape[0]
    picked = halos[0][rows - 16 :, :].astype(f32)
    for r in range(1, len(halos)):
        picked = jnp.where(me == r, halos[r][rows - 16 :, :].astype(f32), picked)
    for at, p in enumerate(pieces):
        wide = picked.shape[1]
        which = iota((8, wide), 0)
        block = jnp.zeros((8, wide), f32)
        for i in range(3):
            block = jnp.where(which == 5 + i, picked[5 * i + p : 5 * i + p + 1, :], block)
        scratch[0:8, at * wide : (at + 1) * wide] = block


def conv_strip(src, columns, masks, taps):
    length = masks.shape[1]
    total = None
    for tap in range(4):
        term = taps[tap] * src[5 + tap : 5 + tap + length, columns]
        if tap < 3:
            term = term * masks[tap]
        total = term if total is None else total + term
    return (total * jax.nn.sigmoid(total)).astype(bf16)


def set_masks(masks, ids):
    length = masks.shape[1]
    own = ids[8 : 8 + length, :]
    for tap in range(3):
        masks[tap] = jnp.where(ids[5 + tap : 5 + tap + length, :] == own, 1.0, 0.0)


def one_hot(first, chunk):
    lane = iota((LANES, chunk), 0)
    head = iota((LANES, chunk), 1) // HD + first
    return jnp.where((lane % LOCAL_HEADS == head) & (lane < 3 * LOCAL_HEADS), 1.0, 0.0).astype(bf16)


def three_parts(value):
    lane = iota(value.shape, 1)
    high = value.astype(bf16).astype(f32)
    rest = value - high
    middle = rest.astype(bf16).astype(f32)
    low = rest - middle
    packed = jnp.where(
        lane < LOCAL_HEADS,
        high,
        jnp.where(
            lane < 2 * LOCAL_HEADS,
            pltpu.roll(middle, LOCAL_HEADS, 1),
            jnp.where(lane < 3 * LOCAL_HEADS, pltpu.roll(low, 2 * LOCAL_HEADS, 1), 0.0),
        ),
    )
    return packed.astype(bf16)


def conv_x_and_state(xs, masks, conv_ref, base, bcc, writes, first, xc_ref, state_ref):
    chunk = xc_ref.shape[1]
    for c in range(chunk // LANES):
        columns = slice(c * LANES, (c + 1) * LANES)
        weights = conv_ref[:, pl.ds(pl.multiple_of(base + c * LANES, LANES), LANES)].astype(f32)
        taps = [weights[t : t + 1, :] for t in range(4)]
        xc_ref[:, columns] = conv_strip(xs, columns, masks, taps)
    factors = jnp.dot(writes, one_hot(first, chunk), preferred_element_type=f32)
    scaled = (xc_ref[...].astype(f32) * factors).astype(bf16)
    state = lax.dot_general(bcc, scaled, (((0,), (0,)), ((), ())), preferred_element_type=f32)
    state_ref[...] = state.astype(state_ref.dtype)


def first_body(share, *refs):
    halos, pieces = refs[:share], refs[share : 2 * share]
    convx, convbc, bias, alog = refs[2 * share : 2 * share + 4]
    xc_o, bcc_o, state_o, ids_o, cum_o, step_o, writes_o, keep_o, xs, bs, masks = refs[
        2 * share + 4 :
    ]
    me = lax.rem(lax.axis_index("ctx"), share)
    chunk = xc_o.shape[1]
    rows = pieces[0].shape[0]
    length = rows * share
    per_block = 4 * LANES
    place_halo(xs, halos, list(range(chunk // per_block)), me)
    place_halo(bs, halos, [4], me)
    for m in range(share):
        at = pl.multiple_of(8 + rows * (me ^ m), 8)
        xs[pl.ds(at, rows), :] = pieces[m][:, :chunk].astype(f32)
        bs[pl.ds(at, rows), :] = pieces[m][:, chunk:].astype(f32)
    ids_o[...] = bs[:, 3 * LANES : 4 * LANES]
    set_masks(masks, ids_o)
    for half in range(2):
        columns = slice(half * LANES, (half + 1) * LANES)
        at = pl.multiple_of(half * G * LANES + me * LANES, LANES)
        weights = convbc[:, pl.ds(at, LANES)].astype(f32)
        taps = [weights[t : t + 1, :] for t in range(4)]
        bcc_o[:, columns] = conv_strip(bs, columns, masks, taps)
    raw = bs[8:, 2 * LANES : 3 * LANES] + bias[...]
    step = jnp.maximum(raw, 0.0) + jnp.log1p(jnp.exp(-jnp.abs(raw)))
    total = step * (-jnp.exp(alog[...]))
    row = iota((length, LANES), 0)
    reach = 1
    while reach < length:
        total = total + jnp.where(row >= reach, pltpu.roll(total, reach, 0), 0.0)
        reach *= 2
    turn = lax.rem(LANES - LOCAL_HEADS * me, LANES)
    total = pltpu.roll(total, turn, 1)
    step = pltpu.roll(step, turn, 1)
    own = ids_o[8:, :]
    last = length - 1
    writes = (
        jnp.where(own == own[last : last + 1, :], jnp.exp(total[last : last + 1, :] - total), 0.0)
        * step
    )
    cum_o[...] = total
    step_o[...] = step
    keep_o[...] = jnp.where(own == ids_o[7:8, :], jnp.exp(total), 0.0)
    packed = three_parts(writes)
    writes_o[...] = packed
    base = me * (chunk * CHUNKS)
    conv_x_and_state(xs, masks, convx, base, bcc_o[:, :LANES], packed, 0, xc_o, state_o)


def second_body(share, *refs):
    halos, pieces = refs[:share], refs[share : 2 * share]
    convx, bcc, ids, writes, xc_o, state_o, xs, masks = refs[2 * share :]
    me = lax.rem(lax.axis_index("ctx"), share)
    chunk = xc_o.shape[1]
    rows = pieces[0].shape[0]
    per_block = 4 * LANES
    blocks = chunk // per_block
    place_halo(xs, halos, list(range(blocks, 2 * blocks)), me)
    for m in range(share):
        at = pl.multiple_of(8 + rows * (me ^ m), 8)
        xs[pl.ds(at, rows), :] = pieces[m][...].astype(f32)
    set_masks(masks, ids)
    base = me * (chunk * CHUNKS) + chunk
    conv_x_and_state(
        xs, masks, convx, base, bcc[:, :LANES], writes[...], chunk // HD, xc_o, state_o
    )


def mixing_body(share, *refs):
    xcs, (bcc, ids, cum, step, skip) = refs[:CHUNKS], refs[CHUNKS : CHUNKS + 5]
    outs = refs[CHUNKS + 5 :]
    me = lax.rem(lax.axis_index("ctx"), share)
    length, chunk = xcs[0].shape
    half = length // 2
    inner = lax.dot_general(
        bcc[:, LANES:], bcc[:, :LANES], (((1,), (1,)), ((), ())), preferred_element_type=f32
    )
    own = ids[8:, :]
    across = own.T[0:1, :]
    own_wide = jnp.concatenate([own, own], axis=1)
    allowed = (iota((length, length), 0) >= iota((length, length), 1)) & (own_wide == across)
    inner = jnp.where(allowed, inner, 0.0)
    cums = cum[...]
    cum_rows = cums.T
    step_rows = step[...].T
    turn = lax.rem(LANES - LOCAL_HEADS * me, LANES)
    gains = three_parts(pltpu.roll(jnp.broadcast_to(skip[...], (8, LANES)), turn, 1))
    even = iota((half, LANES), 1) < HD
    for c in range(CHUNKS):
        first = c * (chunk // HD)
        spread = jnp.dot(gains, one_hot(first, chunk), preferred_element_type=f32)[0:1, :]
        for pair in range(chunk // LANES):
            columns = slice(pair * LANES, (pair + 1) * LANES)
            x_pair = xcs[c][:, columns]
            upper, lower = [], []
            for side in range(2):
                h = first + 2 * pair + side
                fade = cum_rows[h : h + 1, :]
                size = step_rows[h : h + 1, :]
                top = (
                    inner[:half, :half]
                    * (jnp.exp(jnp.minimum(cums[:half, h : h + 1] - fade[:, :half], 0.0)) * size[:, :half])
                ).astype(bf16)
                low = (
                    inner[half:, :]
                    * (jnp.exp(jnp.minimum(cums[half:, h : h + 1] - fade, 0.0)) * size)
                ).astype(bf16)
                upper.append(jnp.dot(top, x_pair[:half, :], preferred_element_type=f32))
                lower.append(jnp.dot(low, x_pair, preferred_element_type=f32))
            gain = spread[:, columns]
            outs[c][:half, columns] = (
                jnp.where(even, upper[0], upper[1]) + gain * x_pair[:half, :].astype(f32)
            )
            outs[c][half:, columns] = (
                jnp.where(even, lower[0], lower[1]) + gain * x_pair[half:, :].astype(f32)
            )


def finish_body(share, first, state, bcc, keep, local, *outs):
    me = lax.rem(lax.axis_index("ctx"), share)
    chunk = local.shape[1]
    rows = outs[0].shape[0]
    carried = jnp.dot(bcc[:, LANES:], state[...], preferred_element_type=f32)
    factors = jnp.dot(three_parts(keep[...]), one_hot(first, chunk), preferred_element_type=f32)
    local[...] = local[...] + carried * factors
    for m in range(share):
        at = pl.multiple_of(rows * (me ^ m), rows)
        outs[m][...] = local[pl.ds(at, rows), :].astype(bf16)


def finish_kernel(share, first, state, bcc, keep, local_in, *rest):
    outs, total = rest[:share], rest[share]
    total[...] = local_in[...]
    finish_body(share, first, state, bcc, keep, total, *outs)


def norm_body(share, *refs):
    firsts, seconds = refs[:share], refs[share : 2 * share]
    z, gain, out = refs[2 * share :]
    me = lax.rem(lax.axis_index("ctx"), share)
    chunk = firsts[0].shape[1]
    piece = 2 * chunk
    for m in range(share):
        base = pl.multiple_of((me ^ m) * piece, LANES)
        gated = []
        for c, source in enumerate((firsts[m], seconds[m])):
            gate = z[:, pl.ds(pl.multiple_of(base + c * chunk, LANES), chunk)].astype(f32)
            gated.append(source[...].astype(f32) * (gate * jax.nn.sigmoid(gate)))
        square = sum(jnp.sum(v * v, axis=1, keepdims=True) for v in gated)
        factor = lax.rsqrt(square / piece + norm_eps)
        for c, value in enumerate(gated):
            at = pl.ds(pl.multiple_of(base + c * chunk, LANES), chunk)
            out[:, at] = (value * factor * gain[:, at]).astype(bf16)


def attention_body(reach, q_ref, *refs):
    pieces, out = refs[: reach + 1], refs[reach + 1]
    rows = q_ref.shape[0]
    keys = rows * (reach + 1)
    padded = -(-keys // LANES) * LANES
    ratio = AH // KVH
    heads_wide = KVH * HD
    id_row = sum(p[rows : rows + 16, :].astype(f32)[15:16, :] for p in pieces)[:, :padded]
    own = pieces[0][rows : rows + 16, :].astype(f32)[15:16, :rows]
    square = iota((rows, rows), 0) == iota((rows, rows), 1)
    column = jnp.sum(
        jnp.where(square, jnp.broadcast_to(own, (rows, rows)), 0.0), axis=1, keepdims=True
    )
    lane = iota((rows, padded), 1)
    allowed = (id_row == column) & ((lane >= rows) | (lane <= iota((rows, padded), 0)))
    bias = jnp.where(allowed, 0.0, -1e30)
    pairs = ratio // 2
    bias = jnp.concatenate([bias] * pairs, axis=0)
    filler = [jnp.zeros((padded - keys, LANES), bf16)] if padded > keys else []
    even = iota((padded, LANES), 1) < HD
    nothing = jnp.zeros((padded, LANES), bf16)
    even_out = iota((rows * pairs, LANES), 1) < HD

    def both(at, side):
        whole = jnp.concatenate(
            [p[:rows, at : at + LANES] for p in pieces] + filler, axis=0
        ).astype(f32)
        kept = jnp.where(even == (side == 0), whole, 0.0)
        other = pltpu.roll(kept, HD, 1)
        first, second = (kept, other) if side == 0 else (other, kept)
        return jnp.concatenate([first.astype(bf16), second.astype(bf16)], axis=0)

    for g in range(KVH):
        block = (g // 2) * LANES
        key_pair = both(block, g % 2)
        value_pair = both(heads_wide + block, g % 2)
        base = g * ratio * HD
        q = jnp.concatenate(
            [q_ref[:, base + i * LANES : base + (i + 1) * LANES] for i in range(pairs)], axis=0
        )
        scores = lax.dot_general(
            q, key_pair, (((1,), (1,)), ((), ())), preferred_element_type=f32
        ) * (1.0 / math.sqrt(HD))
        probs, totals = [], []
        for side in range(2):
            masked = scores[:, side * padded : (side + 1) * padded] + bias
            top = jnp.max(masked, axis=1, keepdims=True)
            weight = jnp.exp(masked - top)
            totals.append(jnp.sum(weight, axis=1, keepdims=True))
            probs.append(weight.astype(bf16))
        mixed = jnp.dot(
            jnp.concatenate(probs, axis=1), value_pair, preferred_element_type=f32
        ) / jnp.where(even_out, totals[0], totals[1])
        for i in range(pairs):
            out[:, base + i * LANES : base + (i + 1) * LANES] = mixed[
                i * rows : (i + 1) * rows, :
            ].astype(bf16)


def gathered_attention(query, keys, values, own_ids):
    tokens_here = query.shape[0]
    place = lax.axis_index("ctx")
    all_ids = lax.all_gather(own_ids, "ctx", axis=0, tiled=True)
    ratio = AH // KVH
    queries = query.reshape(tokens_here, KVH, ratio, HD)
    query_pos = place * tokens_here + jnp.arange(tokens_here)
    key_piece = lax.all_gather(keys, "ctx", axis=0, tiled=True)
    value_piece = lax.all_gather(values, "ctx", axis=0, tiled=True)
    count = key_piece.shape[0]
    width = math.gcd(count, 512)
    key_blocks = key_piece.reshape(count // width, width, KVH, HD)
    value_blocks = value_piece.reshape(count // width, width, KVH, HD)
    shape = (KVH, ratio, tokens_here)

    def visit(running, item):
        key_block, value_block, order = item
        first = order * width
        key_ids = lax.dynamic_slice_in_dim(all_ids, first, width)
        key_pos = first + jnp.arange(width)
        allowed = (query_pos[:, None] >= key_pos[None, :]) & (own_ids[:, None] == key_ids[None, :])
        largest, totals, accum = running
        logits = jnp.einsum(
            "tgrd,mgd->grtm", queries, key_block, preferred_element_type=f32
        ) / math.sqrt(HD)
        masked = jnp.where(allowed, logits, -1e30)
        newest = jnp.maximum(largest, jnp.max(masked, axis=-1))
        weight = jnp.where(allowed, jnp.exp(masked - newest[..., None]), 0.0)
        correct = jnp.exp(largest - newest)
        totals = totals * correct + jnp.sum(weight, axis=-1)
        accum = accum * correct[..., None] + jnp.einsum(
            "grtm,mgd->grtd", weight.astype(bf16), value_block, preferred_element_type=f32
        )
        return (newest, totals, accum), None

    start = (jnp.full(shape, -1e30, f32), jnp.zeros(shape, f32), jnp.zeros(shape + (HD,), f32))
    (_, totals, accum), _ = lax.scan(
        visit, start, (key_blocks, value_blocks, jnp.arange(count // width, dtype=jnp.int32))
    )
    attended = accum / totals[..., None]
    return jnp.transpose(attended, (2, 0, 1, 3)).reshape(tokens_here, AH * HD).astype(bf16)


def on_device(
    x_in,
    z_in,
    bc_in,
    dt_raw,
    a_log,
    dt_bias,
    d_skip,
    conv_x,
    conv_bc,
    norm_gain,
    seg_ids,
    query,
    keys,
    values,
):
    ranks = lax.axis_size("ctx")
    rows, width = x_in.shape[1:]
    share = BLK // rows
    blocks = ranks // share
    piece = width // share
    chunk = piece // CHUNKS
    reach = -(-(rows * ranks // 2 - 1) // rows)
    shape = jax.ShapeDtypeStruct
    state_type = bf16 if blocks <= 2 else f32

    packed = call(
        functools.partial(pack_body, share, chunk),
        [shape((rows, chunk + 4 * LANES), bf16)] * share
        + [shape((rows, chunk), bf16)] * share
        + [shape((rows + 16, 4 * LANES), bf16)] * (share + 1),
        bytes_accessed=5 * 2**20,
    )(x_in[0], bc_in[0], dt_raw[0], seg_ids, keys[0], values[0])
    a_send, b_send, kv_send = packed[:share], packed[share : 2 * share], packed[2 * share :]
    order = [2, 3, 1]
    a_here, b_here = {0: a_send[0]}, {0: b_send[0]}
    for m in order:
        a_here[m] = crossed(a_send[m], "ctx", m)
    kv_here = [kv_send[0]] + [shifted(kv_send[r], "ctx", r) for r in range(1, share + 1)]
    for m in order:
        b_here[m] = crossed(b_send[m], "ctx", m)
    a_all = [a_here[m] for m in range(share)]
    b_all = [b_here[m] for m in range(share)]

    per_token = shape((BLK, LANES), f32)
    xc_a, bcc, state_a, ids_col, cum, step, writes, keep = call(
        functools.partial(first_body, share),
        [
            shape((BLK, chunk), bf16),
            shape((BLK, 2 * LANES), bf16),
            shape((LANES, chunk), state_type),
            shape((BLK + 8, LANES), f32),
            per_token,
            per_token,
            shape((BLK, LANES), bf16),
            per_token,
        ],
        scratch=[
            pltpu.VMEM((BLK + 8, chunk), f32),
            pltpu.VMEM((BLK + 8, 4 * LANES), f32),
            pltpu.VMEM((3, BLK, LANES), f32),
        ],
        flops=2**28,
        bytes_accessed=3 * 2**20,
    )(*kv_here[1:], *a_all, conv_x[0], conv_bc[0], dt_bias, a_log)
    xc_b, state_b = call(
        functools.partial(second_body, share),
        [shape((BLK, chunk), bf16), shape((LANES, chunk), state_type)],
        scratch=[pltpu.VMEM((BLK + 8, chunk), f32), pltpu.VMEM((3, BLK, LANES), f32)],
        flops=2**28,
        bytes_accessed=3 * 2**20,
    )(*kv_here[1:], *b_all, conv_x[0], bcc, ids_col, writes)

    def entering(state, first):
        if blocks > 2:
            heads = chunk // HD
            fade = jnp.repeat(keep[BLK - 1, first : first + heads], HD)[None, :]
            far = 1
            while far < blocks:
                came, came_fade = (
                    shifted(state, "ctx", far * share),
                    shifted(fade, "ctx", far * share),
                )
                state = state + fade * came
                fade = fade * came_fade
                far *= 2
        return shifted(state, "ctx", share).astype(bf16)

    entry_a = entering(state_a, 0)
    entry_b = entering(state_b, chunk // HD)

    local_a, local_b = call(
        functools.partial(mixing_body, share),
        [shape((BLK, chunk), f32)] * CHUNKS,
        flops=2**31,
        bytes_accessed=4 * 2**20,
    )(xc_a, xc_b, bcc, ids_col, cum, step, d_skip)

    if reach <= share:
        attended = call(
            functools.partial(attention_body, reach),
            shape((rows, AH * HD), bf16),
            flops=2**30,
            bytes_accessed=2**20,
        )(query[0], *kv_here[: reach + 1])
    else:
        attended = gathered_attention(query[0], keys[0], values[0], seg_ids[0])
    handoff = from_behind(attended, "pipe", 1)

    sent = []
    for c, (entry, local) in enumerate(((entry_a, local_a), (entry_b, local_b))):
        y = call(
            functools.partial(finish_kernel, share, c * (chunk // HD)),
            [shape((rows, chunk), bf16)] * share,
            scratch=[pltpu.VMEM((BLK, chunk), f32)],
            flops=2**28,
            bytes_accessed=2 * 2**20,
        )(entry, bcc, keep, local)
        here = {0: y[0]}
        for m in order:
            here[m] = crossed(y[m], "ctx", m)
        sent += [here[m] for m in range(share)]
    mamba_out = call(
        functools.partial(norm_body, share),
        shape((rows, width), bf16),
        bytes_accessed=3 * 2**20,
    )(*sent, z_in[0], norm_gain)
    return (mamba_out[None], handoff[None])


def solution(mesh):
    in_specs = (
        P("pipe", "ctx", None),
        P("pipe", "ctx", None),
        P("pipe", "ctx", None),
        P("pipe", "ctx", None),
        P("pipe", None),
        P("pipe", None),
        P("pipe", None),
        P("pipe", None, None),
        P("pipe", None, None),
        P("pipe", None),
        P("pipe", "ctx"),
        P("pipe", "ctx", None),
        P("pipe", "ctx", None),
        P("pipe", "ctx", None),
    )
    out_specs = (P("pipe", "ctx", None), P("pipe", "ctx", None))
    return jax.shard_map(
        on_device, mesh=mesh, in_specs=in_specs, out_specs=out_specs, check_vma=False
    )
```

time: 317 us -> 75.8 us (0.24)
  the two profiles are of different devices: /device:TPU:0 before, /device:TPU:29 now
where the time goes in v1:
time: 75.8 us; the launch traced here: 75.3 us
  waiting for transfers between devices  31.7 us (42%)
  starting transfers between devices  24.2 us (32%)
  Pallas kernels  11.5 us (15%)
  local copies, waits for them, and re-layouts  7.03 us (9%)
  between operations  0.83 us (1%)
    ppermute x6, waiting for transfers between devices, shifted(): lax.ppermute(value, axis, [(i, i + steps) for i in range(count - steps)])  23.3 us
    ppermute x12, starting transfers between devices, crossed(): return lax.ppermute(value, axis, [(i, i ^ mask) for i in range(count)])  15.2 us
    ppermute x12, waiting for transfers between devices, crossed(): return lax.ppermute(value, axis, [(i, i ^ mask) for i in range(count)])  8.38 us
    ppermute x6, starting transfers between devices, shifted(): lax.ppermute(value, axis, [(i, i + steps) for i in range(count - steps)])  7.72 us
    unnamed x29, local copies, waits for them, and re-layouts  7.03 us
    pallas_call x1, Pallas kernels, on_device(): call(functools.partial(first_body, share), [shape((BLK, chunk), bf16), sh...  2.37 us
    pallas_call x1, Pallas kernels, on_device(): call(functools.partial(mixing_body, share), [shape((BLK, chunk), f32)] *...  2.32 us
    pallas_call x1, Pallas kernels, on_device(): call(functools.partial(attention_body, reach), shape((rows, AH * HD), bf1...  1.92 us
  transfers between devices with their start and end apart: 19, of which 8 were waited for; matrix products, arithmetic and copies ran while one was open for 0% of the time, Pallas kernels for 13%

profile of v1, /device:TPU:29, one launch (start us, length us, event | category | flops | bytes accessed | tf_op | source)
XLA Modules:
  0.0 75.3 jit_solution(15526851082244345966)
XLA Ops:
  0.6 0.6 copy-done.9
  1.3 1.2 %copy-done.1 = bf16[1,64,8192]{2,1,0:T(8,128)(2,1)S(1)} copy-done((bf16[1,64,8192]{2,1,0:T(8,128)(2,1)S(1)}, bf16[1,64,8192]{2,1,0:T(8,128)(2,1)}, u32[]{:S(2)}) %copy-start.1) | copy-done | bytes 1048600
  2.5 0.9 %copy-done.3 = bf16[1,64,1024]{2,1,0:T(8,128)(2,1)S(1)} copy-done((bf16[1,64,1024]{2,1,0:T(8,128)(2,1)S(1)}, bf16[1,64,1024]{2,1,0:T(8,128)(2,1)}, u32[]{:S(2)}) %copy-start.3) | copy-done | bytes 131096
  3.4 0.8 %copy-done.5 = bf16[1,64,256]{2,1,0:T(8,128)(2,1)S(1)} copy-done((bf16[1,64,256]{2,1,0:T(8,128)(2,1)S(1)}, bf16[1,64,256]{2,1,0:T(8,128)(2,1)}, u32[]{:S(2)}) %copy-start.5) | copy-done | bytes 32792
  4.2 0.8 %copy-done.6 = bf16[1,64,256]{2,1,0:T(8,128)(2,1)S(1)} copy-done((bf16[1,64,256]{2,1,0:T(8,128)(2,1)S(1)}, bf16[1,64,256]{2,1,0:T(8,128)(2,1)}, u32[]{:S(2)}) %copy-start.6) | copy-done | bytes 32792
  4.9 0.7 copy-done.7
  5.9 0.7 collective-permute-start.4
  6.8 1.5 %collective-permute-start.6 = (bf16[64,1536]{1,0:T(8,128)(2,1)S(1)}, bf16[64,1536]{1,0:T(8,128)(2,1)S(1)}, u32[]{:S(2)}, u32[]{:S(2)}) collective-permute-start(bf16[64,1536]{1,0:T(8,128)(2,1)S(1)} %get-tuple-element.42), channel_id=1, source_target_pairs={{0,3},{1,2},{2,1},{3,0},{4,7},{5,6},{6,5},{7,4},{8,11},{9,10},{10,... | collective-permute-start | bytes 589832 | tf_op jit(solution)/shard_map/ppermute | solution.py:32
  8.3 1.3 %collective-permute-start = (bf16[80,512]{1,0:T(8,128)(2,1)S(1)}, bf16[80,512]{1,0:T(8,128)(2,1)S(1)}, u32[]{:S(2)}, u32[]{:S(2)}) collective-permute-start(bf16[80,512]{1,0:T(8,128)(2,1)S(1)} %get-tuple-element.35), channel_id=1, source_target_pairs={{0,1},{1,2},{2,3},{3,4},{4,5},{5,6},{6,7},{8,9},{9,10},{10,11},{11... | collective-permute-start | bytes 245768 | tf_op jit(solution)/shard_map/ppermute | solution.py:27
  9.6 1.3 %collective-permute-start.1 = (bf16[80,512]{1,0:T(8,128)(2,1)S(1)}, bf16[80,512]{1,0:T(8,128)(2,1)S(1)}, u32[]{:S(2)}, u32[]{:S(2)}) collective-permute-start(bf16[80,512]{1,0:T(8,128)(2,1)S(1)} %get-tuple-element.36), channel_id=1, source_target_pairs={{0,2},{1,3},{2,4},{3,5},{4,6},{5,7},{8,10},{9,11},{10,12},{11,13},... | collective-permute-start | bytes 245768 | tf_op jit(solution)/shard_map/ppermute | solution.py:27
  11.5 1.3 %collective-permute-start.2 = (bf16[80,512]{1,0:T(8,128)(2,1)S(1)}, bf16[80,512]{1,0:T(8,128)(2,1)S(1)}, u32[]{:S(2)}, u32[]{:S(2)}) collective-permute-start(bf16[80,512]{1,0:T(8,128)(2,1)S(1)} %get-tuple-element.37), channel_id=1, source_target_pairs={{0,3},{1,4},{2,5},{3,6},{4,7},{8,11},{9,12},{10,13},{11,14},{12,15... | collective-permute-start | bytes 245768 | tf_op jit(solution)/shard_map/ppermute | solution.py:27
  12.8 7.8 %collective-permute-done.1.refs_1_.refs_2_ = bf16[80,512]{1,0:T(8,128)(2,1)S(1)} collective-permute-done((bf16[80,512]{1,0:T(8,128)(2,1)S(1)}, bf16[80,512]{1,0:T(8,128)(2,1)S(1)}, u32[]{:S(2)}, u32[]{:S(2)}) %collective-permute-start.1) | collective-permute-done | bytes 81952 | tf_op jit(solution)/shard_map/ppermute | solution.py:27
  20.5 1.3 %collective-permute-start.3 = (bf16[80,512]{1,0:T(8,128)(2,1)S(1)}, bf16[80,512]{1,0:T(8,128)(2,1)S(1)}, u32[]{:S(2)}, u32[]{:S(2)}) collective-permute-start(bf16[80,512]{1,0:T(8,128)(2,1)S(1)} %get-tuple-element.38), channel_id=1, source_target_pairs={{0,4},{1,5},{2,6},{3,7},{8,12},{9,13},{10,14},{11,15},{16,20},{17,... | collective-permute-start | bytes 245768 | tf_op jit(solution)/shard_map/ppermute | solution.py:27
  21.8 6.3 %collective-permute-start.8 = (bf16[64,1024]{1,0:T(8,128)(2,1)S(1)}, bf16[64,1024]{1,0:T(8,128)(2,1)S(1)}, u32[]{:S(2)}, u32[]{:S(2)}) collective-permute-start(bf16[64,1024]{1,0:T(8,128)(2,1)S(1)} %get-tuple-element.48), channel_id=1, source_target_pairs={{0,1},{1,0},{2,3},{3,2},{4,5},{5,4},{6,7},{7,6},{8,9},{9,8},{10,11... | collective-permute-start | bytes 393224 | tf_op jit(solution)/shard_map/ppermute | solution.py:32
  28.1 0.8 %collective-permute-done.3.refs_3_.refs_4_ = bf16[80,512]{1,0:T(8,128)(2,1)S(1)} collective-permute-done((bf16[80,512]{1,0:T(8,128)(2,1)S(1)}, bf16[80,512]{1,0:T(8,128)(2,1)S(1)}, u32[]{:S(2)}, u32[]{:S(2)}) %collective-permute-start.3) | collective-permute-done | bytes 81952 | tf_op jit(solution)/shard_map/ppermute | solution.py:27
  29.0 2.0 %collective-permute-start.10 = (bf16[64,1024]{1,0:T(8,128)(2,1)S(1)}, bf16[64,1024]{1,0:T(8,128)(2,1)S(1)}, u32[]{:S(2)}, u32[]{:S(2)}) collective-permute-start(bf16[64,1024]{1,0:T(8,128)(2,1)S(1)} %get-tuple-element.50), channel_id=1, source_target_pairs={{0,3},{1,2},{2,1},{3,0},{4,7},{5,6},{6,5},{7,4},{8,11},{9,10},{10,... | collective-permute-start | bytes 393224 | tf_op jit(solution)/shard_map/ppermute | solution.py:32
  31.7 2.4 %shard_map.150 = (bf16[256,1024]{1,0:T(8,128)(2,1)S(1)}, bf16[256,256]{1,0:T(8,128)(2,1)S(1)}, bf16[128,1024]{1,0:T(8,128)(2,1)S(1)}, f32[264,128]{1,0:T(8,128)S...) custom-call(bf16[80,512]{1,0:T(8,128)(2,1)S(1)} %collective-permute-, ...), custom_call_target="tpu_custom_call" | custom-call | flops 268435456 | bytes 3145728 | tf_op jit(solution)/shard_map/pallas_call | solution.py:489
  34.1 1.3 %collective-permute-start.7 = (bf16[128,1024]{1,0:T(8,128)(2,1)S(1)}, bf16[128,1024]{1,0:T(8,128)(2,1)S(1)}, u32[]{:S(2)}, u32[]{:S(2)}) collective-permute-start(bf16[128,1024]{1,0:T(8,128)(2,1)S(1)} %get-tuple-element.43), channel_id=1, source_target_pairs={{0,4},{1,5},{2,6},{3,7},{8,12},{9,13},{10,14},{11,15},{16,20},{17,... | collective-permute-start | bytes 786440 | tf_op jit(solution)/shard_map/ppermute | solution.py:27
  35.4 1.9 %shard_map.156 = bf16[64,2048]{1,0:T(8,128)(2,1)S(1)} custom-call(bf16[64,2048]{1,0:T(8,128)(2,1)S(1)} %bitcast.20, bf16[80,512]{1,0:T(8,128)(2,1)S(1)} %get-tuple-element.67.refs_0_, bf16[80,512]{1,0:T(8,128)(2,1)S(1)} %collective-permute-done.refs_0_.refs_1_, bf16[80,512]{1,0:T(8,128)(2,1)S(1)} %collective-permute-done.1.refs_1_.refs_2_, ...), custom_call_target="tpu_custom_call" | custom-call | flops 1073741824 | bytes 1048576 | tf_op jit(solution)/shard_map/pallas_call | solution.py:543
  37.3 1.3 %collective-permute-start.18 = (bf16[64,2048]{1,0:T(8,128)(2,1)S(1)}, bf16[64,2048]{1,0:T(8,128)(2,1)S(1)}, u32[]{:S(2)}, u32[]{:S(2)}) collective-permute-start(bf16[64,2048]{1,0:T(8,128)(2,1)S(1)} %shard_map.156), channel_id=1, source_target_pairs={{0,8},{8,16},{16,24},{24,0},{1,9},{9,17},{17,25},{25,1},{2,10},{10... | collective-permute-start | bytes 786440 | tf_op jit(solution)/shard_map/ppermute | solution.py:37
  38.6 1.8 %shard_map.151 = (bf16[256,1024]{1,0:T(8,128)(2,1)S(1)}, bf16[128,1024]{1,0:T(8,128)(2,1)S(1)}) custom-call(bf16[80,512]{1,0:T(8,128)(2,1)S(1)} %collective-permute-done.refs_0_.refs_1_, bf16[80,512]{1,0:T(8,128)(2,1)S(1)} %collective-permute-done.1.refs_1_.refs_2_, bf16[80,512]{1,0:T(8,128)(2,1)S(1)} %collective-permute-done.2.refs_2_.refs_3_, ...), custom_call_target="tpu_custom_call" | custom-call | flops 268435456 | bytes 3145728 | tf_op jit(solution)/shard_map/pallas_call | solution.py:509
  40.4 1.3 %collective-permute-start.14 = (bf16[128,1024]{1,0:T(8,128)(2,1)S(1)}, bf16[128,1024]{1,0:T(8,128)(2,1)S(1)}, u32[]{:S(2)}, u32[]{:S(2)}) collective-permute-start(bf16[128,1024]{1,0:T(8,128)(2,1)S(1)} %get-tuple-element.61), channel_id=1, source_target_pairs={{0,4},{1,5},{2,6},{3,7},{8,12},{9,13},{10,14},{11,15},{16,20},{17,... | collective-permute-start | bytes 786440 | tf_op jit(solution)/shard_map/ppermute | solution.py:27
  42.3 2.3 %shard_map.152 = (f32[256,1024]{1,0:T(8,128)S(1)}, f32[256,1024]{1,0:T(8,128)S(1)}) custom-call(bf16[256,1024]{1,0:T(8,128)(2,1)S(1)} %get-tuple-element.46.refs_0_, bf16[256,1024]{1,0:T(8,128)(2,1)S(1)} %get-tuple-element.53.refs_1_, bf16[256,256]{1,0:T(8,128)(2,1)S(1)} %get-tuple-element.44.refs_9_.refs_2_.bcc, ...), custom_call_target="tpu_custom_call" | custom-call | flops 2147483648 | bytes 4194304 | tf_op jit(solution)/shard_map/pallas_call | solution.py:535
  44.7 11.2 %collective-permute-done.7.state = bf16[128,1024]{1,0:T(8,128)(2,1)S(1)} collective-permute-done((bf16[128,1024]{1,0:T(8,128)(2,1)S(1)}, bf16[128,1024]{1,0:T(8,128)(2,1)S(1)}, u32[]{:S(2)}, u32[]{:S(2)}) %collective-permute-start.7) | collective-permute-done | bytes 262176 | tf_op jit(solution)/shard_map/ppermute | solution.py:27
  56.9 1.7 %collective-permute-start.13 = (bf16[64,1024]{1,0:T(8,128)(2,1)S(1)}, bf16[64,1024]{1,0:T(8,128)(2,1)S(1)}, u32[]{:S(2)}, u32[]{:S(2)}) collective-permute-start(bf16[64,1024]{1,0:T(8,128)(2,1)S(1)} %get-tuple-element.60), channel_id=1, source_target_pairs={{0,3},{1,2},{2,1},{3,0},{4,7},{5,6},{6,5},{7,4},{8,11},{9,10},{10,... | collective-permute-start | bytes 393224 | tf_op jit(solution)/shard_map/ppermute | solution.py:32
  58.6 2.9 %collective-permute-done.14.state = bf16[128,1024]{1,0:T(8,128)(2,1)S(1)} collective-permute-done((bf16[128,1024]{1,0:T(8,128)(2,1)S(1)}, bf16[128,1024]{1,0:T(8,128)(2,1)S(1)}, u32[]{:S(2)}, u32[]{:S(2)}) %collective-permute-start.14) | collective-permute-done | bytes 262176 | tf_op jit(solution)/shard_map/ppermute | solution.py:27
  62.6 1.7 %collective-permute-start.17 = (bf16[64,1024]{1,0:T(8,128)(2,1)S(1)}, bf16[64,1024]{1,0:T(8,128)(2,1)S(1)}, u32[]{:S(2)}, u32[]{:S(2)}) collective-permute-start(bf16[64,1024]{1,0:T(8,128)(2,1)S(1)} %get-tuple-element.66), channel_id=1, source_target_pairs={{0,3},{1,2},{2,1},{3,0},{4,7},{5,6},{6,5},{7,4},{8,11},{9,10},{10,... | collective-permute-start | bytes 393224 | tf_op jit(solution)/shard_map/ppermute | solution.py:32
  64.4 2.7 %collective-permute-done.13.refs_3_ = bf16[64,1024]{1,0:T(8,128)(2,1)S(1)} collective-permute-done((bf16[64,1024]{1,0:T(8,128)(2,1)S(1)}, bf16[64,1024]{1,0:T(8,128)(2,1)S(1)}, u32[]{:S(2)}, u32[]{:S(2)}) %collective-permute-start.13) | collective-permute-done | bytes 131104 | tf_op jit(solution)/shard_map/ppermute | solution.py:32
  67.1 2.8 %collective-permute-done.16.refs_6_ = bf16[64,1024]{1,0:T(8,128)(2,1)S(1)} collective-permute-done((bf16[64,1024]{1,0:T(8,128)(2,1)S(1)}, bf16[64,1024]{1,0:T(8,128)(2,1)S(1)}, u32[]{:S(2)}, u32[]{:S(2)}) %collective-permute-start.16) | collective-permute-done | bytes 131104 | tf_op jit(solution)/shard_map/ppermute | solution.py:32
  69.9 2.8 %collective-permute-done.17.refs_7_ = bf16[64,1024]{1,0:T(8,128)(2,1)S(1)} collective-permute-done((bf16[64,1024]{1,0:T(8,128)(2,1)S(1)}, bf16[64,1024]{1,0:T(8,128)(2,1)S(1)}, u32[]{:S(2)}, u32[]{:S(2)}) %collective-permute-start.17) | collective-permute-done | bytes 131104 | tf_op jit(solution)/shard_map/ppermute | solution.py:32
  72.7 1.8 %shard_map.155 = bf16[64,8192]{1,0:T(8,128)(2,1)} custom-call(bf16[64,1024]{1,0:T(8,128)(2,1)S(1)} %get-tuple-element.57.refs_0_, bf16[64,1024]{1,0:T(8,128)(2,1)S(1)} %collective-permute-done.11.refs_1_, bf16[64,1024]{1,0:T(8,128)(2,1)S(1)} %collective-permute-done.12.refs_2_, bf16[64,1024]{1,0:T(8,128)(2,1)S(1)} %collective-permute-done.13.refs_3_, ...), custom_call_target="tpu_custom_call" | custom-call | bytes 3145728 | tf_op jit(solution)/shard_map/pallas_call | solution.py:566
  74.6 0.7 copy.17
  (43 shorter events, 4.4 us)
Async XLA Ops:
  1.3 1.2 %copy-start.1 = (bf16[1,64,8192]{2,1,0:T(8,128)(2,1)S(1)}, bf16[1,64,8192]{2,1,0:T(8,128)(2,1)}, u32[]{:S(2)}) copy-start(bf16[1,64,8192]{2,1,0:T(8,128)(2,1)} %param.14) | copy-start | bytes 3145732
  2.5 0.9 %copy-start.3 = (bf16[1,64,1024]{2,1,0:T(8,128)(2,1)S(1)}, bf16[1,64,1024]{2,1,0:T(8,128)(2,1)}, u32[]{:S(2)}) copy-start(bf16[1,64,1024]{2,1,0:T(8,128)(2,1)} %param.16) | copy-start | bytes 393220
  3.4 0.8 %copy-start.5 = (bf16[1,64,256]{2,1,0:T(8,128)(2,1)S(1)}, bf16[1,64,256]{2,1,0:T(8,128)(2,1)}, u32[]{:S(2)}) copy-start(bf16[1,64,256]{2,1,0:T(8,128)(2,1)} %param.26) | copy-start | bytes 98308
  4.2 0.8 %copy-start.6 = (bf16[1,64,256]{2,1,0:T(8,128)(2,1)S(1)}, bf16[1,64,256]{2,1,0:T(8,128)(2,1)}, u32[]{:S(2)}) copy-start(bf16[1,64,256]{2,1,0:T(8,128)(2,1)} %param.27) | copy-start | bytes 98308
  4.9 0.7 copy-start.7
  5.7 25.4 %copy-start.2 = (bf16[1,4,8192]{2,1,0:T(4,128)(2,1)S(1)}, bf16[1,4,8192]{2,1,0:T(4,128)(2,1)}, u32[]{:S(2)}) copy-start(bf16[1,4,8192]{2,1,0:T(4,128)(2,1)} %param.21) | copy-start | bytes 196612
  5.9 23.1 %collective-permute-start.4 = (bf16[64,1536]{1,0:T(8,128)(2,1)S(1)}, bf16[64,1536]{1,0:T(8,128)(2,1)S(1)}, u32[]{:S(2)}, u32[]{:S(2)}) collective-permute-start(bf16[64,1536]{1,0:T(8,128)(2,1)S(1)} %get-tuple-element.40), channel_id=1, source_target_pairs={{0,1},{1,0},{2,3},{3,2},{4,5},{5,4},{6,7},{7,6},{8,9},{9,8},{10,11... | collective-permute-start | bytes 589832 | tf_op jit(solution)/shard_map/ppermute | solution.py:32
  6.6 24.4 %collective-permute-start.5 = (bf16[64,1536]{1,0:T(8,128)(2,1)S(1)}, bf16[64,1536]{1,0:T(8,128)(2,1)S(1)}, u32[]{:S(2)}, u32[]{:S(2)}) collective-permute-start(bf16[64,1536]{1,0:T(8,128)(2,1)S(1)} %get-tuple-element.41), channel_id=1, source_target_pairs={{0,2},{1,3},{2,0},{3,1},{4,6},{5,7},{6,4},{7,5},{8,10},{9,11},{10,... | collective-permute-start | bytes 589832 | tf_op jit(solution)/shard_map/ppermute | solution.py:32
  6.8 24.2 %collective-permute-start.6 = (bf16[64,1536]{1,0:T(8,128)(2,1)S(1)}, bf16[64,1536]{1,0:T(8,128)(2,1)S(1)}, u32[]{:S(2)}, u32[]{:S(2)}) collective-permute-start(bf16[64,1536]{1,0:T(8,128)(2,1)S(1)} %get-tuple-element.42), channel_id=1, source_target_pairs={{0,3},{1,2},{2,1},{3,0},{4,7},{5,6},{6,5},{7,4},{8,11},{9,10},{10,... | collective-permute-start | bytes 589832 | tf_op jit(solution)/shard_map/ppermute | solution.py:32
  8.3 3.2 %collective-permute-start = (bf16[80,512]{1,0:T(8,128)(2,1)S(1)}, bf16[80,512]{1,0:T(8,128)(2,1)S(1)}, u32[]{:S(2)}, u32[]{:S(2)}) collective-permute-start(bf16[80,512]{1,0:T(8,128)(2,1)S(1)} %get-tuple-element.35), channel_id=1, source_target_pairs={{0,1},{1,2},{2,3},{3,4},{4,5},{5,6},{6,7},{8,9},{9,10},{10,11},{11... | collective-permute-start | bytes 245768 | tf_op jit(solution)/shard_map/ppermute | solution.py:27
  9.6 21.4 %copy-start.8 = (bf16[1,4,1024]{2,1,0:T(4,128)(2,1)S(1)}, bf16[1,4,1024]{2,1,0:T(4,128)(2,1)}, u32[]{:S(2)}) copy-start(bf16[1,4,1024]{2,1,0:T(4,128)(2,1)} %param.22) | copy-start | bytes 24580
  9.6 10.9 %collective-permute-start.1 = (bf16[80,512]{1,0:T(8,128)(2,1)S(1)}, bf16[80,512]{1,0:T(8,128)(2,1)S(1)}, u32[]{:S(2)}, u32[]{:S(2)}) collective-permute-start(bf16[80,512]{1,0:T(8,128)(2,1)S(1)} %get-tuple-element.36), channel_id=1, source_target_pairs={{0,2},{1,3},{2,4},{3,5},{4,6},{5,7},{8,10},{9,11},{10,12},{11,13},... | collective-permute-start | bytes 245768 | tf_op jit(solution)/shard_map/ppermute | solution.py:27
  11.5 10.3 %collective-permute-start.2 = (bf16[80,512]{1,0:T(8,128)(2,1)S(1)}, bf16[80,512]{1,0:T(8,128)(2,1)S(1)}, u32[]{:S(2)}, u32[]{:S(2)}) collective-permute-start(bf16[80,512]{1,0:T(8,128)(2,1)S(1)} %get-tuple-element.37), channel_id=1, source_target_pairs={{0,3},{1,4},{2,5},{3,6},{4,7},{8,11},{9,12},{10,13},{11,14},{12,15... | collective-permute-start | bytes 245768 | tf_op jit(solution)/shard_map/ppermute | solution.py:27
  20.5 8.4 %collective-permute-start.3 = (bf16[80,512]{1,0:T(8,128)(2,1)S(1)}, bf16[80,512]{1,0:T(8,128)(2,1)S(1)}, u32[]{:S(2)}, u32[]{:S(2)}) collective-permute-start(bf16[80,512]{1,0:T(8,128)(2,1)S(1)} %get-tuple-element.38), channel_id=1, source_target_pairs={{0,4},{1,5},{2,6},{3,7},{8,12},{9,13},{10,14},{11,15},{16,20},{17,... | collective-permute-start | bytes 245768 | tf_op jit(solution)/shard_map/ppermute | solution.py:27
  21.8 16.7 %collective-permute-start.8 = (bf16[64,1024]{1,0:T(8,128)(2,1)S(1)}, bf16[64,1024]{1,0:T(8,128)(2,1)S(1)}, u32[]{:S(2)}, u32[]{:S(2)}) collective-permute-start(bf16[64,1024]{1,0:T(8,128)(2,1)S(1)} %get-tuple-element.48), channel_id=1, source_target_pairs={{0,1},{1,0},{2,3},{3,2},{4,5},{5,4},{6,7},{7,6},{8,9},{9,8},{10,11... | collective-permute-start | bytes 393224 | tf_op jit(solution)/shard_map/ppermute | solution.py:32
  29.0 9.6 %collective-permute-start.9 = (bf16[64,1024]{1,0:T(8,128)(2,1)S(1)}, bf16[64,1024]{1,0:T(8,128)(2,1)S(1)}, u32[]{:S(2)}, u32[]{:S(2)}) collective-permute-start(bf16[64,1024]{1,0:T(8,128)(2,1)S(1)} %get-tuple-element.49), channel_id=1, source_target_pairs={{0,2},{1,3},{2,0},{3,1},{4,6},{5,7},{6,4},{7,5},{8,10},{9,11},{10,... | collective-permute-start | bytes 393224 | tf_op jit(solution)/shard_map/ppermute | solution.py:32
  29.0 9.6 %collective-permute-start.10 = (bf16[64,1024]{1,0:T(8,128)(2,1)S(1)}, bf16[64,1024]{1,0:T(8,128)(2,1)S(1)}, u32[]{:S(2)}, u32[]{:S(2)}) collective-permute-start(bf16[64,1024]{1,0:T(8,128)(2,1)S(1)} %get-tuple-element.50), channel_id=1, source_target_pairs={{0,3},{1,2},{2,1},{3,0},{4,7},{5,6},{6,5},{7,4},{8,11},{9,10},{10,... | collective-permute-start | bytes 393224 | tf_op jit(solution)/shard_map/ppermute | solution.py:32
  31.0 0.7 copy-start.10
  31.0 0.7 copy-start.11
  31.7 3.7 %copy-start.12 = (bf16[1,64,2048]{2,1,0:T(8,128)(2,1)S(1)}, bf16[1,64,2048]{2,1,0:T(8,128)(2,1)}, u32[]{:S(2)}) copy-start(bf16[1,64,2048]{2,1,0:T(8,128)(2,1)} %param.25) | copy-start | bytes 786436
  34.1 21.8 %collective-permute-start.7 = (bf16[128,1024]{1,0:T(8,128)(2,1)S(1)}, bf16[128,1024]{1,0:T(8,128)(2,1)S(1)}, u32[]{:S(2)}, u32[]{:S(2)}) collective-permute-start(bf16[128,1024]{1,0:T(8,128)(2,1)S(1)} %get-tuple-element.43), channel_id=1, source_target_pairs={{0,4},{1,5},{2,6},{3,7},{8,12},{9,13},{10,14},{11,15},{16,20},{17,... | collective-permute-start | bytes 786440 | tf_op jit(solution)/shard_map/ppermute | solution.py:27
  37.3 25.3 %collective-permute-start.18 = (bf16[64,2048]{1,0:T(8,128)(2,1)S(1)}, bf16[64,2048]{1,0:T(8,128)(2,1)S(1)}, u32[]{:S(2)}, u32[]{:S(2)}) collective-permute-start(bf16[64,2048]{1,0:T(8,128)(2,1)S(1)} %shard_map.156), channel_id=1, source_target_pairs={{0,8},{8,16},{16,24},{24,0},{1,9},{9,17},{17,25},{25,1},{2,10},{10... | collective-permute-start | bytes 786440 | tf_op jit(solution)/shard_map/ppermute | solution.py:37
  40.4 21.2 %collective-permute-start.14 = (bf16[128,1024]{1,0:T(8,128)(2,1)S(1)}, bf16[128,1024]{1,0:T(8,128)(2,1)S(1)}, u32[]{:S(2)}, u32[]{:S(2)}) collective-permute-start(bf16[128,1024]{1,0:T(8,128)(2,1)S(1)} %get-tuple-element.61), channel_id=1, source_target_pairs={{0,4},{1,5},{2,6},{3,7},{8,12},{9,13},{10,14},{11,15},{16,20},{17,... | collective-permute-start | bytes 786440 | tf_op jit(solution)/shard_map/ppermute | solution.py:27
  41.7 0.7 copy-start.13
  56.4 16.3 %copy-start = (bf16[1,64,8192]{2,1,0:T(8,128)(2,1)S(1)}, bf16[1,64,8192]{2,1,0:T(8,128)(2,1)}, u32[]{:S(2)}) copy-start(bf16[1,64,8192]{2,1,0:T(8,128)(2,1)} %param.15) | copy-start | bytes 3145732
  56.4 6.2 %collective-permute-start.11 = (bf16[64,1024]{1,0:T(8,128)(2,1)S(1)}, bf16[64,1024]{1,0:T(8,128)(2,1)S(1)}, u32[]{:S(2)}, u32[]{:S(2)}) collective-permute-start(bf16[64,1024]{1,0:T(8,128)(2,1)S(1)} %get-tuple-element.58), channel_id=1, source_target_pairs={{0,1},{1,0},{2,3},{3,2},{4,5},{5,4},{6,7},{7,6},{8,9},{9,8},{10,11... | collective-permute-start | bytes 393224 | tf_op jit(solution)/shard_map/ppermute | solution.py:32
  56.9 7.4 %collective-permute-start.12 = (bf16[64,1024]{1,0:T(8,128)(2,1)S(1)}, bf16[64,1024]{1,0:T(8,128)(2,1)S(1)}, u32[]{:S(2)}, u32[]{:S(2)}) collective-permute-start(bf16[64,1024]{1,0:T(8,128)(2,1)S(1)} %get-tuple-element.59), channel_id=1, source_target_pairs={{0,2},{1,3},{2,0},{3,1},{4,6},{5,7},{6,4},{7,5},{8,10},{9,11},{10,... | collective-permute-start | bytes 393224 | tf_op jit(solution)/shard_map/ppermute | solution.py:32
  56.9 10.2 %collective-permute-start.13 = (bf16[64,1024]{1,0:T(8,128)(2,1)S(1)}, bf16[64,1024]{1,0:T(8,128)(2,1)S(1)}, u32[]{:S(2)}, u32[]{:S(2)}) collective-permute-start(bf16[64,1024]{1,0:T(8,128)(2,1)S(1)} %get-tuple-element.60), channel_id=1, source_target_pairs={{0,3},{1,2},{2,1},{3,0},{4,7},{5,6},{6,5},{7,4},{8,11},{9,10},{10,... | collective-permute-start | bytes 393224 | tf_op jit(solution)/shard_map/ppermute | solution.py:32
  61.5 11.2 %copy-start.4 = (f32[1,8192]{1,0:T(1,128)S(1)}, f32[1,8192]{1,0:T(1,128)}, u32[]{:S(2)}) copy-start(f32[1,8192]{1,0:T(1,128)} %refs_9_.1) | copy-start | bytes 98308
  62.1 5.0 %collective-permute-start.15 = (bf16[64,1024]{1,0:T(8,128)(2,1)S(1)}, bf16[64,1024]{1,0:T(8,128)(2,1)S(1)}, u32[]{:S(2)}, u32[]{:S(2)}) collective-permute-start(bf16[64,1024]{1,0:T(8,128)(2,1)S(1)} %get-tuple-element.64), channel_id=1, source_target_pairs={{0,1},{1,0},{2,3},{3,2},{4,5},{5,4},{6,7},{7,6},{8,9},{9,8},{10,11... | collective-permute-start | bytes 393224 | tf_op jit(solution)/shard_map/ppermute | solution.py:32
  62.6 7.3 %collective-permute-start.16 = (bf16[64,1024]{1,0:T(8,128)(2,1)S(1)}, bf16[64,1024]{1,0:T(8,128)(2,1)S(1)}, u32[]{:S(2)}, u32[]{:S(2)}) collective-permute-start(bf16[64,1024]{1,0:T(8,128)(2,1)S(1)} %get-tuple-element.65), channel_id=1, source_target_pairs={{0,2},{1,3},{2,0},{3,1},{4,6},{5,7},{6,4},{7,5},{8,10},{9,11},{10,... | collective-permute-start | bytes 393224 | tf_op jit(solution)/shard_map/ppermute | solution.py:32
  62.6 10.1 %collective-permute-start.17 = (bf16[64,1024]{1,0:T(8,128)(2,1)S(1)}, bf16[64,1024]{1,0:T(8,128)(2,1)S(1)}, u32[]{:S(2)}, u32[]{:S(2)}) collective-permute-start(bf16[64,1024]{1,0:T(8,128)(2,1)S(1)} %get-tuple-element.66), channel_id=1, source_target_pairs={{0,3},{1,2},{2,1},{3,0},{4,7},{5,6},{6,5},{7,4},{8,11},{9,10},{10,... | collective-permute-start | bytes 393224 | tf_op jit(solution)/shard_map/ppermute | solution.py:32
  (1 other events, 0.7 us)

commit v2 on v1

v2 whole, which is shorter than its diff:
```python
import functools
import math

import jax
import jax.numpy as jnp
from jax import lax
from jax.experimental import pallas as pl
from jax.experimental.pallas import tpu as pltpu
from jax.sharding import PartitionSpec as P

G = 4
AH = 32
KVH = 4
HD = 64
BLK = 256
LANES = 128
LOCAL_HEADS = 32
CHUNKS = 2
PACK_ROOM = 58
WHOLE = (False, False)

norm_eps = 1e-05
bf16 = jnp.bfloat16
f32 = jnp.float32


def shifted(value, axis, steps):
    count = lax.axis_size(axis)
    return lax.ppermute(value, axis, [(i, i + steps) for i in range(count - steps)])


def turned_on(value, axis, steps):
    count = lax.axis_size(axis)
    return lax.ppermute(value, axis, [(i, (i + steps) % count) for i in range(count)])


def crossed(value, axis, mask):
    count = lax.axis_size(axis)
    return lax.ppermute(value, axis, [(i, i ^ mask) for i in range(count)])


def iota(shape, dim):
    return lax.broadcasted_iota(jnp.int32, shape, dim)


def call(body, outs, scratch=(), flops=0, bytes_accessed=0, room=48, **specs):
    return pl.pallas_call(
        body,
        out_shape=outs,
        scratch_shapes=list(scratch),
        compiler_params=pltpu.CompilerParams(vmem_limit_bytes=int(room * 2**20)),
        cost_estimate=pl.CostEstimate(
            flops=flops, bytes_accessed=bytes_accessed, transcendentals=0
        ),
        **specs,
    )


def hbm():
    return pl.BlockSpec(memory_space=pltpu.HBM)


def vmem():
    return pl.BlockSpec(memory_space=pltpu.VMEM)


def pack_body(share, x_hbm, bc_hbm, dt_hbm, ids_ref, k_hbm, v_hbm, *refs):
    sends, seconds = refs[:share], refs[share : 2 * share]
    own_kv, near_kv, far_kv, bc_ref, dt_ref, sems, tails = refs[2 * share :]
    me = lax.rem(lax.axis_index("ctx"), share)
    rows, width = x_hbm.shape
    piece = width // share
    chunk = piece // CHUNKS
    states = bc_hbm.shape[1] // (2 * G)
    wide = 4 * LANES
    copies = [
        pltpu.make_async_copy(bc_hbm, bc_ref, sems.at[0]),
        pltpu.make_async_copy(dt_hbm, dt_ref, sems.at[1]),
    ]
    for m in (2, 3, 1, 0):
        for c, target in enumerate((sends[m].at[:, pl.ds(0, chunk)], seconds[m])):
            base = pl.multiple_of((me ^ m) * piece + c * chunk, LANES)
            copies.append(
                pltpu.make_async_copy(
                    x_hbm.at[:, pl.ds(base, chunk)], target, sems.at[2 + share * c + m]
                )
            )
    for i, kv in enumerate((own_kv, near_kv, far_kv)):
        for side, source in enumerate((k_hbm, v_hbm)):
            copies.append(
                pltpu.make_async_copy(
                    source,
                    kv.at[pl.ds(0, rows), pl.ds(side * wide // 2, wide // 2)],
                    sems.at[2 + 2 * share + 2 * i + side],
                )
            )
    copies.append(
        pltpu.make_async_copy(x_hbm.at[pl.ds(rows - 16, 16), :], tails, sems.at[2 * share + 8])
    )
    for copy in copies:
        copy.start()
    number = ids_ref[...].astype(f32) + 1.0
    square = iota((rows, rows), 0) == iota((rows, rows), 1)
    column = jnp.sum(
        jnp.where(square, jnp.broadcast_to(number, (rows, rows)), 0.0), axis=1, keepdims=True
    )
    lane = iota((rows, wide), 1)
    row = iota((rows, wide), 0)
    which = iota((16, wide), 0)
    small = iota((rows, LANES), 1)
    copies[0].wait()
    copies[1].wait()
    steps = dt_ref[...].astype(f32)

    def head_part(s):
        turned = pltpu.roll(steps, lax.rem(LANES - LOCAL_HEADS * s, LANES), 1)
        return jnp.where(small < LOCAL_HEADS, turned, column)

    for m in (2, 3, 1, 0):
        s = me ^ m
        b_at = pl.multiple_of(s * states, LANES)
        c_at = pl.multiple_of(G * states + s * states, LANES)
        sends[m][:, chunk : chunk + states] = bc_ref[:, pl.ds(b_at, states)]
        sends[m][:, chunk + states : chunk + 2 * states] = bc_ref[:, pl.ds(c_at, states)]
        sends[m][:, chunk + 2 * states :] = head_part(s).astype(bf16)
    for copy in copies[2:]:
        copy.wait()
    last = slice(rows - 16, rows)
    for slot, kv in enumerate((own_kv, near_kv, far_kv)):
        at = jnp.where(lane >= 3 * rows, lane - 3 * rows, lane)
        id_row = jnp.sum(jnp.where(at == row + rows * slot, column, 0.0), axis=0, keepdims=True)
        if slot == 0:
            kv[rows:, :] = jnp.where(which == 15, id_row, 0.0).astype(bf16)
            continue
        for part in range(2):
            s = 2 * (slot - 1) + part
            block = jnp.where(which == 15, id_row, 0.0)
            blocks = [
                tails[:, s * piece + p * wide : s * piece + (p + 1) * wide].astype(f32)
                for p in range(piece // wide)
            ]
            blocks.append(
                jnp.concatenate(
                    [
                        bc_ref[last, s * states : (s + 1) * states].astype(f32),
                        bc_ref[last, (G + s) * states : (G + s + 1) * states].astype(f32),
                        jnp.broadcast_to(column[last, :], (16, 2 * LANES)),
                    ],
                    axis=1,
                )
            )
            for i in range(3):
                for p, source in enumerate(blocks):
                    block = jnp.where(which == 5 * i + p, source[13 + i : 14 + i, :], block)
            kv[rows + 16 * part : rows + 16 * (part + 1), :] = block.astype(bf16)


def pick_halo(me, rows, mine, other):
    count = rows + 16
    second = count + rows
    third = second + rows + 32
    options = [
        other[second : second + 16, :],
        mine[second + 16 : second + 32, :],
        other[third : third + 16, :],
        mine[third + 16 : third + 32, :],
    ]
    picked = options[0].astype(f32)
    for j in range(1, 4):
        picked = jnp.where(me == j, options[j].astype(f32), picked)
    return jnp.where(lax.axis_index("ctx") >= 4, picked, 0.0)


def place_halo(scratch, picked, pieces):
    wide = picked.shape[1]
    for at, p in enumerate(pieces):
        which = iota((8, wide), 0)
        block = jnp.zeros((8, wide), f32)
        for i in range(3):
            block = jnp.where(which == 5 + i, picked[5 * i + p : 5 * i + p + 1, :], block)
        scratch[0:8, at * wide : (at + 1) * wide] = block


def conv_strip(src, columns, masks, taps):
    length = masks.shape[1]
    total = None
    for tap in range(4):
        term = taps[tap] * src[5 + tap : 5 + tap + length, columns]
        if tap < 3:
            term = term * masks[tap]
        total = term if total is None else total + term
    return (total * jax.nn.sigmoid(total)).astype(bf16)


def set_masks(masks, ids):
    length = masks.shape[1]
    own = ids[8 : 8 + length, :]
    for tap in range(3):
        masks[tap] = jnp.where(ids[5 + tap : 5 + tap + length, :] == own, 1.0, 0.0)


def taps_at(conv_ref, at):
    weights = conv_ref[:, pl.ds(pl.multiple_of(at, LANES), LANES)].astype(f32)
    return [weights[t : t + 1, :] for t in range(4)]


def one_hot(first, chunk):
    lane = iota((LANES, chunk), 0)
    head = iota((LANES, chunk), 1) // HD + first
    return jnp.where((lane % LOCAL_HEADS == head) & (lane < 3 * LOCAL_HEADS), 1.0, 0.0).astype(bf16)


def three_parts(value):
    lane = iota(value.shape, 1)
    high = value.astype(bf16).astype(f32)
    rest = value - high
    middle = rest.astype(bf16).astype(f32)
    low = rest - middle
    packed = jnp.where(
        lane < LOCAL_HEADS,
        high,
        jnp.where(
            lane < 2 * LOCAL_HEADS,
            pltpu.roll(middle, LOCAL_HEADS, 1),
            jnp.where(lane < 3 * LOCAL_HEADS, pltpu.roll(low, 2 * LOCAL_HEADS, 1), 0.0),
        ),
    )
    return packed.astype(bf16)


def conv_x_and_state(xs, masks, conv_ref, base, bcc, writes, first, xc_ref, state_ref):
    chunk = xc_ref.shape[1]
    for c in range(chunk // LANES):
        columns = slice(c * LANES, (c + 1) * LANES)
        xc_ref[:, columns] = conv_strip(xs, columns, masks, taps_at(conv_ref, base + c * LANES))
    factors = jnp.dot(writes, one_hot(first, chunk), preferred_element_type=f32)
    scaled = (xc_ref[...].astype(f32) * factors).astype(bf16)
    state = lax.dot_general(bcc, scaled, (((0,), (0,)), ((), ())), preferred_element_type=f32)
    state_ref[...] = state.astype(state_ref.dtype)


def turned(row, me):
    return pltpu.roll(
        jnp.broadcast_to(row, (8, LANES)), lax.rem(LANES - LOCAL_HEADS * me, LANES), 1
    )


def first_body(share, with_halo, *refs):
    pieces = refs[:share]
    convx, convbc, bias, alog = refs[share : share + 4]
    rest = refs[share + 4 :]
    me = lax.rem(lax.axis_index("ctx"), share)
    if with_halo:
        picked = pick_halo(me, pieces[0].shape[0], rest[0], rest[1])
        rest = rest[2:]
    xc_o, bcc_o, state_o, ids_o, cum_o, step_o, writes_o, xs, bs, masks = rest
    chunk = xc_o.shape[1]
    piece = chunk * CHUNKS
    rows = pieces[0].shape[0]
    length = rows * share
    per_block = 4 * LANES
    if with_halo:
        place_halo(xs, picked, list(range(chunk // per_block)))
        place_halo(bs, picked, [4])
    else:
        xs[0:8, :] = jnp.zeros((8, chunk), f32)
        bs[0:8, :] = jnp.zeros((8, per_block), f32)
    for m in range(share):
        at = pl.multiple_of(8 + rows * (me ^ m), 8)
        xs[pl.ds(at, rows), :] = pieces[m][:, :chunk].astype(f32)
        bs[pl.ds(at, rows), : 3 * LANES] = pieces[m][:, chunk:].astype(f32)
    where_ids = 2 * LANES + LOCAL_HEADS
    ids_o[...] = jnp.broadcast_to(bs[:, where_ids : where_ids + 1], (length + 8, LANES))
    set_masks(masks, ids_o)
    for half in range(2):
        columns = slice(half * LANES, (half + 1) * LANES)
        taps = taps_at(convbc, half * G * LANES + me * LANES)
        bcc_o[:, columns] = conv_strip(bs, columns, masks, taps)
    raw = bs[8:, 2 * LANES : 3 * LANES] + turned(bias[...], me)[0:1, :]
    step = jnp.maximum(raw, 0.0) + jnp.log1p(jnp.exp(-jnp.abs(raw)))
    total = step * (-jnp.exp(turned(alog[...], me)[0:1, :]))
    row = iota((length, LANES), 0)
    reach = 1
    while reach < length:
        total = total + jnp.where(row >= reach, pltpu.roll(total, reach, 0), 0.0)
        reach *= 2
    own = ids_o[8:, :]
    last = length - 1
    writes = (
        jnp.where(own == own[last : last + 1, :], jnp.exp(total[last : last + 1, :] - total), 0.0)
        * step
    )
    cum_o[...] = total
    step_o[...] = step
    packed = three_parts(writes)
    writes_o[...] = packed
    conv_x_and_state(xs, masks, convx, me * piece, bcc_o[:, :LANES], packed, 0, xc_o, state_o)


def second_body(share, with_halo, *refs):
    pieces = refs[:share]
    convx, bcc, ids, writes = refs[share : share + 4]
    rest = refs[share + 4 :]
    me = lax.rem(lax.axis_index("ctx"), share)
    if with_halo:
        picked = pick_halo(me, pieces[0].shape[0], rest[0], rest[1])
        rest = rest[2:]
    xc_o, state_o, xs, masks = rest
    chunk = xc_o.shape[1]
    rows = pieces[0].shape[0]
    blocks = chunk // (4 * LANES)
    if with_halo:
        place_halo(xs, picked, list(range(blocks, 2 * blocks)))
    else:
        xs[0:8, :] = jnp.zeros((8, chunk), f32)
    for m in range(share):
        at = pl.multiple_of(8 + rows * (me ^ m), 8)
        xs[pl.ds(at, rows), :] = pieces[m][...].astype(f32)
    set_masks(masks, ids)
    base = me * (chunk * CHUNKS) + chunk
    conv_x_and_state(
        xs, masks, convx, base, bcc[:, :LANES], writes[...], chunk // HD, xc_o, state_o
    )


def mixing_body(share, *refs):
    pieces, seconds = refs[:share], refs[share : 2 * share]
    xcs, refs = refs[2 * share : 2 * share + CHUNKS], refs[2 * share + CHUNKS :]
    mine, other, convx, convbc, bcc_in, cum, step, skip = refs[:8]
    rest = refs[8:]
    outs, (bcc, keep, head, head_ids, masks, first_x) = rest[:CHUNKS], rest[CHUNKS:]
    me = lax.rem(lax.axis_index("ctx"), share)
    length, chunk = xcs[0].shape
    rows = pieces[0].shape[0]
    piece = chunk * CHUNKS
    half = length // 2
    picked = pick_halo(me, rows, mine, other)
    place_halo(head, picked, list(range(5)))

    def first_rows(buffers, columns):
        start = buffers[0][:16, columns].astype(f32)
        for m in range(1, share):
            start = jnp.where(me == m, buffers[m][:16, columns].astype(f32), start)
        return start

    head[8:, :chunk] = first_rows(pieces, slice(0, chunk))
    head[8:, chunk:piece] = first_rows(seconds, slice(0, chunk))
    head[8:, piece : piece + 3 * LANES] = first_rows(pieces, slice(chunk, chunk + 3 * LANES))
    where_ids = piece + 2 * LANES + LOCAL_HEADS
    head_ids[...] = jnp.broadcast_to(head[:, where_ids : where_ids + 1], (24, LANES))
    set_masks(masks, head_ids)
    for c in range(piece // LANES):
        columns = slice(c * LANES, (c + 1) * LANES)
        first_x[:, columns] = conv_strip(
            head, columns, masks, taps_at(convx, me * piece + c * LANES)
        )
    bcc[16:, :] = bcc_in[16:, :]
    for side in range(2):
        columns = slice(piece + side * LANES, piece + (side + 1) * LANES)
        taps = taps_at(convbc, side * G * LANES + me * LANES)
        bcc[:16, side * LANES : (side + 1) * LANES] = conv_strip(head, columns, masks, taps)

    inner = lax.dot_general(
        bcc[:, LANES:], bcc[:, :LANES], (((1,), (1,)), ((), ())), preferred_element_type=f32
    )
    ids = []
    for i in range(share):
        part = pieces[0][:, chunk + 2 * LANES :].astype(f32)
        for m in range(1, share):
            part = jnp.where((me ^ m) == i, pieces[m][:, chunk + 2 * LANES :].astype(f32), part)
        ids.append(part)
    ids = jnp.concatenate(ids, axis=0)
    across = ids.T[LOCAL_HEADS : LOCAL_HEADS + 1, :]
    own = jnp.broadcast_to(ids[:, LOCAL_HEADS : LOCAL_HEADS + 1], (length, length))
    allowed = (iota((length, length), 0) >= iota((length, length), 1)) & (own == across)
    inner = jnp.where(allowed, inner, 0.0)
    cums = cum[...]
    keep[...] = jnp.where(own[:, :LANES] == head_ids[7:8, :], jnp.exp(cums), 0.0)
    cum_rows = cums.T
    step_rows = step[...].T
    gains = three_parts(turned(skip[...], me))
    even = iota((half, LANES), 1) < HD
    for c in range(CHUNKS):
        first = c * (chunk // HD)
        spread = jnp.dot(gains, one_hot(first, chunk), preferred_element_type=f32)[0:1, :]
        for pair in range(chunk // LANES):
            columns = slice(pair * LANES, (pair + 1) * LANES)
            x_pair = jnp.concatenate(
                [
                    first_x[:, c * chunk + pair * LANES : c * chunk + (pair + 1) * LANES],
                    xcs[c][16:, columns],
                ],
                axis=0,
            )
            upper, lower = [], []
            for side in range(2):
                h = first + 2 * pair + side
                fade = cum_rows[h : h + 1, :]
                size = step_rows[h : h + 1, :]
                col = cums[:, h : h + 1]
                top = (
                    inner[:half, :half]
                    * (jnp.exp(jnp.minimum(col[:half] - fade[:, :half], 0.0)) * size[:, :half])
                ).astype(bf16)
                low = (
                    inner[half:, :] * (jnp.exp(jnp.minimum(col[half:] - fade, 0.0)) * size)
                ).astype(bf16)
                upper.append(jnp.dot(top, x_pair[:half, :], preferred_element_type=f32))
                lower.append(jnp.dot(low, x_pair, preferred_element_type=f32))
            gain = spread[:, columns]
            outs[c][:half, columns] = jnp.where(even, upper[0], upper[1]) + gain * x_pair[
                :half, :
            ].astype(f32)
            outs[c][half:, columns] = jnp.where(even, lower[0], lower[1]) + gain * x_pair[
                half:, :
            ].astype(f32)


def finish_body(share, first, state, bcc, keep, local, *rest):
    outs, total = rest[:-1], rest[-1]
    me = lax.rem(lax.axis_index("ctx"), share)
    chunk = local.shape[1]
    rows = outs[0].shape[-2]
    carried = jnp.dot(bcc[:, LANES:], state[...], preferred_element_type=f32)
    factors = jnp.dot(three_parts(keep[...]), one_hot(first, chunk), preferred_element_type=f32)
    total[...] = local[...] + carried * factors
    if len(outs) == 1:
        for i in range(share):
            outs[0][i] = total[rows * i : rows * (i + 1), :].astype(bf16)
        return
    for m in range(share):
        at = pl.multiple_of(rows * (me ^ m), rows)
        outs[m][...] = total[pl.ds(at, rows), :].astype(bf16)


def norm_body(share, *refs):
    z, gain, handed, out, handoff, buffer, sems = refs[-7:]
    me = lax.rem(lax.axis_index("ctx"), share)
    chunk = refs[0].shape[-1]
    parts, at = [], 0
    for whole in WHOLE:
        if whole:
            parts.append([lambda m, r=refs[at]: r[me ^ m]])
            at += 1
        else:
            parts.append([lambda m, r=refs[at : at + share]: r[m][...]])
            at += share
    piece = 2 * chunk
    copies = [pltpu.make_async_copy(handed, handoff, sems.at[share])]
    copies[0].start()
    for m in (0, 2, 3, 1):
        base = pl.multiple_of((me ^ m) * piece, LANES)
        gated = []
        for c, (source,) in enumerate(parts):
            gate = z[:, pl.ds(pl.multiple_of(base + c * chunk, LANES), chunk)].astype(f32)
            gated.append(source(m).astype(f32) * (gate * jax.nn.sigmoid(gate)))
        square = sum(jnp.sum(v * v, axis=1, keepdims=True) for v in gated)
        factor = lax.rsqrt(square / piece + norm_eps)
        for c, value in enumerate(gated):
            at = pl.ds(pl.multiple_of(base + c * chunk, LANES), chunk)
            buffer[m, :, c * chunk : (c + 1) * chunk] = (value * factor * gain[:, at]).astype(bf16)
        copies.append(
            pltpu.make_async_copy(buffer.at[m], out.at[:, pl.ds(base, piece)], sems.at[m])
        )
        copies[-1].start()
    for copy in copies:
        copy.wait()


def attention_body(q_ref, mine, other, out):
    rows = q_ref.shape[0]
    keys = 6 * rows
    ratio = AH // KVH
    heads_wide = KVH * HD
    here = lax.axis_index("ctx")
    odd = lax.rem(here, 2) == 1
    starts = (0, rows + 16, 2 * rows + 48)

    def id_rows(buffer):
        total = None
        for at in starts:
            row = buffer[at + rows : at + rows + 16, :].astype(f32)[15:16, :keys]
            total = row if total is None else total + row
        return total

    lane_row = iota((1, keys), 1)
    id_row = jnp.where(lane_row < 3 * rows, id_rows(mine), id_rows(other))
    own = mine[rows : rows + 16, :].astype(f32)[15:16, :rows]
    square = iota((rows, rows), 0) == iota((rows, rows), 1)
    column = jnp.sum(
        jnp.where(square, jnp.broadcast_to(own, (rows, rows)), 0.0), axis=1, keepdims=True
    )
    lane = iota((rows, keys), 1)
    earlier = (lane >= rows) | (lane <= iota((rows, keys), 0))
    sibling = (lane < 3 * rows) | (lane >= 4 * rows) | odd
    slot = lane % (3 * rows) // rows
    before = (slot == 0) | ((slot == 1) & (here >= 2)) | ((slot == 2) & (here >= 4))
    bias = jnp.where((id_row == column) & earlier & sibling & before, 0.0, -1e30)
    pairs = ratio // 2
    bias = jnp.concatenate([bias] * pairs, axis=0)
    even = iota((keys, LANES), 1) < HD
    even_out = iota((rows * pairs, LANES), 1) < HD

    def both(at, side):
        whole = jnp.concatenate(
            [b[s : s + rows, at : at + LANES] for b in (mine, other) for s in starts], axis=0
        ).astype(f32)
        kept = jnp.where(even == (side == 0), whole, 0.0)
        moved = pltpu.roll(kept, HD, 1)
        first, second = (kept, moved) if side == 0 else (moved, kept)
        return jnp.concatenate([first.astype(bf16), second.astype(bf16)], axis=0)

    for g in range(KVH):
        block = (g // 2) * LANES
        key_pair = both(block, g % 2)
        value_pair = both(heads_wide + block, g % 2)
        base = g * ratio * HD
        q = jnp.concatenate(
            [q_ref[:, base + i * LANES : base + (i + 1) * LANES] for i in range(pairs)], axis=0
        )
        scores = lax.dot_general(
            q, key_pair, (((1,), (1,)), ((), ())), preferred_element_type=f32
        ) * (1.0 / math.sqrt(HD))
        probs, totals = [], []
        for side in range(2):
            masked = scores[:, side * keys : (side + 1) * keys] + bias
            top = jnp.max(masked, axis=1, keepdims=True)
            weight = jnp.exp(masked - top)
            totals.append(jnp.sum(weight, axis=1, keepdims=True))
            probs.append(weight.astype(bf16))
        mixed = jnp.dot(
            jnp.concatenate(probs, axis=1), value_pair, preferred_element_type=f32
        ) / jnp.where(even_out, totals[0], totals[1])
        for i in range(pairs):
            out[:, base + i * LANES : base + (i + 1) * LANES] = mixed[
                i * rows : (i + 1) * rows, :
            ].astype(bf16)


def gathered_attention(query, keys, values, own_ids):
    tokens_here = query.shape[0]
    place = lax.axis_index("ctx")
    all_ids = lax.all_gather(own_ids, "ctx", axis=0, tiled=True)
    ratio = AH // KVH
    queries = query.reshape(tokens_here, KVH, ratio, HD)
    query_pos = place * tokens_here + jnp.arange(tokens_here)
    key_piece = lax.all_gather(keys, "ctx", axis=0, tiled=True)
    value_piece = lax.all_gather(values, "ctx", axis=0, tiled=True)
    count = key_piece.shape[0]
    width = math.gcd(count, 512)
    key_blocks = key_piece.reshape(count // width, width, KVH, HD)
    value_blocks = value_piece.reshape(count // width, width, KVH, HD)
    shape = (KVH, ratio, tokens_here)

    def visit(running, item):
        key_block, value_block, order = item
        first = order * width
        key_ids = lax.dynamic_slice_in_dim(all_ids, first, width)
        key_pos = first + jnp.arange(width)
        allowed = (query_pos[:, None] >= key_pos[None, :]) & (own_ids[:, None] == key_ids[None, :])
        largest, totals, accum = running
        logits = jnp.einsum(
            "tgrd,mgd->grtm", queries, key_block, preferred_element_type=f32
        ) / math.sqrt(HD)
        masked = jnp.where(allowed, logits, -1e30)
        newest = jnp.maximum(largest, jnp.max(masked, axis=-1))
        weight = jnp.where(allowed, jnp.exp(masked - newest[..., None]), 0.0)
        correct = jnp.exp(largest - newest)
        totals = totals * correct + jnp.sum(weight, axis=-1)
        accum = accum * correct[..., None] + jnp.einsum(
            "grtm,mgd->grtd", weight.astype(bf16), value_block, preferred_element_type=f32
        )
        return (newest, totals, accum), None

    start = (jnp.full(shape, -1e30, f32), jnp.zeros(shape, f32), jnp.zeros(shape + (HD,), f32))
    (_, totals, accum), _ = lax.scan(
        visit, start, (key_blocks, value_blocks, jnp.arange(count // width, dtype=jnp.int32))
    )
    attended = accum / totals[..., None]
    return jnp.transpose(attended, (2, 0, 1, 3)).reshape(tokens_here, AH * HD).astype(bf16)


def on_device(
    x_in,
    z_in,
    bc_in,
    dt_raw,
    a_log,
    dt_bias,
    d_skip,
    conv_x,
    conv_bc,
    norm_gain,
    seg_ids,
    query,
    keys,
    values,
):
    ranks = lax.axis_size("ctx")
    rows, width = x_in.shape[1:]
    share = BLK // rows
    blocks = ranks // share
    piece = width // share
    chunk = piece // CHUNKS
    reach = -(-(rows * ranks // 2 - 1) // rows)
    shape = jax.ShapeDtypeStruct
    state_type = bf16 if blocks <= 2 else f32

    wide = 4 * LANES
    packed = call(
        functools.partial(pack_body, share),
        [shape((rows, chunk + 3 * LANES), bf16)] * share
        + [shape((rows, chunk), bf16)] * share
        + [shape((rows + 16, wide), bf16)]
        + [shape((rows + 32, wide), bf16)] * 2,
        scratch=[
            pltpu.VMEM((rows, bc_in.shape[2]), bf16),
            pltpu.VMEM((rows, LANES), bf16),
            pltpu.SemaphoreType.DMA((2 * share + 9,)),
            pltpu.VMEM((16, width), bf16),
        ],
        in_specs=[hbm()] * 3 + [vmem()] + [hbm()] * 2,
        room=PACK_ROOM,
        bytes_accessed=5 * 2**20,
    )(x_in[0], bc_in[0], dt_raw[0], seg_ids, keys[0], values[0])
    send, send_b, (kv_own, kv_near, kv_far) = (
        packed[:share],
        packed[share : 2 * share],
        packed[2 * share :],
    )
    order = [2, 3, 1]

    def exchanged(values):
        here = {0: values[0]}
        for m in order:
            here[m] = crossed(values[m], "ctx", m)
        return [here[m] for m in range(share)]

    pieces = exchanged(send)
    near, far = turned_on(kv_near, "ctx", 2), turned_on(kv_far, "ctx", 4)
    pieces_b = exchanged(send_b)
    halo = []
    if blocks > 2:
        mine = jnp.concatenate([kv_own, near, far], axis=0)
        other = crossed(mine, "ctx", 1)
        halo = [mine, other]
    per_token = shape((BLK, LANES), f32)
    xc_a, bcc_first, state_a, ids_col, cum, step, writes = call(
        functools.partial(first_body, share, blocks > 2),
        [
            shape((BLK, chunk), bf16),
            shape((BLK, 2 * LANES), bf16),
            shape((LANES, chunk), state_type),
            shape((BLK + 8, LANES), f32),
            per_token,
            per_token,
            shape((BLK, LANES), bf16),
        ],
        scratch=[
            pltpu.VMEM((BLK + 8, chunk), f32),
            pltpu.VMEM((BLK + 8, wide), f32),
            pltpu.VMEM((3, BLK, LANES), f32),
        ],
        flops=2**28,
        bytes_accessed=3 * 2**20,
    )(*pieces, conv_x[0], conv_bc[0], dt_bias, a_log, *halo)
    if blocks <= 2:
        near, far, cum = lax.optimization_barrier((near, far, cum))
        mine = jnp.concatenate([kv_own, near, far], axis=0)
        other = crossed(mine, "ctx", 1)
    xc_b, state_b = call(
        functools.partial(second_body, share, blocks > 2),
        [shape((BLK, chunk), bf16), shape((LANES, chunk), state_type)],
        scratch=[pltpu.VMEM((BLK + 8, chunk), f32), pltpu.VMEM((3, BLK, LANES), f32)],
        flops=2**28,
        bytes_accessed=3 * 2**20,
    )(*pieces_b, conv_x[0], bcc_first, ids_col, writes, *halo)
    per_head = chunk // HD

    def entering(state, first):
        if blocks > 2:
            same = ids_col[BLK + 7, :] == ids_col[7, :]
            fade = jnp.where(same, jnp.exp(cum[BLK - 1, :]), 0.0)[first : first + per_head]
            fade = jnp.repeat(fade, HD)[None, :]
            far = 1
            while far < blocks:
                came = shifted(state, "ctx", far * share)
                came_fade = shifted(fade, "ctx", far * share)
                state = state + fade * came
                fade = fade * came_fade
                far *= 2
        return turned_on(state, "ctx", share).astype(bf16)

    entry_a = entering(state_a, 0)
    entry_b = entering(state_b, per_head)

    local_a, local_b, bcc, keep = call(
        functools.partial(mixing_body, share),
        [shape((BLK, chunk), f32)] * CHUNKS + [shape((BLK, 2 * LANES), bf16), per_token],
        scratch=[
            pltpu.VMEM((24, piece + wide), f32),
            pltpu.VMEM((24, LANES), f32),
            pltpu.VMEM((3, 16, LANES), f32),
            pltpu.VMEM((16, piece), bf16),
        ],
        flops=2**31,
        bytes_accessed=4 * 2**20,
    )(*pieces, *pieces_b, xc_a, xc_b, mine, other, conv_x[0], conv_bc[0], bcc_first, cum, step, d_skip)

    if reach <= share:
        attended = call(
            attention_body,
            shape((rows, AH * HD), bf16),
            flops=2**30,
            bytes_accessed=2**20,
        )(query[0], mine, other)
    else:
        attended = gathered_attention(query[0], keys[0], values[0], seg_ids[0])
    local_a, attended = lax.optimization_barrier((local_a, attended))
    handoff = turned_on(attended, "pipe", 1)

    sent = []
    for c, (entry, local) in enumerate(((entry_a, local_a), (entry_b, local_b))):
        y = call(
            functools.partial(finish_body, share, c * per_head),
            [shape((share, rows, chunk), bf16)] if WHOLE[c] else [shape((rows, chunk), bf16)] * share,
            scratch=[pltpu.VMEM((BLK, chunk), f32)],
            flops=2**28,
            bytes_accessed=2 * 2**20,
        )(entry, bcc, keep, local)
        if WHOLE[c]:
            groups = [[b * share + i for i in range(share)] for b in range(blocks)]
            sent.append(
                lax.all_to_all(y[0], "ctx", 0, 0, tiled=True, axis_index_groups=groups)
            )
            continue
        sent += exchanged(y)
    mamba_out, handoff = call(
        functools.partial(norm_body, share),
        [shape((rows, width), bf16), shape((rows, AH * HD), bf16)],
        scratch=[pltpu.VMEM((share, rows, piece), bf16), pltpu.SemaphoreType.DMA((share + 1,))],
        out_specs=[hbm()] * 2,
        bytes_accessed=3 * 2**20,
    )(*sent, z_in[0], norm_gain, handoff)
    return (mamba_out[None], handoff[None])


def solution(mesh):
    in_specs = (
        P("pipe", "ctx", None),
        P("pipe", "ctx", None),
        P("pipe", "ctx", None),
        P("pipe", "ctx", None),
        P("pipe", None),
        P("pipe", None),
        P("pipe", None),
        P("pipe", None, None),
        P("pipe", None, None),
        P("pipe", None),
        P("pipe", "ctx"),
        P("pipe", "ctx", None),
        P("pipe", "ctx", None),
        P("pipe", "ctx", None),
    )
    out_specs = (P("pipe", "ctx", None), P("pipe", "ctx", None))
    return jax.shard_map(
        on_device, mesh=mesh, in_specs=in_specs, out_specs=out_specs, check_vma=False
    )
```

time: 75.8 us -> 64.7 us (0.85)
  the two profiles are of different devices: /device:TPU:29 before, /device:TPU:0 now
where the time goes in v2:
time: 64.7 us; the launch traced here: 64.5 us
  waiting for transfers between devices  29.2 us (45%)
  starting transfers between devices  17 us (26%)
  Pallas kernels  15 us (23%)
  local copies, waits for them, and re-layouts  2.52 us (4%)
  between operations  0.84 us (1%)
    ppermute x13, waiting for transfers between devices, crossed(): return lax.ppermute(value, axis, [(i, i ^ mask) for i in range(count)])  24.8 us
    ppermute x5, starting transfers between devices, turned_on(): lax.ppermute(value, axis, [(i, (i + steps) % count) for i in range(count)])  8.55 us
    ppermute x13, starting transfers between devices, crossed(): return lax.ppermute(value, axis, [(i, i ^ mask) for i in range(count)])  8.43 us
    ppermute x5, waiting for transfers between devices, turned_on(): lax.ppermute(value, axis, [(i, (i + steps) % count) for i in range(count)])  4.36 us
    pallas_call x1, Pallas kernels, on_device(): call(functools.partial(pack_body, share), [shape((rows, chunk + 3 * LANES...  3.43 us
    pallas_call x1, Pallas kernels, on_device(): call(functools.partial(mixing_body, share), [shape((BLK, chunk), f32)] *...  2.59 us
    unnamed x28, local copies, waits for them, and re-layouts  2.51 us
    pallas_call x1, Pallas kernels, on_device(): call(functools.partial(first_body, share, blocks > 2), [shape((BLK, chunk...  2.32 us
  transfers between devices with their start and end apart: 18, of which 9 were waited for; matrix products, arithmetic and copies ran while one was open for 1% of the time, Pallas kernels for 15%

profile of v2, /device:TPU:0, one launch (start us, length us, event | category | flops | bytes accessed | tf_op | source)
XLA Modules:
  0.0 64.5 jit_solution(1378034835593275910)
XLA Ops:
  0.7 3.4 %shard_map.149 = (bf16[64,1408]{1,0:T(8,128)(2,1)}, bf16[64,1408]{1,0:T(8,128)(2,1)}, bf16[64,1408]{1,0:T(8,128)(2,1)}, bf16[64,1408]{1,0:T(8,128)(2,1)}, bf16[6...) custom-call(bf16[64,8192]{1,0:T(8,128)(2,1)} %bitcast.18, ...), custom_call_target="tpu_custom_call" | custom-call | bytes 5242880 | tf_op jit(solution)/shard_map/pallas_call | solution.py:610
  4.1 0.5 collective-permute-start
  4.6 2.6 %collective-permute-start.1 = (bf16[64,1408]{1,0:T(8,128)(2,1)}, bf16[64,1408]{1,0:T(8,128)(2,1)S(1)}, u32[]{:S(2)}, u32[]{:S(2)}) collective-permute-start(bf16[64,1408]{1,0:T(8,128)(2,1)} %get-tuple-element.43), channel_id=1, source_target_pairs={{0,2},{1,3},{2,0},{3,1},{4,6},{5,7},{6,4},{7,5},{8,10},{9,11},{10,... | collective-permute-start | bytes 540680 | tf_op jit(solution)/shard_map/ppermute | solution.py:39
  7.3 1.7 %collective-permute-start.7 = (bf16[96,512]{1,0:T(8,128)(2,1)}, bf16[96,512]{1,0:T(8,128)(2,1)S(1)}, u32[]{:S(2)}, u32[]{:S(2)}) collective-permute-start(bf16[96,512]{1,0:T(8,128)(2,1)} %get-tuple-element.56), channel_id=1, source_target_pairs={{0,2},{1,3},{2,4},{3,5},{4,6},{5,7},{6,0},{7,1},{8,10},{9,11},{10,... | collective-permute-start | bytes 294920 | tf_op jit(solution)/shard_map/ppermute | solution.py:34
  9.1 2.6 %collective-permute-start.8 = (bf16[96,512]{1,0:T(8,128)(2,1)}, bf16[96,512]{1,0:T(8,128)(2,1)S(1)}, u32[]{:S(2)}, u32[]{:S(2)}) collective-permute-start(bf16[96,512]{1,0:T(8,128)(2,1)} %get-tuple-element.57), channel_id=1, source_target_pairs={{0,4},{1,5},{2,6},{3,7},{4,0},{5,1},{6,2},{7,3},{8,12},{9,13},{10,... | collective-permute-start | bytes 294920 | tf_op jit(solution)/shard_map/ppermute | solution.py:34
  11.7 0.9 %constant_dynamic-update-slice_fusion.2 = bf16[272,512]{1,0:T(8,128)(2,1)S(1)} fusion(bf16[80,512]{1,0:T(8,128)(2,1)} %get-tuple-element.55), kind=kLoop, calls=%fused_computation.2 | loop fusion | bytes 163840
  12.6 0.3 collective-permute-done.1.refs_2_
  12.9 5.5 %collective-permute-done.2.refs_3_ = bf16[64,1408]{1,0:T(8,128)(2,1)S(1)} collective-permute-done((bf16[64,1408]{1,0:T(8,128)(2,1)}, bf16[64,1408]{1,0:T(8,128)(2,1)S(1)}, u32[]{:S(2)}, u32[]{:S(2)}) %collective-permute-start.2) | collective-permute-done | bytes 180256 | tf_op jit(solution)/shard_map/ppermute | solution.py:39
  18.4 0.6 copy-done.7
  19.1 2.3 %shard_map.150 = (bf16[256,1024]{1,0:T(8,128)(2,1)S(1)}, bf16[256,256]{1,0:T(8,128)(2,1)S(1)}, bf16[128,1024]{1,0:T(8,128)(2,1)S(1)}, f32[264,128]{1,0:T(8,128)S...) custom-call(bf16[64,1408]{1,0:T(8,128)(2,1)S(1)} %copy-done.3, ...), custom_call_target="tpu_custom_call" | custom-call | flops 268435456 | bytes 3145728 | tf_op jit(solution)/shard_map/pallas_call | solution.py:648
  21.5 0.4 collective-permute-start.9
  22.1 0.3 copy-done.11
  22.3 2.0 %collective-permute-start.5 = (bf16[64,1024]{1,0:T(8,128)(2,1)S(1)}, bf16[64,1024]{1,0:T(8,128)(2,1)S(1)}, u32[]{:S(2)}, u32[]{:S(2)}) collective-permute-start(bf16[64,1024]{1,0:T(8,128)(2,1)S(1)} %copy-done.11), channel_id=1, source_target_pairs={{0,2},{1,3},{2,0},{3,1},{4,6},{5,7},{6,4},{7,5},{8,10},{9,11},{10,... | collective-permute-start | bytes 393224 | tf_op jit(solution)/shard_map/ppermute | solution.py:39
  24.4 2.4 %collective-permute-start.3 = (bf16[128,1024]{1,0:T(8,128)(2,1)S(1)}, bf16[128,1024]{1,0:T(8,128)(2,1)S(1)}, u32[]{:S(2)}, u32[]{:S(2)}) collective-permute-start(bf16[128,1024]{1,0:T(8,128)(2,1)S(1)} %get-tuple-element.45), channel_id=1, source_target_pairs={{0,4},{1,5},{2,6},{3,7},{4,0},{5,1},{6,2},{7,3},{8,12},{9,13},{10,... | collective-permute-start | bytes 786440 | tf_op jit(solution)/shard_map/ppermute | solution.py:34
  26.8 6.9 %collective-permute-done.5.refs_2_.refs_6_ = bf16[64,1024]{1,0:T(8,128)(2,1)S(1)} collective-permute-done((bf16[64,1024]{1,0:T(8,128)(2,1)S(1)}, bf16[64,1024]{1,0:T(8,128)(2,1)S(1)}, u32[]{:S(2)}, u32[]{:S(2)}) %collective-permute-start.5) | collective-permute-done | bytes 131104 | tf_op jit(solution)/shard_map/ppermute | solution.py:39
  33.7 1.7 %collective-permute-done.6.refs_3_.refs_7_ = bf16[64,1024]{1,0:T(8,128)(2,1)S(1)} collective-permute-done((bf16[64,1024]{1,0:T(8,128)(2,1)S(1)}, bf16[64,1024]{1,0:T(8,128)(2,1)S(1)}, u32[]{:S(2)}, u32[]{:S(2)}) %collective-permute-start.6) | collective-permute-done | bytes 131104 | tf_op jit(solution)/shard_map/ppermute | solution.py:39
  35.4 1.7 %shard_map.151 = (bf16[256,1024]{1,0:T(8,128)(2,1)S(1)}, bf16[128,1024]{1,0:T(8,128)(2,1)S(1)}) custom-call(bf16[64,1024]{1,0:T(8,128)(2,1)S(1)} %copy-done.4, bf16[64,1024]{1,0:T(8,128)(2,1)S(1)} %collective-permute-done.4.refs_1_.refs_5_, bf16[64,1024]{1,0:T(8,128)(2,1)S(1)} %collective-permute-done.5.refs_2_.refs_6_, ...), custom_call_target="tpu_custom_call" | custom-call | flops 268435456 | bytes 3145728 | tf_op jit(solution)/shard_map/pallas_call | solution.py:671
  37.1 0.3 collective-permute-start.13
  37.4 0.7 %copy-done.9 = f32[1,128]{1,0:T(1,128)S(1)} copy-done((f32[1,128]{1,0:T(1,128)S(1)}, f32[1,128]{1,0:T(1,128)}, u32[]{:S(2)}) %copy-start.9) | copy-done | bytes 536
  38.1 2.6 %shard_map.152 = (f32[256,1024]{1,0:T(8,128)S(1)}, f32[256,1024]{1,0:T(8,128)S(1)}, bf16[256,256]{1,0:T(8,128)(2,1)S(1)}, f32[256,128]{1,0:T(8,128)S(1)}) custom-call(bf16[64,1408]{1,0:T(8,128)(2,1)S(1)} %copy-done.3, bf16[64,1408]{1,0:T(8,128)(2,1)S(1)} %collective-permute-done.refs_1_, bf16[64,1408]{1,0:T(8,128)(2,1)S(1)} %collective-permute-done.1.refs_2_, ...), custom_call_target="tpu_custom_call" | custom-call | flops 2147483648 | bytes 4194304 | tf_op jit(solution)/shard_map/pallas_call | solution.py:697
  40.7 2.1 %shard_map.153 = bf16[64,2048]{1,0:T(8,128)(2,1)S(1)} custom-call(bf16[64,2048]{1,0:T(8,128)(2,1)S(1)} %bitcast.12, bf16[272,512]{1,0:T(8,128)(2,1)S(1)} %constant_dynamic-update-slice_fusion.refs_10_.mine, bf16[272,512]{1,0:T(8,128)(2,1)S(1)} %collective-permute-done.9.refs_11_.other), custom_call_target="tpu_custom_call" | custom-call | flops 1073741824 | bytes 1048576 | tf_op jit(solution)/shard_map/pallas_call | solution.py:711
  42.8 0.5 shard_map.154
  43.3 0.6 collective-permute-start.10
  43.9 1.9 %collective-permute-start.11 = (bf16[64,1024]{1,0:T(8,128)(2,1)S(1)}, bf16[64,1024]{1,0:T(8,128)(2,1)S(1)}, u32[]{:S(2)}, u32[]{:S(2)}) collective-permute-start(bf16[64,1024]{1,0:T(8,128)(2,1)S(1)} %get-tuple-element.69), channel_id=1, source_target_pairs={{0,2},{1,3},{2,0},{3,1},{4,6},{5,7},{6,4},{7,5},{8,10},{9,11},{10,... | collective-permute-start | bytes 393224 | tf_op jit(solution)/shard_map/ppermute | solution.py:39
  45.7 1.5 %collective-permute-start.17 = (bf16[64,2048]{1,0:T(8,128)(2,1)S(1)}, bf16[64,2048]{1,0:T(8,128)(2,1)S(1)}, u32[]{:S(2)}, u32[]{:S(2)}) collective-permute-start(bf16[64,2048]{1,0:T(8,128)(2,1)S(1)} %shard_map.153), channel_id=1, source_target_pairs={{0,8},{8,16},{16,24},{24,0},{1,9},{9,17},{17,25},{25,1},{2,10},{10... | collective-permute-start | bytes 786440 | tf_op jit(solution)/shard_map/ppermute | solution.py:34
  47.3 4.3 %collective-permute-done.13.state = bf16[128,1024]{1,0:T(8,128)(2,1)S(1)} collective-permute-done((bf16[128,1024]{1,0:T(8,128)(2,1)S(1)}, bf16[128,1024]{1,0:T(8,128)(2,1)S(1)}, u32[]{:S(2)}, u32[]{:S(2)}) %collective-permute-start.13) | collective-permute-done | bytes 262176 | tf_op jit(solution)/shard_map/ppermute | solution.py:34
  51.6 0.5 shard_map.155
  52.3 2.1 %collective-permute-done.11.refs_2_ = bf16[64,1024]{1,0:T(8,128)(2,1)S(1)} collective-permute-done((bf16[64,1024]{1,0:T(8,128)(2,1)S(1)}, bf16[64,1024]{1,0:T(8,128)(2,1)S(1)}, u32[]{:S(2)}, u32[]{:S(2)}) %collective-permute-start.11) | collective-permute-done | bytes 131104 | tf_op jit(solution)/shard_map/ppermute | solution.py:39
  54.4 2.7 %collective-permute-done.12.refs_3_ = bf16[64,1024]{1,0:T(8,128)(2,1)S(1)} collective-permute-done((bf16[64,1024]{1,0:T(8,128)(2,1)S(1)}, bf16[64,1024]{1,0:T(8,128)(2,1)S(1)}, u32[]{:S(2)}, u32[]{:S(2)}) %collective-permute-start.12) | collective-permute-done | bytes 131104 | tf_op jit(solution)/shard_map/ppermute | solution.py:39
  57.1 2.9 %collective-permute-done.15.refs_6_ = bf16[64,1024]{1,0:T(8,128)(2,1)S(1)} collective-permute-done((bf16[64,1024]{1,0:T(8,128)(2,1)S(1)}, bf16[64,1024]{1,0:T(8,128)(2,1)S(1)}, u32[]{:S(2)}, u32[]{:S(2)}) %collective-permute-start.15) | collective-permute-done | bytes 131104 | tf_op jit(solution)/shard_map/ppermute | solution.py:39
  60.0 2.7 %collective-permute-done.16.refs_7_ = bf16[64,1024]{1,0:T(8,128)(2,1)S(1)} collective-permute-done((bf16[64,1024]{1,0:T(8,128)(2,1)S(1)}, bf16[64,1024]{1,0:T(8,128)(2,1)S(1)}, u32[]{:S(2)}, u32[]{:S(2)}) %collective-permute-start.16) | collective-permute-done | bytes 131104 | tf_op jit(solution)/shard_map/ppermute | solution.py:39
  62.7 1.8 %shard_map.156 = (bf16[64,8192]{1,0:T(8,128)(2,1)}, bf16[64,2048]{1,0:T(8,128)(2,1)}) custom-call(bf16[64,1024]{1,0:T(8,128)(2,1)S(1)} %get-tuple-element.67.refs_0_, bf16[64,1024]{1,0:T(8,128)(2,1)S(1)} %collective-permute-done.10.refs_1_, bf16[64,1024]{1,0:T(8,128)(2,1)S(1)} %collective-permute-done.11.refs_2_, ...), custom_call_target="tpu_custom_call" | custom-call | bytes 3145728 | tf_op jit(solution)/shard_map/pallas_call | solution.py:738
  (41 shorter events, 0.5 us)
Async XLA Ops:
  0.6 17.8 %copy-start.5 = (bf16[1,4,8192]{2,1,0:T(4,128)(2,1)S(1)}, bf16[1,4,8192]{2,1,0:T(4,128)(2,1)}, u32[]{:S(2)}) copy-start(bf16[1,4,8192]{2,1,0:T(4,128)(2,1)} %param.21) | copy-start | bytes 196612
  0.6 17.8 %copy-start.6 = (bf16[1,4,1024]{2,1,0:T(4,128)(2,1)S(1)}, bf16[1,4,1024]{2,1,0:T(4,128)(2,1)}, u32[]{:S(2)}) copy-start(bf16[1,4,1024]{2,1,0:T(4,128)(2,1)} %param.22) | copy-start | bytes 24580
  4.1 14.3 %copy-start.3 = (bf16[64,1408]{1,0:T(8,128)(2,1)S(1)}, bf16[64,1408]{1,0:T(8,128)(2,1)}, u32[]{:S(2)}) copy-start(bf16[64,1408]{1,0:T(8,128)(2,1)} %get-tuple-element.41.refs_0_) | copy-start | bytes 540676
  4.1 8.5 %collective-permute-start = (bf16[64,1408]{1,0:T(8,128)(2,1)}, bf16[64,1408]{1,0:T(8,128)(2,1)S(1)}, u32[]{:S(2)}, u32[]{:S(2)}) collective-permute-start(bf16[64,1408]{1,0:T(8,128)(2,1)} %get-tuple-element.42), channel_id=1, source_target_pairs={{0,1},{1,0},{2,3},{3,2},{4,5},{5,4},{6,7},{7,6},{8,9},{9,8},{10,11... | collective-permute-start | bytes 540680 | tf_op jit(solution)/shard_map/ppermute | solution.py:39
  4.6 8.3 %collective-permute-start.1 = (bf16[64,1408]{1,0:T(8,128)(2,1)}, bf16[64,1408]{1,0:T(8,128)(2,1)S(1)}, u32[]{:S(2)}, u32[]{:S(2)}) collective-permute-start(bf16[64,1408]{1,0:T(8,128)(2,1)} %get-tuple-element.43), channel_id=1, source_target_pairs={{0,2},{1,3},{2,0},{3,1},{4,6},{5,7},{6,4},{7,5},{8,10},{9,11},{10,... | collective-permute-start | bytes 540680 | tf_op jit(solution)/shard_map/ppermute | solution.py:39
  7.3 11.1 %collective-permute-start.2 = (bf16[64,1408]{1,0:T(8,128)(2,1)}, bf16[64,1408]{1,0:T(8,128)(2,1)S(1)}, u32[]{:S(2)}, u32[]{:S(2)}) collective-permute-start(bf16[64,1408]{1,0:T(8,128)(2,1)} %get-tuple-element.44), channel_id=1, source_target_pairs={{0,3},{1,2},{2,1},{3,0},{4,7},{5,6},{6,5},{7,4},{8,11},{9,10},{10,... | collective-permute-start | bytes 540680 | tf_op jit(solution)/shard_map/ppermute | solution.py:39
  7.3 14.1 %collective-permute-start.7 = (bf16[96,512]{1,0:T(8,128)(2,1)}, bf16[96,512]{1,0:T(8,128)(2,1)S(1)}, u32[]{:S(2)}, u32[]{:S(2)}) collective-permute-start(bf16[96,512]{1,0:T(8,128)(2,1)} %get-tuple-element.56), channel_id=1, source_target_pairs={{0,2},{1,3},{2,4},{3,5},{4,6},{5,7},{6,0},{7,1},{8,10},{9,11},{10,... | collective-permute-start | bytes 294920 | tf_op jit(solution)/shard_map/ppermute | solution.py:34
  9.1 12.4 %collective-permute-start.8 = (bf16[96,512]{1,0:T(8,128)(2,1)}, bf16[96,512]{1,0:T(8,128)(2,1)S(1)}, u32[]{:S(2)}, u32[]{:S(2)}) collective-permute-start(bf16[96,512]{1,0:T(8,128)(2,1)} %get-tuple-element.57), channel_id=1, source_target_pairs={{0,4},{1,5},{2,6},{3,7},{4,0},{5,1},{6,2},{7,3},{8,12},{9,13},{10,... | collective-permute-start | bytes 294920 | tf_op jit(solution)/shard_map/ppermute | solution.py:34
  18.4 0.7 %copy-start.7 = (f32[1,128]{1,0:T(1,128)S(1)}, f32[1,128]{1,0:T(1,128)}, u32[]{:S(2)}) copy-start(f32[1,128]{1,0:T(1,128)} %refs_6_.1) | copy-start | bytes 1540
  18.4 0.7 %copy-start.8 = (f32[1,128]{1,0:T(1,128)S(1)}, f32[1,128]{1,0:T(1,128)}, u32[]{:S(2)}) copy-start(f32[1,128]{1,0:T(1,128)} %refs_7_.1) | copy-start | bytes 1540
  19.1 2.8 %copy-start.12 = (bf16[64,1024]{1,0:T(8,128)(2,1)S(1)}, bf16[64,1024]{1,0:T(8,128)(2,1)}, u32[]{:S(2)}) copy-start(bf16[64,1024]{1,0:T(8,128)(2,1)} %get-tuple-element.47) | copy-start | bytes 393220
  21.4 0.9 %copy-start.11 = (bf16[64,1024]{1,0:T(8,128)(2,1)S(1)}, bf16[64,1024]{1,0:T(8,128)(2,1)}, u32[]{:S(2)}) copy-start(bf16[64,1024]{1,0:T(8,128)(2,1)} %get-tuple-element.48) | copy-start | bytes 393220
  21.4 2.9 %copy-start.10 = (bf16[64,1024]{1,0:T(8,128)(2,1)S(1)}, bf16[64,1024]{1,0:T(8,128)(2,1)}, u32[]{:S(2)}) copy-start(bf16[64,1024]{1,0:T(8,128)(2,1)} %get-tuple-element.49) | copy-start | bytes 393220
  21.5 13.9 %copy-start.4 = (bf16[64,1024]{1,0:T(8,128)(2,1)S(1)}, bf16[64,1024]{1,0:T(8,128)(2,1)}, u32[]{:S(2)}) copy-start(bf16[64,1024]{1,0:T(8,128)(2,1)} %get-tuple-element.46.refs_0_.refs_4_) | copy-start | bytes 393220
  21.5 15.9 %collective-permute-start.9 = (bf16[272,512]{1,0:T(8,128)(2,1)S(1)}, bf16[272,512]{1,0:T(8,128)(2,1)S(1)}, u32[]{:S(2)}, u32[]{:S(2)}) collective-permute-start(bf16[272,512]{1,0:T(8,128)(2,1)S(1)} %constant_dynamic-update-slice_fusion.refs_10_.mine), channel_id=1, source_target_pairs={{0,1},{1,0},{2,3},{3,2},{4,5},{5,4},{6,7},{7,6},{8,9},{9,8},{10,11... | collective-permute-start | bytes 835592 | tf_op jit(solution)/shard_map/ppermute | solution.py:39
  21.9 4.9 %collective-permute-start.4 = (bf16[64,1024]{1,0:T(8,128)(2,1)S(1)}, bf16[64,1024]{1,0:T(8,128)(2,1)S(1)}, u32[]{:S(2)}, u32[]{:S(2)}) collective-permute-start(bf16[64,1024]{1,0:T(8,128)(2,1)S(1)} %copy-done.12), channel_id=1, source_target_pairs={{0,1},{1,0},{2,3},{3,2},{4,5},{5,4},{6,7},{7,6},{8,9},{9,8},{10,11... | collective-permute-start | bytes 393224 | tf_op jit(solution)/shard_map/ppermute | solution.py:39
  22.3 11.4 %collective-permute-start.5 = (bf16[64,1024]{1,0:T(8,128)(2,1)S(1)}, bf16[64,1024]{1,0:T(8,128)(2,1)S(1)}, u32[]{:S(2)}, u32[]{:S(2)}) collective-permute-start(bf16[64,1024]{1,0:T(8,128)(2,1)S(1)} %copy-done.11), channel_id=1, source_target_pairs={{0,2},{1,3},{2,0},{3,1},{4,6},{5,7},{6,4},{7,5},{8,10},{9,11},{10,... | collective-permute-start | bytes 393224 | tf_op jit(solution)/shard_map/ppermute | solution.py:39
  24.4 11.0 %collective-permute-start.6 = (bf16[64,1024]{1,0:T(8,128)(2,1)S(1)}, bf16[64,1024]{1,0:T(8,128)(2,1)S(1)}, u32[]{:S(2)}, u32[]{:S(2)}) collective-permute-start(bf16[64,1024]{1,0:T(8,128)(2,1)S(1)} %copy-done.10), channel_id=1, source_target_pairs={{0,3},{1,2},{2,1},{3,0},{4,7},{5,6},{6,5},{7,4},{8,11},{9,10},{10,... | collective-permute-start | bytes 393224 | tf_op jit(solution)/shard_map/ppermute | solution.py:39
  24.4 18.4 %collective-permute-start.3 = (bf16[128,1024]{1,0:T(8,128)(2,1)S(1)}, bf16[128,1024]{1,0:T(8,128)(2,1)S(1)}, u32[]{:S(2)}, u32[]{:S(2)}) collective-permute-start(bf16[128,1024]{1,0:T(8,128)(2,1)S(1)} %get-tuple-element.45), channel_id=1, source_target_pairs={{0,4},{1,5},{2,6},{3,7},{4,0},{5,1},{6,2},{7,3},{8,12},{9,13},{10,... | collective-permute-start | bytes 786440 | tf_op jit(solution)/shard_map/ppermute | solution.py:34
  37.1 14.5 %collective-permute-start.13 = (bf16[128,1024]{1,0:T(8,128)(2,1)S(1)}, bf16[128,1024]{1,0:T(8,128)(2,1)S(1)}, u32[]{:S(2)}, u32[]{:S(2)}) collective-permute-start(bf16[128,1024]{1,0:T(8,128)(2,1)S(1)} %get-tuple-element.71), channel_id=1, source_target_pairs={{0,4},{1,5},{2,6},{3,7},{4,0},{5,1},{6,2},{7,3},{8,12},{9,13},{10,... | collective-permute-start | bytes 786440 | tf_op jit(solution)/shard_map/ppermute | solution.py:34
  37.4 0.7 %copy-start.9 = (f32[1,128]{1,0:T(1,128)S(1)}, f32[1,128]{1,0:T(1,128)}, u32[]{:S(2)}) copy-start(f32[1,128]{1,0:T(1,128)} %refs_17_.1) | copy-start | bytes 1540
  38.1 2.6 %copy-start.2 = (bf16[1,64,2048]{2,1,0:T(8,128)(2,1)S(1)}, bf16[1,64,2048]{2,1,0:T(8,128)(2,1)}, u32[]{:S(2)}) copy-start(bf16[1,64,2048]{2,1,0:T(8,128)(2,1)} %param.25) | copy-start | bytes 786436
  43.3 19.4 %copy-start = (bf16[1,64,8192]{2,1,0:T(8,128)(2,1)S(1)}, bf16[1,64,8192]{2,1,0:T(8,128)(2,1)}, u32[]{:S(2)}) copy-start(bf16[1,64,8192]{2,1,0:T(8,128)(2,1)} %param.15) | copy-start | bytes 3145732
  43.3 8.9 %collective-permute-start.10 = (bf16[64,1024]{1,0:T(8,128)(2,1)S(1)}, bf16[64,1024]{1,0:T(8,128)(2,1)S(1)}, u32[]{:S(2)}, u32[]{:S(2)}) collective-permute-start(bf16[64,1024]{1,0:T(8,128)(2,1)S(1)} %get-tuple-element.68), channel_id=1, source_target_pairs={{0,1},{1,0},{2,3},{3,2},{4,5},{5,4},{6,7},{7,6},{8,9},{9,8},{10,11... | collective-permute-start | bytes 393224 | tf_op jit(solution)/shard_map/ppermute | solution.py:39
  43.9 10.5 %collective-permute-start.11 = (bf16[64,1024]{1,0:T(8,128)(2,1)S(1)}, bf16[64,1024]{1,0:T(8,128)(2,1)S(1)}, u32[]{:S(2)}, u32[]{:S(2)}) collective-permute-start(bf16[64,1024]{1,0:T(8,128)(2,1)S(1)} %get-tuple-element.69), channel_id=1, source_target_pairs={{0,2},{1,3},{2,0},{3,1},{4,6},{5,7},{6,4},{7,5},{8,10},{9,11},{10,... | collective-permute-start | bytes 393224 | tf_op jit(solution)/shard_map/ppermute | solution.py:39
  45.7 17.0 %collective-permute-start.17 = (bf16[64,2048]{1,0:T(8,128)(2,1)S(1)}, bf16[64,2048]{1,0:T(8,128)(2,1)S(1)}, u32[]{:S(2)}, u32[]{:S(2)}) collective-permute-start(bf16[64,2048]{1,0:T(8,128)(2,1)S(1)} %shard_map.153), channel_id=1, source_target_pairs={{0,8},{8,16},{16,24},{24,0},{1,9},{9,17},{17,25},{25,1},{2,10},{10... | collective-permute-start | bytes 786440 | tf_op jit(solution)/shard_map/ppermute | solution.py:34
  47.3 9.8 %collective-permute-start.12 = (bf16[64,1024]{1,0:T(8,128)(2,1)S(1)}, bf16[64,1024]{1,0:T(8,128)(2,1)S(1)}, u32[]{:S(2)}, u32[]{:S(2)}) collective-permute-start(bf16[64,1024]{1,0:T(8,128)(2,1)S(1)} %get-tuple-element.70), channel_id=1, source_target_pairs={{0,3},{1,2},{2,1},{3,0},{4,7},{5,6},{6,5},{7,4},{8,11},{9,10},{10,... | collective-permute-start | bytes 393224 | tf_op jit(solution)/shard_map/ppermute | solution.py:39
  51.6 11.1 %copy-start.1 = (f32[1,8192]{1,0:T(1,128)S(1)}, f32[1,8192]{1,0:T(1,128)}, u32[]{:S(2)}) copy-start(f32[1,8192]{1,0:T(1,128)} %refs_9_.1) | copy-start | bytes 98308
  52.1 4.9 %collective-permute-start.14 = (bf16[64,1024]{1,0:T(8,128)(2,1)S(1)}, bf16[64,1024]{1,0:T(8,128)(2,1)S(1)}, u32[]{:S(2)}, u32[]{:S(2)}) collective-permute-start(bf16[64,1024]{1,0:T(8,128)(2,1)S(1)} %get-tuple-element.74), channel_id=1, source_target_pairs={{0,1},{1,0},{2,3},{3,2},{4,5},{5,4},{6,7},{7,6},{8,9},{9,8},{10,11... | collective-permute-start | bytes 393224 | tf_op jit(solution)/shard_map/ppermute | solution.py:39
  52.2 7.7 %collective-permute-start.15 = (bf16[64,1024]{1,0:T(8,128)(2,1)S(1)}, bf16[64,1024]{1,0:T(8,128)(2,1)S(1)}, u32[]{:S(2)}, u32[]{:S(2)}) collective-permute-start(bf16[64,1024]{1,0:T(8,128)(2,1)S(1)} %get-tuple-element.75), channel_id=1, source_target_pairs={{0,2},{1,3},{2,0},{3,1},{4,6},{5,7},{6,4},{7,5},{8,10},{9,11},{10,... | collective-permute-start | bytes 393224 | tf_op jit(solution)/shard_map/ppermute | solution.py:39
  54.4 8.3 %collective-permute-start.16 = (bf16[64,1024]{1,0:T(8,128)(2,1)S(1)}, bf16[64,1024]{1,0:T(8,128)(2,1)S(1)}, u32[]{:S(2)}, u32[]{:S(2)}) collective-permute-start(bf16[64,1024]{1,0:T(8,128)(2,1)S(1)} %get-tuple-element.76), channel_id=1, source_target_pairs={{0,3},{1,2},{2,1},{3,0},{4,7},{5,6},{6,5},{7,4},{8,11},{9,10},{10,... | collective-permute-start | bytes 393224 | tf_op jit(solution)/shard_map/ppermute | solution.py:39

commit v3 on v2

--- a/solution.py
+++ b/solution.py
@@ -65,94 +65,105 @@
 
 
 def pack_body(share, x_hbm, bc_hbm, dt_hbm, ids_ref, k_hbm, v_hbm, *refs):
-    sends, seconds = refs[:share], refs[share : 2 * share]
-    own_kv, near_kv, far_kv, bc_ref, dt_ref, sems, tails = refs[2 * share :]
+    sends, seconds = refs[:share], refs[share]
+    kvs, rest = refs[share + 1 : share + 4], refs[share + 4 :]
+    dt_ref, bc_ref, x_firsts, x_seconds, kv_ref, marks, own_extra, near_extra, far_extra = rest[:-2]
+    x_tail, sems = rest[-2:]
+    extras = (own_extra, near_extra, far_extra)
     me = lax.rem(lax.axis_index("ctx"), share)
     rows, width = x_hbm.shape
     piece = width // share
     chunk = piece // CHUNKS
     states = bc_hbm.shape[1] // (2 * G)
     wide = 4 * LANES
-    copies = [
-        pltpu.make_async_copy(bc_hbm, bc_ref, sems.at[0]),
-        pltpu.make_async_copy(dt_hbm, dt_ref, sems.at[1]),
+    started = []
+
+    def start(source, target):
+        copy = pltpu.make_async_copy(source, target, sems.at[len(started)])
+        copy.start()
+        started.append(copy)
+        return copy
+
+    order = (2, 3, 1, 0)
+    steps_in, small_in = start(dt_hbm, dt_ref), start(bc_hbm, bc_ref)
+    parts_in = []
+    for c, held in enumerate((x_firsts, x_seconds)):
+        for m in order:
+            at = pl.multiple_of((me ^ m) * piece + c * chunk, LANES)
+            if c == 0:
+                parts_in.append(start(x_hbm.at[:, pl.ds(at, chunk)], held.at[m]))
+            else:
+                at = m * piece + chunk
+                parts_in.append(start(x_hbm.at[:, pl.ds(at, chunk)], held.at[m]))
+    kv_in = [
+        start(source, kv_ref.at[:, pl.ds(side * wide // 2, wide // 2)])
+        for side, source in enumerate((k_hbm, v_hbm))
     ]
-    for m in (2, 3, 1, 0):
-        for c, target in enumerate((sends[m].at[:, pl.ds(0, chunk)], seconds[m])):
-            base = pl.multiple_of((me ^ m) * piece + c * chunk, LANES)
-            copies.append(
-                pltpu.make_async_copy(
-                    x_hbm.at[:, pl.ds(base, chunk)], target, sems.at[2 + share * c + m]
-                )
-            )
-    for i, kv in enumerate((own_kv, near_kv, far_kv)):
-        for side, source in enumerate((k_hbm, v_hbm)):
-            copies.append(
-                pltpu.make_async_copy(
-                    source,
-                    kv.at[pl.ds(0, rows), pl.ds(side * wide // 2, wide // 2)],
-                    sems.at[2 + 2 * share + 2 * i + side],
-                )
-            )
-    copies.append(
-        pltpu.make_async_copy(x_hbm.at[pl.ds(rows - 16, 16), :], tails, sems.at[2 * share + 8])
-    )
-    for copy in copies:
-        copy.start()
+    tail_in = start(x_hbm.at[pl.ds(rows - 16, 16), :], x_tail)
+    arriving = len(started)
     number = ids_ref[...].astype(f32) + 1.0
     square = iota((rows, rows), 0) == iota((rows, rows), 1)
     column = jnp.sum(
         jnp.where(square, jnp.broadcast_to(number, (rows, rows)), 0.0), axis=1, keepdims=True
     )
+    small = iota((rows, LANES), 1)
+    steps_in.wait()
+    steps = dt_ref[...].astype(f32)
+    small_in.wait()
+    for m in order:
+        s = me ^ m
+        turn = lax.rem(LANES - LOCAL_HEADS * s, LANES)
+        marked = jnp.where(small < LOCAL_HEADS, pltpu.roll(steps, turn, 1), column).astype(bf16)
+        for side in range(2):
+            at = pl.multiple_of((side * G + s) * states, LANES)
+            marks[m, :, side * states : (side + 1) * states] = bc_ref[:, pl.ds(at, states)]
+        marks[m, :, 2 * states :] = marked
+        start(marks.at[m], sends[m].at[:, pl.ds(chunk, 2 * states + LANES)])
+    for i, m in enumerate(order):
+        parts_in[i].wait()
+        start(x_firsts.at[m], sends[m].at[:, pl.ds(0, chunk)])
+    for i, m in enumerate(order):
+        parts_in[share + i].wait()
+        start(x_seconds.at[m], seconds.at[m])
+    for copy in kv_in:
+        copy.wait()
+    for kv in kvs:
+        start(kv_ref, kv.at[pl.ds(0, rows), :])
     lane = iota((rows, wide), 1)
+    at = jnp.where(lane >= 3 * rows, lane - 3 * rows, lane)
     row = iota((rows, wide), 0)
     which = iota((16, wide), 0)
-    small = iota((rows, LANES), 1)
-    copies[0].wait()
-    copies[1].wait()
-    steps = dt_ref[...].astype(f32)
-
-    def head_part(s):
-        turned = pltpu.roll(steps, lax.rem(LANES - LOCAL_HEADS * s, LANES), 1)
-        return jnp.where(small < LOCAL_HEADS, turned, column)
-
-    for m in (2, 3, 1, 0):
-        s = me ^ m
-        b_at = pl.multiple_of(s * states, LANES)
-        c_at = pl.multiple_of(G * states + s * states, LANES)
-        sends[m][:, chunk : chunk + states] = bc_ref[:, pl.ds(b_at, states)]
-        sends[m][:, chunk + states : chunk + 2 * states] = bc_ref[:, pl.ds(c_at, states)]
-        sends[m][:, chunk + 2 * states :] = head_part(s).astype(bf16)
-    for copy in copies[2:]:
-        copy.wait()
-    last = slice(rows - 16, rows)
-    for slot, kv in enumerate((own_kv, near_kv, far_kv)):
-        at = jnp.where(lane >= 3 * rows, lane - 3 * rows, lane)
+    tail_in.wait()
+    bc_tail = bc_ref[rows - 16 :, :]
+    for slot, extra in enumerate(extras):
         id_row = jnp.sum(jnp.where(at == row + rows * slot, column, 0.0), axis=0, keepdims=True)
         if slot == 0:
-            kv[rows:, :] = jnp.where(which == 15, id_row, 0.0).astype(bf16)
-            continue
-        for part in range(2):
-            s = 2 * (slot - 1) + part
-            block = jnp.where(which == 15, id_row, 0.0)
-            blocks = [
-                tails[:, s * piece + p * wide : s * piece + (p + 1) * wide].astype(f32)
-                for p in range(piece // wide)
-            ]
-            blocks.append(
-                jnp.concatenate(
-                    [
-                        bc_ref[last, s * states : (s + 1) * states].astype(f32),
-                        bc_ref[last, (G + s) * states : (G + s + 1) * states].astype(f32),
-                        jnp.broadcast_to(column[last, :], (16, 2 * LANES)),
-                    ],
-                    axis=1,
+            extra[...] = jnp.where(which == 15, id_row, 0.0).astype(bf16)
+        else:
+            for part in range(2):
+                s = 2 * (slot - 1) + part
+                block = jnp.where(which == 15, id_row, 0.0)
+                blocks = [
+                    x_tail[:, s * piece + p * wide : s * piece + (p + 1) * wide].astype(f32)
+                    for p in range(piece // wide)
+                ]
+                blocks.append(
+                    jnp.concatenate(
+                        [
+                            bc_tail[:, s * states : (s + 1) * states].astype(f32),
+                            bc_tail[:, (G + s) * states : (G + s + 1) * states].astype(f32),
+                            jnp.broadcast_to(column[rows - 16 :, :], (16, 2 * LANES)),
+                        ],
+                        axis=1,
+                    )
                 )
-            )
-            for i in range(3):
-                for p, source in enumerate(blocks):
-                    block = jnp.where(which == 5 * i + p, source[13 + i : 14 + i, :], block)
-            kv[rows + 16 * part : rows + 16 * (part + 1), :] = block.astype(bf16)
+                for i in range(3):
+                    for p, source in enumerate(blocks):
+                        block = jnp.where(which == 5 * i + p, source[13 + i : 14 + i, :], block)
+                extra[16 * part : 16 * (part + 1), :] = block.astype(bf16)
+        start(extra, kvs[slot].at[pl.ds(rows, extra.shape[0]), :])
+    for copy in started[arriving:]:
+        copy.wait()
 
 
 def pick_halo(me, rows, mine, other):
@@ -247,8 +258,8 @@
 
 def first_body(share, with_halo, *refs):
     pieces = refs[:share]
-    convx, convbc, bias, alog = refs[share : share + 4]
-    rest = refs[share + 4 :]
+    convx, convbc, gains = refs[share : share + 3]
+    rest = refs[share + 3 :]
     me = lax.rem(lax.axis_index("ctx"), share)
     if with_halo:
         picked = pick_halo(me, pieces[0].shape[0], rest[0], rest[1])
@@ -276,9 +287,9 @@
         columns = slice(half * LANES, (half + 1) * LANES)
         taps = taps_at(convbc, half * G * LANES + me * LANES)
         bcc_o[:, columns] = conv_strip(bs, columns, masks, taps)
-    raw = bs[8:, 2 * LANES : 3 * LANES] + turned(bias[...], me)[0:1, :]
+    raw = bs[8:, 2 * LANES : 3 * LANES] + turned(gains[0:1, :], me)[0:1, :]
     step = jnp.maximum(raw, 0.0) + jnp.log1p(jnp.exp(-jnp.abs(raw)))
-    total = step * (-jnp.exp(turned(alog[...], me)[0:1, :]))
+    total = step * (-jnp.exp(turned(gains[1:2, :], me)[0:1, :]))
     row = iota((length, LANES), 0)
     reach = 1
     while reach < length:
@@ -298,24 +309,23 @@
 
 
 def second_body(share, with_halo, *refs):
-    pieces = refs[:share]
-    convx, bcc, ids, writes = refs[share : share + 4]
-    rest = refs[share + 4 :]
+    pieces = refs[0]
+    convx, bcc, ids, writes = refs[1:5]
+    rest = refs[5:]
     me = lax.rem(lax.axis_index("ctx"), share)
     if with_halo:
-        picked = pick_halo(me, pieces[0].shape[0], rest[0], rest[1])
+        picked = pick_halo(me, pieces.shape[1], rest[0], rest[1])
         rest = rest[2:]
     xc_o, state_o, xs, masks = rest
     chunk = xc_o.shape[1]
-    rows = pieces[0].shape[0]
+    rows = pieces.shape[1]
     blocks = chunk // (4 * LANES)
     if with_halo:
         place_halo(xs, picked, list(range(blocks, 2 * blocks)))
     else:
         xs[0:8, :] = jnp.zeros((8, chunk), f32)
-    for m in range(share):
-        at = pl.multiple_of(8 + rows * (me ^ m), 8)
-        xs[pl.ds(at, rows), :] = pieces[m][...].astype(f32)
+    for i in range(share):
+        xs[8 + rows * i : 8 + rows * (i + 1), :] = pieces[i].astype(f32)
     set_masks(masks, ids)
     base = me * (chunk * CHUNKS) + chunk
     conv_x_and_state(
@@ -324,8 +334,8 @@
 
 
 def mixing_body(share, *refs):
-    pieces, seconds = refs[:share], refs[share : 2 * share]
-    xcs, refs = refs[2 * share : 2 * share + CHUNKS], refs[2 * share + CHUNKS :]
+    pieces, seconds = refs[:share], refs[share]
+    xcs, refs = refs[share + 1 : share + 1 + CHUNKS], refs[share + 1 + CHUNKS :]
     mine, other, convx, convbc, bcc_in, cum, step, skip = refs[:8]
     rest = refs[8:]
     outs, (bcc, keep, head, head_ids, masks, first_x) = rest[:CHUNKS], rest[CHUNKS:]
@@ -344,7 +354,7 @@
         return start
 
     head[8:, :chunk] = first_rows(pieces, slice(0, chunk))
-    head[8:, chunk:piece] = first_rows(seconds, slice(0, chunk))
+    head[8:, chunk:piece] = seconds[0, :16, :].astype(f32)
     head[8:, piece : piece + 3 * LANES] = first_rows(pieces, slice(chunk, chunk + 3 * LANES))
     where_ids = piece + 2 * LANES + LOCAL_HEADS
     head_ids[...] = jnp.broadcast_to(head[:, where_ids : where_ids + 1], (24, LANES))
@@ -378,7 +388,7 @@
     keep[...] = jnp.where(own[:, :LANES] == head_ids[7:8, :], jnp.exp(cums), 0.0)
     cum_rows = cums.T
     step_rows = step[...].T
-    gains = three_parts(turned(skip[...], me))
+    gains = three_parts(turned(skip[2:3, :], me))
     even = iota((half, LANES), 1) < HD
     for c in range(CHUNKS):
         first = c * (chunk // HD)
@@ -610,24 +620,28 @@
     packed = call(
         functools.partial(pack_body, share),
         [shape((rows, chunk + 3 * LANES), bf16)] * share
-        + [shape((rows, chunk), bf16)] * share
+        + [shape((share, rows, chunk), bf16)]
         + [shape((rows + 16, wide), bf16)]
         + [shape((rows + 32, wide), bf16)] * 2,
         scratch=[
+            pltpu.VMEM((rows, LANES), bf16),
             pltpu.VMEM((rows, bc_in.shape[2]), bf16),
-            pltpu.VMEM((rows, LANES), bf16),
-            pltpu.SemaphoreType.DMA((2 * share + 9,)),
+            pltpu.VMEM((share, rows, chunk), bf16),
+            pltpu.VMEM((share, rows, chunk), bf16),
+            pltpu.VMEM((rows, wide), bf16),
+            pltpu.VMEM((share, rows, 3 * LANES), bf16),
+            pltpu.VMEM((16, wide), bf16),
+            pltpu.VMEM((32, wide), bf16),
+            pltpu.VMEM((32, wide), bf16),
             pltpu.VMEM((16, width), bf16),
+            pltpu.SemaphoreType.DMA((5 * share + 11,)),
         ],
         in_specs=[hbm()] * 3 + [vmem()] + [hbm()] * 2,
+        out_specs=[hbm()] * (share + 4),
         room=PACK_ROOM,
         bytes_accessed=5 * 2**20,
     )(x_in[0], bc_in[0], dt_raw[0], seg_ids, keys[0], values[0])
-    send, send_b, (kv_own, kv_near, kv_far) = (
-        packed[:share],
-        packed[share : 2 * share],
-        packed[2 * share :],
-    )
+    send, send_b, (kv_own, kv_near, kv_far) = packed[:share], packed[share], packed[share + 1 :]
     order = [2, 3, 1]
 
     def exchanged(values):
@@ -638,13 +652,16 @@
 
     pieces = exchanged(send)
     near, far = turned_on(kv_near, "ctx", 2), turned_on(kv_far, "ctx", 4)
-    pieces_b = exchanged(send_b)
+    send_b, pieces[2] = lax.optimization_barrier((send_b, pieces[2]))
+    groups = [[b * share + i for i in range(share)] for b in range(blocks)]
+    pieces_b = lax.all_to_all(send_b, "ctx", 0, 0, tiled=True, axis_index_groups=groups)
     halo = []
     if blocks > 2:
         mine = jnp.concatenate([kv_own, near, far], axis=0)
         other = crossed(mine, "ctx", 1)
         halo = [mine, other]
     per_token = shape((BLK, LANES), f32)
+    head_gains = jnp.concatenate([dt_bias, a_log, d_skip], axis=0)
     xc_a, bcc_first, state_a, ids_col, cum, step, writes = call(
         functools.partial(first_body, share, blocks > 2),
         [
@@ -661,9 +678,9 @@
             pltpu.VMEM((BLK + 8, wide), f32),
             pltpu.VMEM((3, BLK, LANES), f32),
         ],
-        flops=2**28,
-        bytes_accessed=3 * 2**20,
-    )(*pieces, conv_x[0], conv_bc[0], dt_bias, a_log, *halo)
+        flops=0,
+        bytes_accessed=1024,
+    )(*pieces, conv_x[0], conv_bc[0], head_gains, *halo)
     if blocks <= 2:
         near, far, cum = lax.optimization_barrier((near, far, cum))
         mine = jnp.concatenate([kv_own, near, far], axis=0)
@@ -674,7 +691,7 @@
         scratch=[pltpu.VMEM((BLK + 8, chunk), f32), pltpu.VMEM((3, BLK, LANES), f32)],
         flops=2**28,
         bytes_accessed=3 * 2**20,
-    )(*pieces_b, conv_x[0], bcc_first, ids_col, writes, *halo)
+    )(pieces_b, conv_x[0], bcc_first, ids_col, writes, *halo)
     per_head = chunk // HD
 
     def entering(state, first):
@@ -705,7 +722,7 @@
         ],
         flops=2**31,
         bytes_accessed=4 * 2**20,
-    )(*pieces, *pieces_b, xc_a, xc_b, mine, other, conv_x[0], conv_bc[0], bcc_first, cum, step, d_skip)
+    )(*pieces, pieces_b, xc_a, xc_b, mine, other, conv_x[0], conv_bc[0], bcc_first, cum, step, head_gains)
 
     if reach <= share:
         attended = call(

time: 64.7 us -> 62.5 us (0.966)
  waiting for transfers between devices: 29.2 us -> 22 us
  starting transfers between devices: 17 us -> 23.5 us
  local copies, waits for them, and re-layouts: 2.52 us -> 1.21 us
    ppermute x13 -> x10, waiting for transfers between devices: 24.8 us -> 10.8 us  [crossed(): return lax.ppermute(value, axis, [(i, i ^ mask) for i in range(count)])]
    ppermute x5, waiting for transfers between devices: 4.36 us -> 11.2 us  [turned_on(): lax.ppermute(value, axis, [(i, (i + steps) % count) for i in range(count)])]
    ppermute x5, starting transfers between devices: 8.55 us -> 13.6 us  [turned_on(): lax.ppermute(value, axis, [(i, (i + steps) % count) for i in range(count)])]
    all_to_all x0 -> x1, starting transfers between devices: none -> 3.6 us  [on_device(): lax.all_to_all(send_b, 'ctx', 0, 0, tiled=True, axis_index_groups=groups)]
    ppermute x13 -> x10, starting transfers between devices: 8.43 us -> 6.29 us  [crossed(): return lax.ppermute(value, axis, [(i, i ^ mask) for i in range(count)])]
    unnamed x28 -> x30, local copies, waits for them, and re-layouts: 2.51 us -> 1.2 us
  transfers between devices with their start and end apart: 18 -> 16, of which waited for: 9 -> 10; matrix products, arithmetic and copies ran while one was open for 1% -> 0% of each run, Pallas kernels for 15% -> 15%
where the time goes in v3:
time: 62.5 us; the launch traced here: 62 us
  starting transfers between devices  23.5 us (38%)
  waiting for transfers between devices  22 us (35%)
  Pallas kernels  14.4 us (23%)
  local copies, waits for them, and re-layouts  1.21 us (2%)
  between operations  0.86 us (1%)
    ppermute x5, starting transfers between devices, turned_on(): lax.ppermute(value, axis, [(i, (i + steps) % count) for i in range(count)])  13.6 us
    ppermute x5, waiting for transfers between devices, turned_on(): lax.ppermute(value, axis, [(i, (i + steps) % count) for i in range(count)])  11.2 us
    ppermute x10, waiting for transfers between devices, crossed(): return lax.ppermute(value, axis, [(i, i ^ mask) for i in range(count)])  10.8 us
    ppermute x10, starting transfers between devices, crossed(): return lax.ppermute(value, axis, [(i, i ^ mask) for i in range(count)])  6.29 us
    all_to_all x1, starting transfers between devices, on_device(): lax.all_to_all(send_b, 'ctx', 0, 0, tiled=True, axis_index_groups=groups)  3.6 us
    pallas_call x1, Pallas kernels, on_device(): call(functools.partial(pack_body, share), [shape((rows, chunk + 3 * LANES...  3.09 us
    pallas_call x1, Pallas kernels, on_device(): call(functools.partial(mixing_body, share), [shape((BLK, chunk), f32)] *...  2.4 us
    pallas_call x1, Pallas kernels, on_device(): call(functools.partial(first_body, share, blocks > 2), [shape((BLK, chunk...  2.33 us
  transfers between devices with their start and end apart: 16, of which 10 were waited for; matrix products, arithmetic and copies ran while one was open for 0% of the time, Pallas kernels for 15%

profile of v3, /device:TPU:0, one launch (start us, length us, event | category | flops | bytes accessed | tf_op | source)
XLA Modules:
  0.0 62.0 jit_solution(6482003694928798270)
XLA Ops:
  0.6 3.1 %shard_map.149 = (bf16[64,1408]{1,0:T(8,128)(2,1)}, bf16[64,1408]{1,0:T(8,128)(2,1)}, bf16[64,1408]{1,0:T(8,128)(2,1)}, bf16[64,1408]{1,0:T(8,128)(2,1)}, bf16[4...) custom-call(bf16[64,8192]{1,0:T(8,128)(2,1)} %bitcast.18, ...), custom_call_target="tpu_custom_call" | custom-call | bytes 5242880 | tf_op jit(solution)/shard_map/pallas_call | solution.py:620
  3.7 3.1 %collective-permute-start.1 = (bf16[64,1408]{1,0:T(8,128)(2,1)}, bf16[64,1408]{1,0:T(8,128)(2,1)S(1)}, u32[]{:S(2)}, u32[]{:S(2)}) collective-permute-start(bf16[64,1408]{1,0:T(8,128)(2,1)} %get-tuple-element.43), channel_id=1, source_target_pairs={{0,2},{1,3},{2,0},{3,1},{4,6},{5,7},{6,4},{7,5},{8,10},{9,11},{10,... | collective-permute-start | bytes 540680 | tf_op jit(solution)/shard_map/ppermute | solution.py:39
  6.8 0.2 collective-permute-start.2
  7.0 1.9 %collective-permute-start.4 = (bf16[96,512]{1,0:T(8,128)(2,1)}, bf16[96,512]{1,0:T(8,128)(2,1)S(1)}, u32[]{:S(2)}, u32[]{:S(2)}) collective-permute-start(bf16[96,512]{1,0:T(8,128)(2,1)} %get-tuple-element.54), channel_id=1, source_target_pairs={{0,2},{1,3},{2,4},{3,5},{4,6},{5,7},{6,0},{7,1},{8,10},{9,11},{10,... | collective-permute-start | bytes 294920 | tf_op jit(solution)/shard_map/ppermute | solution.py:34
  9.0 2.6 %collective-permute-start.5 = (bf16[96,512]{1,0:T(8,128)(2,1)}, bf16[96,512]{1,0:T(8,128)(2,1)S(1)}, u32[]{:S(2)}, u32[]{:S(2)}) collective-permute-start(bf16[96,512]{1,0:T(8,128)(2,1)} %get-tuple-element.55), channel_id=1, source_target_pairs={{0,4},{1,5},{2,6},{3,7},{4,0},{5,1},{6,2},{7,3},{8,12},{9,13},{10,... | collective-permute-start | bytes 294920 | tf_op jit(solution)/shard_map/ppermute | solution.py:34
  11.6 0.9 %collective-permute-done.1.refs_2_ = bf16[64,1408]{1,0:T(8,128)(2,1)S(1)} collective-permute-done((bf16[64,1408]{1,0:T(8,128)(2,1)}, bf16[64,1408]{1,0:T(8,128)(2,1)S(1)}, u32[]{:S(2)}, u32[]{:S(2)}) %collective-permute-start.1) | collective-permute-done | bytes 180256 | tf_op jit(solution)/shard_map/ppermute | solution.py:39
  12.4 3.6 %all-to-all-start = ((bf16[4,64,1024]{2,1,0:T(8,128)(2,1)}), bf16[4,64,1024]{2,1,0:T(8,128)(2,1)S(1)}, u32[]{:S(2)}, u32[]{:S(2)}) async-start(bf16[4,64,1024]{2,1,0:T(8,128)(2,1)} %get-tuple-element.47), calls=%async_computation | async-start | bytes 1048576 | tf_op jit(solution)/shard_map/all_to_all | solution.py:657
  16.1 0.6 copy-done.11
  16.8 0.2 collective-permute-done.2.refs_3_
  16.9 0.5 copy-done.4
  17.4 2.3 %shard_map.150 = (bf16[256,1024]{1,0:T(8,128)(2,1)S(1)}, bf16[256,256]{1,0:T(8,128)(2,1)S(1)}, bf16[128,1024]{1,0:T(8,128)(2,1)S(1)}, f32[264,128]{1,0:T(8,128)S...) custom-call(bf16[64,1408]{1,0:T(8,128)(2,1)S(1)} %copy-done.1, ...), custom_call_target="tpu_custom_call" | custom-call | bytes 1024 | tf_op jit(solution)/shard_map/pallas_call | solution.py:665
  19.8 1.1 %collective-permute-done.4 = bf16[96,512]{1,0:T(8,128)(2,1)S(1)} collective-permute-done((bf16[96,512]{1,0:T(8,128)(2,1)}, bf16[96,512]{1,0:T(8,128)(2,1)S(1)}, u32[]{:S(2)}, u32[]{:S(2)}) %collective-permute-start.4) | collective-permute-done | bytes 98336 | tf_op jit(solution)/shard_map/ppermute | solution.py:34
  20.9 0.5 collective-permute-start.6
  21.5 4.0 %collective-permute-start.3 = (bf16[128,1024]{1,0:T(8,128)(2,1)S(1)}, bf16[128,1024]{1,0:T(8,128)(2,1)S(1)}, u32[]{:S(2)}, u32[]{:S(2)}) collective-permute-start(bf16[128,1024]{1,0:T(8,128)(2,1)S(1)} %get-tuple-element.46), channel_id=1, source_target_pairs={{0,4},{1,5},{2,6},{3,7},{4,0},{5,1},{6,2},{7,3},{8,12},{9,13},{10,... | collective-permute-start | bytes 786440 | tf_op jit(solution)/shard_map/ppermute | solution.py:34
  25.5 2.1 %shard_map.153 = bf16[64,2048]{1,0:T(8,128)(2,1)S(1)} custom-call(bf16[64,2048]{1,0:T(8,128)(2,1)S(1)} %bitcast.17, bf16[272,512]{1,0:T(8,128)(2,1)S(1)} %constant_dynamic-update-slice_fusion.refs_7_.mine, bf16[272,512]{1,0:T(8,128)(2,1)S(1)} %collective-permute-done.6.refs_8_.other), custom_call_target="tpu_custom_call" | custom-call | flops 1073741824 | bytes 1048576 | tf_op jit(solution)/shard_map/pallas_call | solution.py:728
  27.6 1.7 %shard_map.151 = (bf16[256,1024]{1,0:T(8,128)(2,1)S(1)}, bf16[128,1024]{1,0:T(8,128)(2,1)S(1)}) custom-call(bf16[4,64,1024]{2,1,0:T(8,128)(2,1)S(1)} %all-to-all-done.refs_0_.refs_4_, bf16[4,8192]{1,0:T(4,128)(2,1)S(1)} %bitcast.13, bf16[256,256]{1,0:T(8,128)(2,1)S(1)} %get-tuple-element.49.refs_2_.refs_11_, f32[264,128]{1,0:T(8,128)S(1)} %get-tuple-element.50.refs_3_, ...), custom_call_target="tpu_custom_call" | custom-call | flops 268435456 | bytes 3145728 | tf_op jit(solution)/shard_map/pallas_call | solution.py:688
  29.4 2.5 %collective-permute-start.10 = (bf16[128,1024]{1,0:T(8,128)(2,1)S(1)}, bf16[128,1024]{1,0:T(8,128)(2,1)S(1)}, u32[]{:S(2)}, u32[]{:S(2)}) collective-permute-start(bf16[128,1024]{1,0:T(8,128)(2,1)S(1)} %get-tuple-element.69), channel_id=1, source_target_pairs={{0,4},{1,5},{2,6},{3,7},{4,0},{5,1},{6,2},{7,3},{8,12},{9,13},{10,... | collective-permute-start | bytes 786440 | tf_op jit(solution)/shard_map/ppermute | solution.py:34
  31.9 2.4 %shard_map.152 = (f32[256,1024]{1,0:T(8,128)S(1)}, f32[256,1024]{1,0:T(8,128)S(1)}, bf16[256,256]{1,0:T(8,128)(2,1)S(1)}, f32[256,128]{1,0:T(8,128)S(1)}) custom-call(bf16[64,1408]{1,0:T(8,128)(2,1)S(1)} %copy-done.1, bf16[64,1408]{1,0:T(8,128)(2,1)S(1)} %collective-permute-done.refs_1_, bf16[64,1408]{1,0:T(8,128)(2,1)S(1)} %collective-permute-done.1.refs_2_, ...), custom_call_target="tpu_custom_call" | custom-call | flops 2147483648 | bytes 4194304 | tf_op jit(solution)/shard_map/pallas_call | solution.py:714
  34.3 9.6 %collective-permute-done.3.state = bf16[128,1024]{1,0:T(8,128)(2,1)S(1)} collective-permute-done((bf16[128,1024]{1,0:T(8,128)(2,1)S(1)}, bf16[128,1024]{1,0:T(8,128)(2,1)S(1)}, u32[]{:S(2)}, u32[]{:S(2)}) %collective-permute-start.3) | collective-permute-done | bytes 262176 | tf_op jit(solution)/shard_map/ppermute | solution.py:34
  43.8 0.5 shard_map.154
  44.5 2.5 %collective-permute-start.14 = (bf16[64,2048]{1,0:T(8,128)(2,1)S(1)}, bf16[64,2048]{1,0:T(8,128)(2,1)S(1)}, u32[]{:S(2)}, u32[]{:S(2)}) collective-permute-start(bf16[64,2048]{1,0:T(8,128)(2,1)S(1)} %shard_map.153), channel_id=1, source_target_pairs={{0,8},{8,16},{16,24},{24,0},{1,9},{9,17},{17,25},{25,1},{2,10},{10... | collective-permute-start | bytes 786440 | tf_op jit(solution)/shard_map/ppermute | solution.py:34
  47.0 1.5 %collective-permute-start.9 = (bf16[64,1024]{1,0:T(8,128)(2,1)S(1)}, bf16[64,1024]{1,0:T(8,128)(2,1)S(1)}, u32[]{:S(2)}, u32[]{:S(2)}) collective-permute-start(bf16[64,1024]{1,0:T(8,128)(2,1)S(1)} %get-tuple-element.68), channel_id=1, source_target_pairs={{0,3},{1,2},{2,1},{3,0},{4,7},{5,6},{6,5},{7,4},{8,11},{9,10},{10,... | collective-permute-start | bytes 393224 | tf_op jit(solution)/shard_map/ppermute | solution.py:39
  48.5 0.3 collective-permute-done.10.state
  48.8 0.5 shard_map.155
  49.3 0.4 collective-permute-start.11
  49.7 0.5 collective-permute-start.12
  50.2 3.1 %collective-permute-done.8.refs_2_ = bf16[64,1024]{1,0:T(8,128)(2,1)S(1)} collective-permute-done((bf16[64,1024]{1,0:T(8,128)(2,1)S(1)}, bf16[64,1024]{1,0:T(8,128)(2,1)S(1)}, u32[]{:S(2)}, u32[]{:S(2)}) %collective-permute-start.8) | collective-permute-done | bytes 131104 | tf_op jit(solution)/shard_map/ppermute | solution.py:39
  53.3 1.3 %collective-permute-done.9.refs_3_ = bf16[64,1024]{1,0:T(8,128)(2,1)S(1)} collective-permute-done((bf16[64,1024]{1,0:T(8,128)(2,1)S(1)}, bf16[64,1024]{1,0:T(8,128)(2,1)S(1)}, u32[]{:S(2)}, u32[]{:S(2)}) %collective-permute-start.9) | collective-permute-done | bytes 131104 | tf_op jit(solution)/shard_map/ppermute | solution.py:39
  54.6 0.3 collective-permute-done.14.refs_10_
  54.9 4.1 %collective-permute-done.12.refs_6_ = bf16[64,1024]{1,0:T(8,128)(2,1)S(1)} collective-permute-done((bf16[64,1024]{1,0:T(8,128)(2,1)S(1)}, bf16[64,1024]{1,0:T(8,128)(2,1)S(1)}, u32[]{:S(2)}, u32[]{:S(2)}) %collective-permute-start.12) | collective-permute-done | bytes 131104 | tf_op jit(solution)/shard_map/ppermute | solution.py:39
  59.0 1.3 %collective-permute-done.13.refs_7_ = bf16[64,1024]{1,0:T(8,128)(2,1)S(1)} collective-permute-done((bf16[64,1024]{1,0:T(8,128)(2,1)S(1)}, bf16[64,1024]{1,0:T(8,128)(2,1)S(1)}, u32[]{:S(2)}, u32[]{:S(2)}) %collective-permute-start.13) | collective-permute-done | bytes 131104 | tf_op jit(solution)/shard_map/ppermute | solution.py:39
  60.2 1.7 %shard_map.156 = (bf16[64,8192]{1,0:T(8,128)(2,1)}, bf16[64,2048]{1,0:T(8,128)(2,1)}) custom-call(bf16[64,1024]{1,0:T(8,128)(2,1)S(1)} %get-tuple-element.65.refs_0_, bf16[64,1024]{1,0:T(8,128)(2,1)S(1)} %collective-permute-done.7.refs_1_, bf16[64,1024]{1,0:T(8,128)(2,1)S(1)} %collective-permute-done.8.refs_2_, ...), custom_call_target="tpu_custom_call" | custom-call | bytes 3145728 | tf_op jit(solution)/shard_map/pallas_call | solution.py:755
  (40 shorter events, 0.2 us)
Async XLA Ops:
  3.7 8.7 %collective-permute-start.1 = (bf16[64,1408]{1,0:T(8,128)(2,1)}, bf16[64,1408]{1,0:T(8,128)(2,1)S(1)}, u32[]{:S(2)}, u32[]{:S(2)}) collective-permute-start(bf16[64,1408]{1,0:T(8,128)(2,1)} %get-tuple-element.43), channel_id=1, source_target_pairs={{0,2},{1,3},{2,0},{3,1},{4,6},{5,7},{6,4},{7,5},{8,10},{9,11},{10,... | collective-permute-start | bytes 540680 | tf_op jit(solution)/shard_map/ppermute | solution.py:39
  6.8 9.9 %collective-permute-start = (bf16[64,1408]{1,0:T(8,128)(2,1)}, bf16[64,1408]{1,0:T(8,128)(2,1)S(1)}, u32[]{:S(2)}, u32[]{:S(2)}) collective-permute-start(bf16[64,1408]{1,0:T(8,128)(2,1)} %get-tuple-element.41), channel_id=1, source_target_pairs={{0,1},{1,0},{2,3},{3,2},{4,5},{5,4},{6,7},{7,6},{8,9},{9,8},{10,11... | collective-permute-start | bytes 540680 | tf_op jit(solution)/shard_map/ppermute | solution.py:39
  6.8 10.1 %collective-permute-start.2 = (bf16[64,1408]{1,0:T(8,128)(2,1)}, bf16[64,1408]{1,0:T(8,128)(2,1)S(1)}, u32[]{:S(2)}, u32[]{:S(2)}) collective-permute-start(bf16[64,1408]{1,0:T(8,128)(2,1)} %get-tuple-element.45), channel_id=1, source_target_pairs={{0,3},{1,2},{2,1},{3,0},{4,7},{5,6},{6,5},{7,4},{8,11},{9,10},{10,... | collective-permute-start | bytes 540680 | tf_op jit(solution)/shard_map/ppermute | solution.py:39
  7.0 13.9 %collective-permute-start.4 = (bf16[96,512]{1,0:T(8,128)(2,1)}, bf16[96,512]{1,0:T(8,128)(2,1)S(1)}, u32[]{:S(2)}, u32[]{:S(2)}) collective-permute-start(bf16[96,512]{1,0:T(8,128)(2,1)} %get-tuple-element.54), channel_id=1, source_target_pairs={{0,2},{1,3},{2,4},{3,5},{4,6},{5,7},{6,0},{7,1},{8,10},{9,11},{10,... | collective-permute-start | bytes 294920 | tf_op jit(solution)/shard_map/ppermute | solution.py:34
  9.0 11.9 %collective-permute-start.5 = (bf16[96,512]{1,0:T(8,128)(2,1)}, bf16[96,512]{1,0:T(8,128)(2,1)S(1)}, u32[]{:S(2)}, u32[]{:S(2)}) collective-permute-start(bf16[96,512]{1,0:T(8,128)(2,1)} %get-tuple-element.55), channel_id=1, source_target_pairs={{0,4},{1,5},{2,6},{3,7},{4,0},{5,1},{6,2},{7,3},{8,12},{9,13},{10,... | collective-permute-start | bytes 294920 | tf_op jit(solution)/shard_map/ppermute | solution.py:34
  12.4 3.6 %copy-start.10 = (bf16[80,512]{1,0:T(8,128)(2,1)S(1)}, bf16[80,512]{1,0:T(8,128)(2,1)}, u32[]{:S(2)}) copy-start(bf16[80,512]{1,0:T(8,128)(2,1)} %get-tuple-element.53) | copy-start | bytes 245764
  12.4 4.5 %copy-start.1 = (bf16[64,1408]{1,0:T(8,128)(2,1)S(1)}, bf16[64,1408]{1,0:T(8,128)(2,1)}, u32[]{:S(2)}) copy-start(bf16[64,1408]{1,0:T(8,128)(2,1)} %get-tuple-element.40.refs_0_) | copy-start | bytes 540676
  12.4 15.2 %all-to-all-start = ((bf16[4,64,1024]{2,1,0:T(8,128)(2,1)}), bf16[4,64,1024]{2,1,0:T(8,128)(2,1)S(1)}, u32[]{:S(2)}, u32[]{:S(2)}) async-start(bf16[4,64,1024]{2,1,0:T(8,128)(2,1)} %get-tuple-element.47), calls=%async_computation | async-start | bytes 1048576 | tf_op jit(solution)/shard_map/all_to_all | solution.py:657
  16.0 0.7 %copy-start.11 = (f32[1,128]{1,0:T(1,128)S(1)}, f32[1,128]{1,0:T(1,128)}, u32[]{:S(2)}) copy-start(f32[1,128]{1,0:T(1,128)} %param.20) | copy-start | bytes 1540
  16.1 0.7 %copy-start.12 = (f32[1,128]{1,0:T(1,128)S(1)}, f32[1,128]{1,0:T(1,128)}, u32[]{:S(2)}) copy-start(f32[1,128]{1,0:T(1,128)} %param.18) | copy-start | bytes 1540
  16.1 0.7 %copy-start.13 = (f32[1,128]{1,0:T(1,128)S(1)}, f32[1,128]{1,0:T(1,128)}, u32[]{:S(2)}) copy-start(f32[1,128]{1,0:T(1,128)} %param.19) | copy-start | bytes 1540
  16.1 0.9 %copy-start.2 = (bf16[1,4,8192]{2,1,0:T(4,128)(2,1)S(1)}, bf16[1,4,8192]{2,1,0:T(4,128)(2,1)}, u32[]{:S(2)}) copy-start(bf16[1,4,8192]{2,1,0:T(4,128)(2,1)} %param.21) | copy-start | bytes 196612
  16.7 0.7 %copy-start.4 = (bf16[1,4,1024]{2,1,0:T(4,128)(2,1)S(1)}, bf16[1,4,1024]{2,1,0:T(4,128)(2,1)}, u32[]{:S(2)}) copy-start(bf16[1,4,1024]{2,1,0:T(4,128)(2,1)} %param.22) | copy-start | bytes 24580
  19.8 1.2 %copy-start.6 = (f32[256,128]{1,0:T(8,128)}, f32[256,128]{1,0:T(8,128)S(1)}, u32[]{:S(2)}) copy-start(f32[256,128]{1,0:T(8,128)S(1)} %get-tuple-element.59.refs_12_) | copy-start | bytes 393220
  19.8 1.2 %copy-start.8 = (f32[256,128]{1,0:T(8,128)}, f32[256,128]{1,0:T(8,128)S(1)}, u32[]{:S(2)}) copy-start(f32[256,128]{1,0:T(8,128)S(1)} %get-tuple-element.60.refs_13_) | copy-start | bytes 393220
  19.8 5.7 %copy-start.5 = (bf16[1,64,2048]{2,1,0:T(8,128)(2,1)S(1)}, bf16[1,64,2048]{2,1,0:T(8,128)(2,1)}, u32[]{:S(2)}) copy-start(bf16[1,64,2048]{2,1,0:T(8,128)(2,1)} %param.25) | copy-start | bytes 786436
  20.9 4.6 %collective-permute-start.6 = (bf16[272,512]{1,0:T(8,128)(2,1)S(1)}, bf16[272,512]{1,0:T(8,128)(2,1)S(1)}, u32[]{:S(2)}, u32[]{:S(2)}) collective-permute-start(bf16[272,512]{1,0:T(8,128)(2,1)S(1)} %constant_dynamic-update-slice_fusion.refs_7_.mine), channel_id=1, source_target_pairs={{0,1},{1,0},{2,3},{3,2},{4,5},{5,4},{6,7},{7,6},{8,9},{9,8},{10,11... | collective-permute-start | bytes 835592 | tf_op jit(solution)/shard_map/ppermute | solution.py:39
  21.5 22.4 %collective-permute-start.3 = (bf16[128,1024]{1,0:T(8,128)(2,1)S(1)}, bf16[128,1024]{1,0:T(8,128)(2,1)S(1)}, u32[]{:S(2)}, u32[]{:S(2)}) collective-permute-start(bf16[128,1024]{1,0:T(8,128)(2,1)S(1)} %get-tuple-element.46), channel_id=1, source_target_pairs={{0,4},{1,5},{2,6},{3,7},{4,0},{5,1},{6,2},{7,3},{8,12},{9,13},{10,... | collective-permute-start | bytes 786440 | tf_op jit(solution)/shard_map/ppermute | solution.py:34
  27.6 4.2 %copy-start.7 = (f32[256,128]{1,0:T(8,128)S(1)}, f32[256,128]{1,0:T(8,128)}, u32[]{:S(2)}) copy-start(f32[256,128]{1,0:T(8,128)} %copy-done.6) | copy-start | bytes 393220
  27.6 4.2 %copy-start.9 = (f32[256,128]{1,0:T(8,128)S(1)}, f32[256,128]{1,0:T(8,128)}, u32[]{:S(2)}) copy-start(f32[256,128]{1,0:T(8,128)} %copy-done.8) | copy-start | bytes 393220
  29.4 19.5 %collective-permute-start.10 = (bf16[128,1024]{1,0:T(8,128)(2,1)S(1)}, bf16[128,1024]{1,0:T(8,128)(2,1)S(1)}, u32[]{:S(2)}, u32[]{:S(2)}) collective-permute-start(bf16[128,1024]{1,0:T(8,128)(2,1)S(1)} %get-tuple-element.69), channel_id=1, source_target_pairs={{0,4},{1,5},{2,6},{3,7},{4,0},{5,1},{6,2},{7,3},{8,12},{9,13},{10,... | collective-permute-start | bytes 786440 | tf_op jit(solution)/shard_map/ppermute | solution.py:34
  44.4 15.9 %copy-start = (bf16[1,64,8192]{2,1,0:T(8,128)(2,1)S(1)}, bf16[1,64,8192]{2,1,0:T(8,128)(2,1)}, u32[]{:S(2)}) copy-start(bf16[1,64,8192]{2,1,0:T(8,128)(2,1)} %param.15) | copy-start | bytes 3145732
  44.4 5.3 %collective-permute-start.7 = (bf16[64,1024]{1,0:T(8,128)(2,1)S(1)}, bf16[64,1024]{1,0:T(8,128)(2,1)S(1)}, u32[]{:S(2)}, u32[]{:S(2)}) collective-permute-start(bf16[64,1024]{1,0:T(8,128)(2,1)S(1)} %get-tuple-element.66), channel_id=1, source_target_pairs={{0,1},{1,0},{2,3},{3,2},{4,5},{5,4},{6,7},{7,6},{8,9},{9,8},{10,11... | collective-permute-start | bytes 393224 | tf_op jit(solution)/shard_map/ppermute | solution.py:39
  44.5 10.4 %collective-permute-start.14 = (bf16[64,2048]{1,0:T(8,128)(2,1)S(1)}, bf16[64,2048]{1,0:T(8,128)(2,1)S(1)}, u32[]{:S(2)}, u32[]{:S(2)}) collective-permute-start(bf16[64,2048]{1,0:T(8,128)(2,1)S(1)} %shard_map.153), channel_id=1, source_target_pairs={{0,8},{8,16},{16,24},{24,0},{1,9},{9,17},{17,25},{25,1},{2,10},{10... | collective-permute-start | bytes 786440 | tf_op jit(solution)/shard_map/ppermute | solution.py:34
  47.0 6.3 %collective-permute-start.8 = (bf16[64,1024]{1,0:T(8,128)(2,1)S(1)}, bf16[64,1024]{1,0:T(8,128)(2,1)S(1)}, u32[]{:S(2)}, u32[]{:S(2)}) collective-permute-start(bf16[64,1024]{1,0:T(8,128)(2,1)S(1)} %get-tuple-element.67), channel_id=1, source_target_pairs={{0,2},{1,3},{2,0},{3,1},{4,6},{5,7},{6,4},{7,5},{8,10},{9,11},{10,... | collective-permute-start | bytes 393224 | tf_op jit(solution)/shard_map/ppermute | solution.py:39
  47.0 7.6 %collective-permute-start.9 = (bf16[64,1024]{1,0:T(8,128)(2,1)S(1)}, bf16[64,1024]{1,0:T(8,128)(2,1)S(1)}, u32[]{:S(2)}, u32[]{:S(2)}) collective-permute-start(bf16[64,1024]{1,0:T(8,128)(2,1)S(1)} %get-tuple-element.68), channel_id=1, source_target_pairs={{0,3},{1,2},{2,1},{3,0},{4,7},{5,6},{6,5},{7,4},{8,11},{9,10},{10,... | collective-permute-start | bytes 393224 | tf_op jit(solution)/shard_map/ppermute | solution.py:39
  48.8 11.4 %copy-start.3 = (f32[1,8192]{1,0:T(1,128)S(1)}, f32[1,8192]{1,0:T(1,128)}, u32[]{:S(2)}) copy-start(f32[1,8192]{1,0:T(1,128)} %refs_9_.1) | copy-start | bytes 98308
  49.3 5.5 %collective-permute-start.11 = (bf16[64,1024]{1,0:T(8,128)(2,1)S(1)}, bf16[64,1024]{1,0:T(8,128)(2,1)S(1)}, u32[]{:S(2)}, u32[]{:S(2)}) collective-permute-start(bf16[64,1024]{1,0:T(8,128)(2,1)S(1)} %get-tuple-element.72), channel_id=1, source_target_pairs={{0,1},{1,0},{2,3},{3,2},{4,5},{5,4},{6,7},{7,6},{8,9},{9,8},{10,11... | collective-permute-start | bytes 393224 | tf_op jit(solution)/shard_map/ppermute | solution.py:39
  49.7 9.2 %collective-permute-start.12 = (bf16[64,1024]{1,0:T(8,128)(2,1)S(1)}, bf16[64,1024]{1,0:T(8,128)(2,1)S(1)}, u32[]{:S(2)}, u32[]{:S(2)}) collective-permute-start(bf16[64,1024]{1,0:T(8,128)(2,1)S(1)} %get-tuple-element.73), channel_id=1, source_target_pairs={{0,2},{1,3},{2,0},{3,1},{4,6},{5,7},{6,4},{7,5},{8,10},{9,11},{10,... | collective-permute-start | bytes 393224 | tf_op jit(solution)/shard_map/ppermute | solution.py:39
  53.3 6.9 %collective-permute-start.13 = (bf16[64,1024]{1,0:T(8,128)(2,1)S(1)}, bf16[64,1024]{1,0:T(8,128)(2,1)S(1)}, u32[]{:S(2)}, u32[]{:S(2)}) collective-permute-start(bf16[64,1024]{1,0:T(8,128)(2,1)S(1)} %get-tuple-element.74), channel_id=1, source_target_pairs={{0,3},{1,2},{2,1},{3,0},{4,7},{5,6},{6,5},{7,4},{8,11},{9,10},{10,... | collective-permute-start | bytes 393224 | tf_op jit(solution)/shard_map/ppermute | solution.py:39

commit v4 on v3

--- a/solution.py
+++ b/solution.py
@@ -256,6 +256,19 @@
     )
 
 
+def decays(marks, gains, me):
+    length = marks.shape[0]
+    raw = marks + turned(gains[0:1, :], me)[0:1, :]
+    step = jnp.maximum(raw, 0.0) + jnp.log1p(jnp.exp(-jnp.abs(raw)))
+    total = step * (-jnp.exp(turned(gains[1:2, :], me)[0:1, :]))
+    row = iota((length, LANES), 0)
+    reach = 1
+    while reach < length:
+        total = total + jnp.where(row >= reach, pltpu.roll(total, reach, 0), 0.0)
+        reach *= 2
+    return step, total
+
+
 def first_body(share, with_halo, *refs):
     pieces = refs[:share]
     convx, convbc, gains = refs[share : share + 3]
@@ -264,7 +277,7 @@
     if with_halo:
         picked = pick_halo(me, pieces[0].shape[0], rest[0], rest[1])
         rest = rest[2:]
-    xc_o, bcc_o, state_o, ids_o, cum_o, step_o, writes_o, xs, bs, masks = rest
+    xc_o, bcc_o, state_o, ids_o, writes_o, *decay_o, xs, bs, masks = rest
     chunk = xc_o.shape[1]
     piece = chunk * CHUNKS
     rows = pieces[0].shape[0]
@@ -287,22 +300,15 @@
         columns = slice(half * LANES, (half + 1) * LANES)
         taps = taps_at(convbc, half * G * LANES + me * LANES)
         bcc_o[:, columns] = conv_strip(bs, columns, masks, taps)
-    raw = bs[8:, 2 * LANES : 3 * LANES] + turned(gains[0:1, :], me)[0:1, :]
-    step = jnp.maximum(raw, 0.0) + jnp.log1p(jnp.exp(-jnp.abs(raw)))
-    total = step * (-jnp.exp(turned(gains[1:2, :], me)[0:1, :]))
-    row = iota((length, LANES), 0)
-    reach = 1
-    while reach < length:
-        total = total + jnp.where(row >= reach, pltpu.roll(total, reach, 0), 0.0)
-        reach *= 2
+    step, total = decays(bs[8:, 2 * LANES : 3 * LANES], gains, me)
     own = ids_o[8:, :]
     last = length - 1
     writes = (
         jnp.where(own == own[last : last + 1, :], jnp.exp(total[last : last + 1, :] - total), 0.0)
         * step
     )
-    cum_o[...] = total
-    step_o[...] = step
+    for fade in decay_o:
+        fade[...] = jnp.broadcast_to(jnp.exp(total[last : last + 1, :]), (8, LANES))
     packed = three_parts(writes)
     writes_o[...] = packed
     conv_x_and_state(xs, masks, convx, me * piece, bcc_o[:, :LANES], packed, 0, xc_o, state_o)
@@ -336,8 +342,8 @@
 def mixing_body(share, *refs):
     pieces, seconds = refs[:share], refs[share]
     xcs, refs = refs[share + 1 : share + 1 + CHUNKS], refs[share + 1 + CHUNKS :]
-    mine, other, convx, convbc, bcc_in, cum, step, skip = refs[:8]
-    rest = refs[8:]
+    mine, other, convx, convbc, bcc_in, skip = refs[:6]
+    rest = refs[6:]
     outs, (bcc, keep, head, head_ids, masks, first_x) = rest[:CHUNKS], rest[CHUNKS:]
     me = lax.rem(lax.axis_index("ctx"), share)
     length, chunk = xcs[0].shape
@@ -384,10 +390,10 @@
     own = jnp.broadcast_to(ids[:, LOCAL_HEADS : LOCAL_HEADS + 1], (length, length))
     allowed = (iota((length, length), 0) >= iota((length, length), 1)) & (own == across)
     inner = jnp.where(allowed, inner, 0.0)
-    cums = cum[...]
+    step, cums = decays(ids, skip, me)
     keep[...] = jnp.where(own[:, :LANES] == head_ids[7:8, :], jnp.exp(cums), 0.0)
     cum_rows = cums.T
-    step_rows = step[...].T
+    step_rows = step.T
     gains = three_parts(turned(skip[2:3, :], me))
     even = iota((half, LANES), 1) < HD
     for c in range(CHUNKS):
@@ -662,17 +668,16 @@
         halo = [mine, other]
     per_token = shape((BLK, LANES), f32)
     head_gains = jnp.concatenate([dt_bias, a_log, d_skip], axis=0)
-    xc_a, bcc_first, state_a, ids_col, cum, step, writes = call(
+    xc_a, bcc_first, state_a, ids_col, writes, *decay = call(
         functools.partial(first_body, share, blocks > 2),
         [
             shape((BLK, chunk), bf16),
             shape((BLK, 2 * LANES), bf16),
             shape((LANES, chunk), state_type),
             shape((BLK + 8, LANES), f32),
-            per_token,
-            per_token,
             shape((BLK, LANES), bf16),
-        ],
+        ]
+        + ([shape((8, LANES), f32)] if blocks > 2 else []),
         scratch=[
             pltpu.VMEM((BLK + 8, chunk), f32),
             pltpu.VMEM((BLK + 8, wide), f32),
@@ -681,8 +686,9 @@
         flops=0,
         bytes_accessed=1024,
     )(*pieces, conv_x[0], conv_bc[0], head_gains, *halo)
+    bcc_mixing = bcc_first
     if blocks <= 2:
-        near, far, cum = lax.optimization_barrier((near, far, cum))
+        near, far, bcc_mixing = lax.optimization_barrier((near, far, bcc_first))
         mine = jnp.concatenate([kv_own, near, far], axis=0)
         other = crossed(mine, "ctx", 1)
     xc_b, state_b = call(
@@ -697,7 +703,7 @@
     def entering(state, first):
         if blocks > 2:
             same = ids_col[BLK + 7, :] == ids_col[7, :]
-            fade = jnp.where(same, jnp.exp(cum[BLK - 1, :]), 0.0)[first : first + per_head]
+            fade = jnp.where(same, decay[0][0, :], 0.0)[first : first + per_head]
             fade = jnp.repeat(fade, HD)[None, :]
             far = 1
             while far < blocks:
@@ -722,7 +728,7 @@
         ],
         flops=2**31,
         bytes_accessed=4 * 2**20,
-    )(*pieces, pieces_b, xc_a, xc_b, mine, other, conv_x[0], conv_bc[0], bcc_first, cum, step, head_gains)
+    )(*pieces, pieces_b, xc_a, xc_b, mine, other, conv_x[0], conv_bc[0], bcc_mixing, head_gains)
 
     if reach <= share:
         attended = call(

time: 62.5 us -> 61.9 us (level)
  waiting for transfers between devices: 22 us -> 21.3 us
  transfers between devices with their start and end apart: 16 -> 16, of which waited for: 10 -> 10; matrix products, arithmetic and copies ran while one was open for 0% -> 0% of each run, Pallas kernels for 15% -> 16%
where the time goes in v4:
time: 61.9 us; the launch traced here: 61.4 us
  starting transfers between devices  23.6 us (38%)
  waiting for transfers between devices  21.3 us (34%)
  Pallas kernels  14.5 us (23%)
  local copies, waits for them, and re-layouts  1.19 us (2%)
  between operations  0.82 us (1%)
    ppermute x5, starting transfers between devices, turned_on(): lax.ppermute(value, axis, [(i, (i + steps) % count) for i in range(count)])  14.1 us
    ppermute x10, waiting for transfers between devices, crossed(): return lax.ppermute(value, axis, [(i, i ^ mask) for i in range(count)])  10.7 us
    ppermute x5, waiting for transfers between devices, turned_on(): lax.ppermute(value, axis, [(i, (i + steps) % count) for i in range(count)])  10.6 us
    ppermute x10, starting transfers between devices, crossed(): return lax.ppermute(value, axis, [(i, i ^ mask) for i in range(count)])  5.84 us
    all_to_all x1, starting transfers between devices, on_device(): lax.all_to_all(send_b, 'ctx', 0, 0, tiled=True, axis_index_groups=groups)  3.6 us
    pallas_call x1, Pallas kernels, on_device(): call(functools.partial(pack_body, share), [shape((rows, chunk + 3 * LANES...  3.1 us
    pallas_call x1, Pallas kernels, on_device(): call(functools.partial(mixing_body, share), [shape((BLK, chunk), f32)] *...  2.54 us
    pallas_call x1, Pallas kernels, on_device(): call(functools.partial(first_body, share, blocks > 2), [shape((BLK, chunk...  2.32 us
  transfers between devices with their start and end apart: 16, of which 10 were waited for; matrix products, arithmetic and copies ran while one was open for 0% of the time, Pallas kernels for 16%

profile of v4, /device:TPU:0, one launch (start us, length us, event | category | flops | bytes accessed | tf_op | source)
XLA Modules:
  0.0 61.4 jit_solution(12378685928327374755)
XLA Ops:
  0.6 3.1 %shard_map.149 = (bf16[64,1408]{1,0:T(8,128)(2,1)}, bf16[64,1408]{1,0:T(8,128)(2,1)}, bf16[64,1408]{1,0:T(8,128)(2,1)}, bf16[64,1408]{1,0:T(8,128)(2,1)}, bf16[4...) custom-call(bf16[64,8192]{1,0:T(8,128)(2,1)} %bitcast.18, ...), custom_call_target="tpu_custom_call" | custom-call | bytes 5242880 | tf_op jit(solution)/shard_map/pallas_call | solution.py:626
  3.7 3.1 %collective-permute-start.1 = (bf16[64,1408]{1,0:T(8,128)(2,1)}, bf16[64,1408]{1,0:T(8,128)(2,1)S(1)}, u32[]{:S(2)}, u32[]{:S(2)}) collective-permute-start(bf16[64,1408]{1,0:T(8,128)(2,1)} %get-tuple-element.41), channel_id=1, source_target_pairs={{0,2},{1,3},{2,0},{3,1},{4,6},{5,7},{6,4},{7,5},{8,10},{9,11},{10,... | collective-permute-start | bytes 540680 | tf_op jit(solution)/shard_map/ppermute | solution.py:39
  6.8 0.2 collective-permute-start.2
  7.0 1.9 %collective-permute-start.4 = (bf16[96,512]{1,0:T(8,128)(2,1)}, bf16[96,512]{1,0:T(8,128)(2,1)S(1)}, u32[]{:S(2)}, u32[]{:S(2)}) collective-permute-start(bf16[96,512]{1,0:T(8,128)(2,1)} %get-tuple-element.52), channel_id=1, source_target_pairs={{0,2},{1,3},{2,4},{3,5},{4,6},{5,7},{6,0},{7,1},{8,10},{9,11},{10,... | collective-permute-start | bytes 294920 | tf_op jit(solution)/shard_map/ppermute | solution.py:34
  9.0 2.6 %collective-permute-start.5 = (bf16[96,512]{1,0:T(8,128)(2,1)}, bf16[96,512]{1,0:T(8,128)(2,1)S(1)}, u32[]{:S(2)}, u32[]{:S(2)}) collective-permute-start(bf16[96,512]{1,0:T(8,128)(2,1)} %get-tuple-element.53), channel_id=1, source_target_pairs={{0,4},{1,5},{2,6},{3,7},{4,0},{5,1},{6,2},{7,3},{8,12},{9,13},{10,... | collective-permute-start | bytes 294920 | tf_op jit(solution)/shard_map/ppermute | solution.py:34
  11.6 0.9 %collective-permute-done.1.refs_2_ = bf16[64,1408]{1,0:T(8,128)(2,1)S(1)} collective-permute-done((bf16[64,1408]{1,0:T(8,128)(2,1)}, bf16[64,1408]{1,0:T(8,128)(2,1)S(1)}, u32[]{:S(2)}, u32[]{:S(2)}) %collective-permute-start.1) | collective-permute-done | bytes 180256 | tf_op jit(solution)/shard_map/ppermute | solution.py:39
  12.4 3.6 %all-to-all-start = ((bf16[4,64,1024]{2,1,0:T(8,128)(2,1)}), bf16[4,64,1024]{2,1,0:T(8,128)(2,1)S(1)}, u32[]{:S(2)}, u32[]{:S(2)}) async-start(bf16[4,64,1024]{2,1,0:T(8,128)(2,1)} %get-tuple-element.45), calls=%async_computation | async-start | bytes 1048576 | tf_op jit(solution)/shard_map/all_to_all | solution.py:663
  16.1 0.6 copy-done.7
  16.8 0.2 collective-permute-done.2.refs_3_
  17.0 0.5 copy-done.4
  17.4 2.3 %shard_map.150 = (bf16[256,1024]{1,0:T(8,128)(2,1)S(1)}, bf16[256,256]{1,0:T(8,128)(2,1)S(1)}, bf16[128,1024]{1,0:T(8,128)(2,1)S(1)}, f32[264,128]{1,0:T(8,128)S(1)}, bf16[256,128]{1,0:T(8,128)(2,1)S(1)}) custom-call(bf16[64,1408]{1,0:T(8,128)(2,1)S(1)} %copy-done.1, bf16[64,1408]{1,0:T(8,128)(2,1)S(1)} %collective-permute-done.refs_1_, ...), custom_call_target="tpu_custom_call" | custom-call | bytes 1024 | tf_op jit(solution)/shard_map/pallas_call | solution.py:671
  19.8 1.1 %collective-permute-done.4 = bf16[96,512]{1,0:T(8,128)(2,1)S(1)} collective-permute-done((bf16[96,512]{1,0:T(8,128)(2,1)}, bf16[96,512]{1,0:T(8,128)(2,1)S(1)}, u32[]{:S(2)}, u32[]{:S(2)}) %collective-permute-start.4) | collective-permute-done | bytes 98336 | tf_op jit(solution)/shard_map/ppermute | solution.py:34
  20.9 0.1 collective-permute-start.6
  21.0 3.9 %collective-permute-start.3 = (bf16[128,1024]{1,0:T(8,128)(2,1)S(1)}, bf16[128,1024]{1,0:T(8,128)(2,1)S(1)}, u32[]{:S(2)}, u32[]{:S(2)}) collective-permute-start(bf16[128,1024]{1,0:T(8,128)(2,1)S(1)} %get-tuple-element.44), channel_id=1, source_target_pairs={{0,4},{1,5},{2,6},{3,7},{4,0},{5,1},{6,2},{7,3},{8,12},{9,13},{10,... | collective-permute-start | bytes 786440 | tf_op jit(solution)/shard_map/ppermute | solution.py:34
  24.9 2.1 %shard_map.153 = bf16[64,2048]{1,0:T(8,128)(2,1)S(1)} custom-call(bf16[64,2048]{1,0:T(8,128)(2,1)S(1)} %bitcast.17, bf16[272,512]{1,0:T(8,128)(2,1)S(1)} %constant_dynamic-update-slice_fusion.refs_7_.mine, bf16[272,512]{1,0:T(8,128)(2,1)S(1)} %collective-permute-done.6.refs_8_.other), custom_call_target="tpu_custom_call" | custom-call | flops 1073741824 | bytes 1048576 | tf_op jit(solution)/shard_map/pallas_call | solution.py:734
  27.1 1.7 %shard_map.151 = (bf16[256,1024]{1,0:T(8,128)(2,1)S(1)}, bf16[128,1024]{1,0:T(8,128)(2,1)S(1)}) custom-call(bf16[4,64,1024]{2,1,0:T(8,128)(2,1)S(1)} %all-to-all-done.refs_0_.refs_4_, bf16[4,8192]{1,0:T(4,128)(2,1)S(1)} %bitcast.13, bf16[256,256]{1,0:T(8,128)(2,1)S(1)} %get-tuple-element.56.refs_2_.refs_11_, f32[264,128]{1,0:T(8,128)S(1)} %get-tuple-element.48.refs_3_, ...), custom_call_target="tpu_custom_call" | custom-call | flops 268435456 | bytes 3145728 | tf_op jit(solution)/shard_map/pallas_call | solution.py:694
  28.8 3.1 %collective-permute-start.10 = (bf16[128,1024]{1,0:T(8,128)(2,1)S(1)}, bf16[128,1024]{1,0:T(8,128)(2,1)S(1)}, u32[]{:S(2)}, u32[]{:S(2)}) collective-permute-start(bf16[128,1024]{1,0:T(8,128)(2,1)S(1)} %get-tuple-element.65), channel_id=1, source_target_pairs={{0,4},{1,5},{2,6},{3,7},{4,0},{5,1},{6,2},{7,3},{8,12},{9,13},{10,... | collective-permute-start | bytes 786440 | tf_op jit(solution)/shard_map/ppermute | solution.py:34
  31.9 2.5 %shard_map.152 = (f32[256,1024]{1,0:T(8,128)S(1)}, f32[256,1024]{1,0:T(8,128)S(1)}, bf16[256,256]{1,0:T(8,128)(2,1)S(1)}, f32[256,128]{1,0:T(8,128)S(1)}) custom-call(bf16[64,1408]{1,0:T(8,128)(2,1)S(1)} %copy-done.1, bf16[64,1408]{1,0:T(8,128)(2,1)S(1)} %collective-permute-done.refs_1_, bf16[64,1408]{1,0:T(8,128)(2,1)S(1)} %collective-permute-done.1.refs_2_, ...), custom_call_target="tpu_custom_call" | custom-call | flops 2147483648 | bytes 4194304 | tf_op jit(solution)/shard_map/pallas_call | solution.py:720
  34.4 8.9 %collective-permute-done.3.state = bf16[128,1024]{1,0:T(8,128)(2,1)S(1)} collective-permute-done((bf16[128,1024]{1,0:T(8,128)(2,1)S(1)}, bf16[128,1024]{1,0:T(8,128)(2,1)S(1)}, u32[]{:S(2)}, u32[]{:S(2)}) %collective-permute-start.3) | collective-permute-done | bytes 262176 | tf_op jit(solution)/shard_map/ppermute | solution.py:34
  43.3 0.5 shard_map.154
  43.9 2.6 %collective-permute-start.14 = (bf16[64,2048]{1,0:T(8,128)(2,1)S(1)}, bf16[64,2048]{1,0:T(8,128)(2,1)S(1)}, u32[]{:S(2)}, u32[]{:S(2)}) collective-permute-start(bf16[64,2048]{1,0:T(8,128)(2,1)S(1)} %shard_map.153), channel_id=1, source_target_pairs={{0,8},{8,16},{16,24},{24,0},{1,9},{9,17},{17,25},{25,1},{2,10},{10... | collective-permute-start | bytes 786440 | tf_op jit(solution)/shard_map/ppermute | solution.py:34
  46.4 1.5 %collective-permute-start.9 = (bf16[64,1024]{1,0:T(8,128)(2,1)S(1)}, bf16[64,1024]{1,0:T(8,128)(2,1)S(1)}, u32[]{:S(2)}, u32[]{:S(2)}) collective-permute-start(bf16[64,1024]{1,0:T(8,128)(2,1)S(1)} %get-tuple-element.64), channel_id=1, source_target_pairs={{0,3},{1,2},{2,1},{3,0},{4,7},{5,6},{6,5},{7,4},{8,11},{9,10},{10,... | collective-permute-start | bytes 393224 | tf_op jit(solution)/shard_map/ppermute | solution.py:39
  48.0 0.4 collective-permute-done.10.state
  48.3 0.5 shard_map.155
  48.8 0.3 collective-permute-start.11
  49.2 0.6 collective-permute-start.12
  49.7 3.0 %collective-permute-done.8.refs_2_ = bf16[64,1024]{1,0:T(8,128)(2,1)S(1)} collective-permute-done((bf16[64,1024]{1,0:T(8,128)(2,1)S(1)}, bf16[64,1024]{1,0:T(8,128)(2,1)S(1)}, u32[]{:S(2)}, u32[]{:S(2)}) %collective-permute-start.8) | collective-permute-done | bytes 131104 | tf_op jit(solution)/shard_map/ppermute | solution.py:39
  52.8 1.3 %collective-permute-done.9.refs_3_ = bf16[64,1024]{1,0:T(8,128)(2,1)S(1)} collective-permute-done((bf16[64,1024]{1,0:T(8,128)(2,1)S(1)}, bf16[64,1024]{1,0:T(8,128)(2,1)S(1)}, u32[]{:S(2)}, u32[]{:S(2)}) %collective-permute-start.9) | collective-permute-done | bytes 131104 | tf_op jit(solution)/shard_map/ppermute | solution.py:39
  54.0 0.3 collective-permute-done.14.refs_10_
  54.3 4.1 %collective-permute-done.12.refs_6_ = bf16[64,1024]{1,0:T(8,128)(2,1)S(1)} collective-permute-done((bf16[64,1024]{1,0:T(8,128)(2,1)S(1)}, bf16[64,1024]{1,0:T(8,128)(2,1)S(1)}, u32[]{:S(2)}, u32[]{:S(2)}) %collective-permute-start.12) | collective-permute-done | bytes 131104 | tf_op jit(solution)/shard_map/ppermute | solution.py:39
  58.4 1.3 %collective-permute-done.13.refs_7_ = bf16[64,1024]{1,0:T(8,128)(2,1)S(1)} collective-permute-done((bf16[64,1024]{1,0:T(8,128)(2,1)S(1)}, bf16[64,1024]{1,0:T(8,128)(2,1)S(1)}, u32[]{:S(2)}, u32[]{:S(2)}) %collective-permute-start.13) | collective-permute-done | bytes 131104 | tf_op jit(solution)/shard_map/ppermute | solution.py:39
  59.7 1.7 %shard_map.156 = (bf16[64,8192]{1,0:T(8,128)(2,1)}, bf16[64,2048]{1,0:T(8,128)(2,1)}) custom-call(bf16[64,1024]{1,0:T(8,128)(2,1)S(1)} %get-tuple-element.61.refs_0_, bf16[64,1024]{1,0:T(8,128)(2,1)S(1)} %collective-permute-done.7.refs_1_, bf16[64,1024]{1,0:T(8,128)(2,1)S(1)} %collective-permute-done.8.refs_2_, ...), custom_call_target="tpu_custom_call" | custom-call | bytes 3145728 | tf_op jit(solution)/shard_map/pallas_call | solution.py:761
  (32 shorter events, 0.2 us)
Async XLA Ops:
  3.7 8.7 %collective-permute-start.1 = (bf16[64,1408]{1,0:T(8,128)(2,1)}, bf16[64,1408]{1,0:T(8,128)(2,1)S(1)}, u32[]{:S(2)}, u32[]{:S(2)}) collective-permute-start(bf16[64,1408]{1,0:T(8,128)(2,1)} %get-tuple-element.41), channel_id=1, source_target_pairs={{0,2},{1,3},{2,0},{3,1},{4,6},{5,7},{6,4},{7,5},{8,10},{9,11},{10,... | collective-permute-start | bytes 540680 | tf_op jit(solution)/shard_map/ppermute | solution.py:39
  6.8 9.9 %collective-permute-start = (bf16[64,1408]{1,0:T(8,128)(2,1)}, bf16[64,1408]{1,0:T(8,128)(2,1)S(1)}, u32[]{:S(2)}, u32[]{:S(2)}) collective-permute-start(bf16[64,1408]{1,0:T(8,128)(2,1)} %get-tuple-element.39), channel_id=1, source_target_pairs={{0,1},{1,0},{2,3},{3,2},{4,5},{5,4},{6,7},{7,6},{8,9},{9,8},{10,11... | collective-permute-start | bytes 540680 | tf_op jit(solution)/shard_map/ppermute | solution.py:39
  6.8 10.1 %collective-permute-start.2 = (bf16[64,1408]{1,0:T(8,128)(2,1)}, bf16[64,1408]{1,0:T(8,128)(2,1)S(1)}, u32[]{:S(2)}, u32[]{:S(2)}) collective-permute-start(bf16[64,1408]{1,0:T(8,128)(2,1)} %get-tuple-element.43), channel_id=1, source_target_pairs={{0,3},{1,2},{2,1},{3,0},{4,7},{5,6},{6,5},{7,4},{8,11},{9,10},{10,... | collective-permute-start | bytes 540680 | tf_op jit(solution)/shard_map/ppermute | solution.py:39
  7.0 13.9 %collective-permute-start.4 = (bf16[96,512]{1,0:T(8,128)(2,1)}, bf16[96,512]{1,0:T(8,128)(2,1)S(1)}, u32[]{:S(2)}, u32[]{:S(2)}) collective-permute-start(bf16[96,512]{1,0:T(8,128)(2,1)} %get-tuple-element.52), channel_id=1, source_target_pairs={{0,2},{1,3},{2,4},{3,5},{4,6},{5,7},{6,0},{7,1},{8,10},{9,11},{10,... | collective-permute-start | bytes 294920 | tf_op jit(solution)/shard_map/ppermute | solution.py:34
  9.0 11.9 %collective-permute-start.5 = (bf16[96,512]{1,0:T(8,128)(2,1)}, bf16[96,512]{1,0:T(8,128)(2,1)S(1)}, u32[]{:S(2)}, u32[]{:S(2)}) collective-permute-start(bf16[96,512]{1,0:T(8,128)(2,1)} %get-tuple-element.53), channel_id=1, source_target_pairs={{0,4},{1,5},{2,6},{3,7},{4,0},{5,1},{6,2},{7,3},{8,12},{9,13},{10,... | collective-permute-start | bytes 294920 | tf_op jit(solution)/shard_map/ppermute | solution.py:34
  12.4 3.6 %copy-start.6 = (bf16[80,512]{1,0:T(8,128)(2,1)S(1)}, bf16[80,512]{1,0:T(8,128)(2,1)}, u32[]{:S(2)}) copy-start(bf16[80,512]{1,0:T(8,128)(2,1)} %get-tuple-element.51) | copy-start | bytes 245764
  12.4 4.5 %copy-start.1 = (bf16[64,1408]{1,0:T(8,128)(2,1)S(1)}, bf16[64,1408]{1,0:T(8,128)(2,1)}, u32[]{:S(2)}) copy-start(bf16[64,1408]{1,0:T(8,128)(2,1)} %get-tuple-element.38.refs_0_) | copy-start | bytes 540676
  12.4 14.6 %all-to-all-start = ((bf16[4,64,1024]{2,1,0:T(8,128)(2,1)}), bf16[4,64,1024]{2,1,0:T(8,128)(2,1)S(1)}, u32[]{:S(2)}, u32[]{:S(2)}) async-start(bf16[4,64,1024]{2,1,0:T(8,128)(2,1)} %get-tuple-element.45), calls=%async_computation | async-start | bytes 1048576 | tf_op jit(solution)/shard_map/all_to_all | solution.py:663
  16.1 0.7 %copy-start.7 = (f32[1,128]{1,0:T(1,128)S(1)}, f32[1,128]{1,0:T(1,128)}, u32[]{:S(2)}) copy-start(f32[1,128]{1,0:T(1,128)} %param.20) | copy-start | bytes 1540
  16.1 0.7 %copy-start.8 = (f32[1,128]{1,0:T(1,128)S(1)}, f32[1,128]{1,0:T(1,128)}, u32[]{:S(2)}) copy-start(f32[1,128]{1,0:T(1,128)} %param.18) | copy-start | bytes 1540
  16.1 0.7 %copy-start.9 = (f32[1,128]{1,0:T(1,128)S(1)}, f32[1,128]{1,0:T(1,128)}, u32[]{:S(2)}) copy-start(f32[1,128]{1,0:T(1,128)} %param.19) | copy-start | bytes 1540
  16.1 0.9 %copy-start.2 = (bf16[1,4,8192]{2,1,0:T(4,128)(2,1)S(1)}, bf16[1,4,8192]{2,1,0:T(4,128)(2,1)}, u32[]{:S(2)}) copy-start(bf16[1,4,8192]{2,1,0:T(4,128)(2,1)} %param.21) | copy-start | bytes 196612
  16.7 0.7 %copy-start.4 = (bf16[1,4,1024]{2,1,0:T(4,128)(2,1)S(1)}, bf16[1,4,1024]{2,1,0:T(4,128)(2,1)}, u32[]{:S(2)}) copy-start(bf16[1,4,1024]{2,1,0:T(4,128)(2,1)} %param.22) | copy-start | bytes 24580
  19.8 5.2 %copy-start.5 = (bf16[1,64,2048]{2,1,0:T(8,128)(2,1)S(1)}, bf16[1,64,2048]{2,1,0:T(8,128)(2,1)}, u32[]{:S(2)}) copy-start(bf16[1,64,2048]{2,1,0:T(8,128)(2,1)} %param.25) | copy-start | bytes 786436
  20.9 4.0 %collective-permute-start.6 = (bf16[272,512]{1,0:T(8,128)(2,1)S(1)}, bf16[272,512]{1,0:T(8,128)(2,1)S(1)}, u32[]{:S(2)}, u32[]{:S(2)}) collective-permute-start(bf16[272,512]{1,0:T(8,128)(2,1)S(1)} %constant_dynamic-update-slice_fusion.refs_7_.mine), channel_id=1, source_target_pairs={{0,1},{1,0},{2,3},{3,2},{4,5},{5,4},{6,7},{7,6},{8,9},{9,8},{10,11... | collective-permute-start | bytes 835592 | tf_op jit(solution)/shard_map/ppermute | solution.py:39
  21.0 22.3 %collective-permute-start.3 = (bf16[128,1024]{1,0:T(8,128)(2,1)S(1)}, bf16[128,1024]{1,0:T(8,128)(2,1)S(1)}, u32[]{:S(2)}, u32[]{:S(2)}) collective-permute-start(bf16[128,1024]{1,0:T(8,128)(2,1)S(1)} %get-tuple-element.44), channel_id=1, source_target_pairs={{0,4},{1,5},{2,6},{3,7},{4,0},{5,1},{6,2},{7,3},{8,12},{9,13},{10,... | collective-permute-start | bytes 786440 | tf_op jit(solution)/shard_map/ppermute | solution.py:34
  28.8 19.6 %collective-permute-start.10 = (bf16[128,1024]{1,0:T(8,128)(2,1)S(1)}, bf16[128,1024]{1,0:T(8,128)(2,1)S(1)}, u32[]{:S(2)}, u32[]{:S(2)}) collective-permute-start(bf16[128,1024]{1,0:T(8,128)(2,1)S(1)} %get-tuple-element.65), channel_id=1, source_target_pairs={{0,4},{1,5},{2,6},{3,7},{4,0},{5,1},{6,2},{7,3},{8,12},{9,13},{10,... | collective-permute-start | bytes 786440 | tf_op jit(solution)/shard_map/ppermute | solution.py:34
  43.8 15.9 %copy-start = (bf16[1,64,8192]{2,1,0:T(8,128)(2,1)S(1)}, bf16[1,64,8192]{2,1,0:T(8,128)(2,1)}, u32[]{:S(2)}) copy-start(bf16[1,64,8192]{2,1,0:T(8,128)(2,1)} %param.15) | copy-start | bytes 3145732
  43.8 5.4 %collective-permute-start.7 = (bf16[64,1024]{1,0:T(8,128)(2,1)S(1)}, bf16[64,1024]{1,0:T(8,128)(2,1)S(1)}, u32[]{:S(2)}, u32[]{:S(2)}) collective-permute-start(bf16[64,1024]{1,0:T(8,128)(2,1)S(1)} %get-tuple-element.62), channel_id=1, source_target_pairs={{0,1},{1,0},{2,3},{3,2},{4,5},{5,4},{6,7},{7,6},{8,9},{9,8},{10,11... | collective-permute-start | bytes 393224 | tf_op jit(solution)/shard_map/ppermute | solution.py:39
  43.9 10.4 %collective-permute-start.14 = (bf16[64,2048]{1,0:T(8,128)(2,1)S(1)}, bf16[64,2048]{1,0:T(8,128)(2,1)S(1)}, u32[]{:S(2)}, u32[]{:S(2)}) collective-permute-start(bf16[64,2048]{1,0:T(8,128)(2,1)S(1)} %shard_map.153), channel_id=1, source_target_pairs={{0,8},{8,16},{16,24},{24,0},{1,9},{9,17},{17,25},{25,1},{2,10},{10... | collective-permute-start | bytes 786440 | tf_op jit(solution)/shard_map/ppermute | solution.py:34
  46.4 6.3 %collective-permute-start.8 = (bf16[64,1024]{1,0:T(8,128)(2,1)S(1)}, bf16[64,1024]{1,0:T(8,128)(2,1)S(1)}, u32[]{:S(2)}, u32[]{:S(2)}) collective-permute-start(bf16[64,1024]{1,0:T(8,128)(2,1)S(1)} %get-tuple-element.63), channel_id=1, source_target_pairs={{0,2},{1,3},{2,0},{3,1},{4,6},{5,7},{6,4},{7,5},{8,10},{9,11},{10,... | collective-permute-start | bytes 393224 | tf_op jit(solution)/shard_map/ppermute | solution.py:39
  46.4 7.6 %collective-permute-start.9 = (bf16[64,1024]{1,0:T(8,128)(2,1)S(1)}, bf16[64,1024]{1,0:T(8,128)(2,1)S(1)}, u32[]{:S(2)}, u32[]{:S(2)}) collective-permute-start(bf16[64,1024]{1,0:T(8,128)(2,1)S(1)} %get-tuple-element.64), channel_id=1, source_target_pairs={{0,3},{1,2},{2,1},{3,0},{4,7},{5,6},{6,5},{7,4},{8,11},{9,10},{10,... | collective-permute-start | bytes 393224 | tf_op jit(solution)/shard_map/ppermute | solution.py:39
  48.3 11.3 %copy-start.3 = (f32[1,8192]{1,0:T(1,128)S(1)}, f32[1,8192]{1,0:T(1,128)}, u32[]{:S(2)}) copy-start(f32[1,8192]{1,0:T(1,128)} %refs_9_.1) | copy-start | bytes 98308
  48.8 5.5 %collective-permute-start.11 = (bf16[64,1024]{1,0:T(8,128)(2,1)S(1)}, bf16[64,1024]{1,0:T(8,128)(2,1)S(1)}, u32[]{:S(2)}, u32[]{:S(2)}) collective-permute-start(bf16[64,1024]{1,0:T(8,128)(2,1)S(1)} %get-tuple-element.68), channel_id=1, source_target_pairs={{0,1},{1,0},{2,3},{3,2},{4,5},{5,4},{6,7},{7,6},{8,9},{9,8},{10,11... | collective-permute-start | bytes 393224 | tf_op jit(solution)/shard_map/ppermute | solution.py:39
  49.2 9.2 %collective-permute-start.12 = (bf16[64,1024]{1,0:T(8,128)(2,1)S(1)}, bf16[64,1024]{1,0:T(8,128)(2,1)S(1)}, u32[]{:S(2)}, u32[]{:S(2)}) collective-permute-start(bf16[64,1024]{1,0:T(8,128)(2,1)S(1)} %get-tuple-element.69), channel_id=1, source_target_pairs={{0,2},{1,3},{2,0},{3,1},{4,6},{5,7},{6,4},{7,5},{8,10},{9,11},{10,... | collective-permute-start | bytes 393224 | tf_op jit(solution)/shard_map/ppermute | solution.py:39
  52.8 6.9 %collective-permute-start.13 = (bf16[64,1024]{1,0:T(8,128)(2,1)S(1)}, bf16[64,1024]{1,0:T(8,128)(2,1)S(1)}, u32[]{:S(2)}, u32[]{:S(2)}) collective-permute-start(bf16[64,1024]{1,0:T(8,128)(2,1)S(1)} %get-tuple-element.70), channel_id=1, source_target_pairs={{0,3},{1,2},{2,1},{3,0},{4,7},{5,6},{6,5},{7,4},{8,11},{9,10},{10,... | collective-permute-start | bytes 393224 | tf_op jit(solution)/shard_map/ppermute | solution.py:39

commit v5 on v4

--- a/solution.py
+++ b/solution.py
@@ -700,7 +700,7 @@
     )(pieces_b, conv_x[0], bcc_first, ids_col, writes, *halo)
     per_head = chunk // HD
 
-    def entering(state, first):
+    def entering(state, first, move):
         if blocks > 2:
             same = ids_col[BLK + 7, :] == ids_col[7, :]
             fade = jnp.where(same, decay[0][0, :], 0.0)[first : first + per_head]
@@ -712,10 +712,10 @@
                 state = state + fade * came
                 fade = fade * came_fade
                 far *= 2
-        return turned_on(state, "ctx", share).astype(bf16)
-
-    entry_a = entering(state_a, 0)
-    entry_b = entering(state_b, per_head)
+        return move(state, "ctx", share).astype(bf16)
+
+    entry_a = entering(state_a, 0, turned_on)
+    entry_b = entering(state_b, per_head, shifted)
 
     local_a, local_b, bcc, keep = call(
         functools.partial(mixing_body, share),

time: 61.9 us -> 60.6 us (0.979); the launches traced: 61.4 us -> 59.4 us
  waiting for transfers between devices: 21.3 us -> 10.6 us
  starting transfers between devices: 23.6 us -> 32.2 us
    ppermute x5 -> x4, waiting for transfers between devices: 10.6 us -> 1.96 us  [turned_on(): lax.ppermute(value, axis, [(i, (i + steps) % count) for i in range(count)])]
    ppermute x10, starting transfers between devices: 5.84 us -> 12.9 us  [crossed(): return lax.ppermute(value, axis, [(i, i ^ mask) for i in range(count)])]
    ppermute x0 -> x1, starting transfers between devices: none -> 4.95 us  [shifted(): lax.ppermute(value, axis, [(i, i + steps) for i in range(count - steps)])]
    ppermute x5 -> x4, starting transfers between devices: 14.1 us -> 10.7 us  [turned_on(): lax.ppermute(value, axis, [(i, (i + steps) % count) for i in range(count)])]
    ppermute x10, waiting for transfers between devices: 10.7 us -> 8.69 us  [crossed(): return lax.ppermute(value, axis, [(i, i ^ mask) for i in range(count)])]
  transfers between devices with their start and end apart: 16 -> 16, of which waited for: 10 -> 8; matrix products, arithmetic and copies ran while one was open for 0% -> 0% of each run, Pallas kernels for 16% -> 16%
where the time goes in v5:
time: 60.6 us; the launch traced here: 59.4 us
  starting transfers between devices  32.2 us (53%)
  Pallas kernels  14.5 us (24%)
  waiting for transfers between devices  10.6 us (17%)
  local copies, waits for them, and re-layouts  1.19 us (2%)
  between operations  0.83 us (1%)
    ppermute x10, starting transfers between devices, crossed(): return lax.ppermute(value, axis, [(i, i ^ mask) for i in range(count)])  12.9 us
    ppermute x4, starting transfers between devices, turned_on(): lax.ppermute(value, axis, [(i, (i + steps) % count) for i in range(count)])  10.7 us
    ppermute x10, waiting for transfers between devices, crossed(): return lax.ppermute(value, axis, [(i, i ^ mask) for i in range(count)])  8.69 us
    ppermute x1, starting transfers between devices, shifted(): lax.ppermute(value, axis, [(i, i + steps) for i in range(count - steps)])  4.95 us
    all_to_all x1, starting transfers between devices, on_device(): lax.all_to_all(send_b, 'ctx', 0, 0, tiled=True, axis_index_groups=groups)  3.6 us
    pallas_call x1, Pallas kernels, on_device(): call(functools.partial(pack_body, share), [shape((rows, chunk + 3 * LANES...  3.1 us
    pallas_call x1, Pallas kernels, on_device(): call(functools.partial(mixing_body, share), [shape((BLK, chunk), f32)] *...  2.54 us
    pallas_call x1, Pallas kernels, on_device(): call(functools.partial(first_body, share, blocks > 2), [shape((BLK, chunk...  2.32 us
  transfers between devices with their start and end apart: 16, of which 8 were waited for; matrix products, arithmetic and copies ran while one was open for 0% of the time, Pallas kernels for 16%

profile of v5, /device:TPU:0, one launch (start us, length us, event | category | flops | bytes accessed | tf_op | source)
XLA Modules:
  0.0 59.4 jit_solution(17299283301120355702)
XLA Ops:
  0.6 3.1 %shard_map.149 = (bf16[64,1408]{1,0:T(8,128)(2,1)}, bf16[64,1408]{1,0:T(8,128)(2,1)}, bf16[64,1408]{1,0:T(8,128)(2,1)}, bf16[64,1408]{1,0:T(8,128)(2,1)}, bf16[4...) custom-call(bf16[64,8192]{1,0:T(8,128)(2,1)} %bitcast.18, ...), custom_call_target="tpu_custom_call" | custom-call | bytes 5242880 | tf_op jit(solution)/shard_map/pallas_call | solution.py:626
  3.7 3.1 %collective-permute-start.1 = (bf16[64,1408]{1,0:T(8,128)(2,1)}, bf16[64,1408]{1,0:T(8,128)(2,1)S(1)}, u32[]{:S(2)}, u32[]{:S(2)}) collective-permute-start(bf16[64,1408]{1,0:T(8,128)(2,1)} %get-tuple-element.41), channel_id=1, source_target_pairs={{0,2},{1,3},{2,0},{3,1},{4,6},{5,7},{6,4},{7,5},{8,10},{9,11},{10,... | collective-permute-start | bytes 540680 | tf_op jit(solution)/shard_map/ppermute | solution.py:39
  6.8 0.2 collective-permute-start.2
  7.0 1.9 %collective-permute-start.4 = (bf16[96,512]{1,0:T(8,128)(2,1)}, bf16[96,512]{1,0:T(8,128)(2,1)S(1)}, u32[]{:S(2)}, u32[]{:S(2)}) collective-permute-start(bf16[96,512]{1,0:T(8,128)(2,1)} %get-tuple-element.52), channel_id=1, source_target_pairs={{0,2},{1,3},{2,4},{3,5},{4,6},{5,7},{6,0},{7,1},{8,10},{9,11},{10,... | collective-permute-start | bytes 294920 | tf_op jit(solution)/shard_map/ppermute | solution.py:34
  9.0 2.6 %collective-permute-start.5 = (bf16[96,512]{1,0:T(8,128)(2,1)}, bf16[96,512]{1,0:T(8,128)(2,1)S(1)}, u32[]{:S(2)}, u32[]{:S(2)}) collective-permute-start(bf16[96,512]{1,0:T(8,128)(2,1)} %get-tuple-element.53), channel_id=1, source_target_pairs={{0,4},{1,5},{2,6},{3,7},{4,0},{5,1},{6,2},{7,3},{8,12},{9,13},{10,... | collective-permute-start | bytes 294920 | tf_op jit(solution)/shard_map/ppermute | solution.py:34
  11.6 0.9 %collective-permute-done.1.refs_2_ = bf16[64,1408]{1,0:T(8,128)(2,1)S(1)} collective-permute-done((bf16[64,1408]{1,0:T(8,128)(2,1)}, bf16[64,1408]{1,0:T(8,128)(2,1)S(1)}, u32[]{:S(2)}, u32[]{:S(2)}) %collective-permute-start.1) | collective-permute-done | bytes 180256 | tf_op jit(solution)/shard_map/ppermute | solution.py:39
  12.4 3.6 %all-to-all-start = ((bf16[4,64,1024]{2,1,0:T(8,128)(2,1)}), bf16[4,64,1024]{2,1,0:T(8,128)(2,1)S(1)}, u32[]{:S(2)}, u32[]{:S(2)}) async-start(bf16[4,64,1024]{2,1,0:T(8,128)(2,1)} %get-tuple-element.45), calls=%async_computation | async-start | bytes 1048576 | tf_op jit(solution)/shard_map/all_to_all | solution.py:663
  16.1 0.6 %copy-done.7 = f32[1,128]{1,0:T(1,128)S(1)} copy-done((f32[1,128]{1,0:T(1,128)S(1)}, f32[1,128]{1,0:T(1,128)}, u32[]{:S(2)}) %copy-start.7) | copy-done | bytes 536
  16.8 0.2 collective-permute-done.2.refs_3_
  17.0 0.5 copy-done.4
  17.4 2.3 %shard_map.150 = (bf16[256,1024]{1,0:T(8,128)(2,1)S(1)}, bf16[256,256]{1,0:T(8,128)(2,1)S(1)}, bf16[128,1024]{1,0:T(8,128)(2,1)S(1)}, f32[264,128]{1,0:T(8,128)S(1)}, bf16[256,128]{1,0:T(8,128)(2,1)S(1)}) custom-call(bf16[64,1408]{1,0:T(8,128)(2,1)S(1)} %copy-done.1, bf16[64,1408]{1,0:T(8,128)(2,1)S(1)} %collective-permute-done.refs_1_, ...), custom_call_target="tpu_custom_call" | custom-call | bytes 1024 | tf_op jit(solution)/shard_map/pallas_call | solution.py:671
  19.8 1.1 %collective-permute-done.4 = bf16[96,512]{1,0:T(8,128)(2,1)S(1)} collective-permute-done((bf16[96,512]{1,0:T(8,128)(2,1)}, bf16[96,512]{1,0:T(8,128)(2,1)S(1)}, u32[]{:S(2)}, u32[]{:S(2)}) %collective-permute-start.4) | collective-permute-done | bytes 98336 | tf_op jit(solution)/shard_map/ppermute | solution.py:34
  20.9 0.1 collective-permute-start.6
  21.0 3.9 %collective-permute-start.3 = (bf16[128,1024]{1,0:T(8,128)(2,1)S(1)}, bf16[128,1024]{1,0:T(8,128)(2,1)S(1)}, u32[]{:S(2)}, u32[]{:S(2)}) collective-permute-start(bf16[128,1024]{1,0:T(8,128)(2,1)S(1)} %get-tuple-element.44), channel_id=1, source_target_pairs={{0,4},{1,5},{2,6},{3,7},{4,0},{5,1},{6,2},{7,3},{8,12},{9,13},{10,... | collective-permute-start | bytes 786440 | tf_op jit(solution)/shard_map/ppermute | solution.py:34
  24.9 2.1 %shard_map.153 = bf16[64,2048]{1,0:T(8,128)(2,1)S(1)} custom-call(bf16[64,2048]{1,0:T(8,128)(2,1)S(1)} %bitcast.17, bf16[272,512]{1,0:T(8,128)(2,1)S(1)} %constant_dynamic-update-slice_fusion.refs_7_.mine, bf16[272,512]{1,0:T(8,128)(2,1)S(1)} %collective-permute-done.6.refs_8_.other), custom_call_target="tpu_custom_call" | custom-call | flops 1073741824 | bytes 1048576 | tf_op jit(solution)/shard_map/pallas_call | solution.py:734
  27.1 1.7 %shard_map.151 = (bf16[256,1024]{1,0:T(8,128)(2,1)S(1)}, bf16[128,1024]{1,0:T(8,128)(2,1)S(1)}) custom-call(bf16[4,64,1024]{2,1,0:T(8,128)(2,1)S(1)} %all-to-all-done.refs_0_.refs_4_, bf16[4,8192]{1,0:T(4,128)(2,1)S(1)} %bitcast.13, bf16[256,256]{1,0:T(8,128)(2,1)S(1)} %get-tuple-element.56.refs_2_.refs_11_, f32[264,128]{1,0:T(8,128)S(1)} %get-tuple-element.48.refs_3_, ...), custom_call_target="tpu_custom_call" | custom-call | flops 268435456 | bytes 3145728 | tf_op jit(solution)/shard_map/pallas_call | solution.py:694
  28.8 5.0 %collective-permute-start.10 = (bf16[128,1024]{1,0:T(8,128)(2,1)S(1)}, bf16[128,1024]{1,0:T(8,128)(2,1)S(1)}, u32[]{:S(2)}, u32[]{:S(2)}) collective-permute-start(bf16[128,1024]{1,0:T(8,128)(2,1)S(1)} %get-tuple-element.65), channel_id=1, source_target_pairs={{0,4},{1,5},{2,6},{3,7},{8,12},{9,13},{10,14},{11,15},{16,20},{17,... | collective-permute-start | bytes 786440 | tf_op jit(solution)/shard_map/ppermute | solution.py:29
  33.7 2.5 %shard_map.152 = (f32[256,1024]{1,0:T(8,128)S(1)}, f32[256,1024]{1,0:T(8,128)S(1)}, bf16[256,256]{1,0:T(8,128)(2,1)S(1)}, f32[256,128]{1,0:T(8,128)S(1)}) custom-call(bf16[64,1408]{1,0:T(8,128)(2,1)S(1)} %copy-done.1, bf16[64,1408]{1,0:T(8,128)(2,1)S(1)} %collective-permute-done.refs_1_, bf16[64,1408]{1,0:T(8,128)(2,1)S(1)} %collective-permute-done.1.refs_2_, ...), custom_call_target="tpu_custom_call" | custom-call | flops 2147483648 | bytes 4194304 | tf_op jit(solution)/shard_map/pallas_call | solution.py:720
  36.3 0.8 %collective-permute-done.3.state = bf16[128,1024]{1,0:T(8,128)(2,1)S(1)} collective-permute-done((bf16[128,1024]{1,0:T(8,128)(2,1)S(1)}, bf16[128,1024]{1,0:T(8,128)(2,1)S(1)}, u32[]{:S(2)}, u32[]{:S(2)}) %collective-permute-start.3) | collective-permute-done | bytes 262176 | tf_op jit(solution)/shard_map/ppermute | solution.py:34
  37.1 0.5 shard_map.154
  37.6 0.1 collective-permute-start.7
  37.7 2.2 %collective-permute-start.14 = (bf16[64,2048]{1,0:T(8,128)(2,1)S(1)}, bf16[64,2048]{1,0:T(8,128)(2,1)S(1)}, u32[]{:S(2)}, u32[]{:S(2)}) collective-permute-start(bf16[64,2048]{1,0:T(8,128)(2,1)S(1)} %shard_map.153), channel_id=1, source_target_pairs={{0,8},{8,16},{16,24},{24,0},{1,9},{9,17},{17,25},{25,1},{2,10},{10... | collective-permute-start | bytes 786440 | tf_op jit(solution)/shard_map/ppermute | solution.py:34
  40.0 5.9 %collective-permute-start.8 = (bf16[64,1024]{1,0:T(8,128)(2,1)S(1)}, bf16[64,1024]{1,0:T(8,128)(2,1)S(1)}, u32[]{:S(2)}, u32[]{:S(2)}) collective-permute-start(bf16[64,1024]{1,0:T(8,128)(2,1)S(1)} %get-tuple-element.63), channel_id=1, source_target_pairs={{0,2},{1,3},{2,0},{3,1},{4,6},{5,7},{6,4},{7,5},{8,10},{9,11},{10,... | collective-permute-start | bytes 393224 | tf_op jit(solution)/shard_map/ppermute | solution.py:39
  45.8 0.5 shard_map.155
  46.3 0.2 collective-permute-start.11
  46.6 3.2 %collective-permute-start.12 = (bf16[64,1024]{1,0:T(8,128)(2,1)S(1)}, bf16[64,1024]{1,0:T(8,128)(2,1)S(1)}, u32[]{:S(2)}, u32[]{:S(2)}) collective-permute-start(bf16[64,1024]{1,0:T(8,128)(2,1)S(1)} %get-tuple-element.69), channel_id=1, source_target_pairs={{0,2},{1,3},{2,0},{3,1},{4,6},{5,7},{6,4},{7,5},{8,10},{9,11},{10,... | collective-permute-start | bytes 393224 | tf_op jit(solution)/shard_map/ppermute | solution.py:39
  49.7 0.4 collective-permute-done.8.refs_2_
  50.1 0.2 collective-permute-start.13
  50.3 2.2 %collective-permute-done.9.refs_3_ = bf16[64,1024]{1,0:T(8,128)(2,1)S(1)} collective-permute-done((bf16[64,1024]{1,0:T(8,128)(2,1)S(1)}, bf16[64,1024]{1,0:T(8,128)(2,1)S(1)}, u32[]{:S(2)}, u32[]{:S(2)}) %collective-permute-start.9) | collective-permute-done | bytes 131104 | tf_op jit(solution)/shard_map/ppermute | solution.py:39
  52.5 3.2 %collective-permute-done.12.refs_6_ = bf16[64,1024]{1,0:T(8,128)(2,1)S(1)} collective-permute-done((bf16[64,1024]{1,0:T(8,128)(2,1)S(1)}, bf16[64,1024]{1,0:T(8,128)(2,1)S(1)}, u32[]{:S(2)}, u32[]{:S(2)}) %collective-permute-start.12) | collective-permute-done | bytes 131104 | tf_op jit(solution)/shard_map/ppermute | solution.py:39
  55.7 1.9 %collective-permute-done.13.refs_7_ = bf16[64,1024]{1,0:T(8,128)(2,1)S(1)} collective-permute-done((bf16[64,1024]{1,0:T(8,128)(2,1)S(1)}, bf16[64,1024]{1,0:T(8,128)(2,1)S(1)}, u32[]{:S(2)}, u32[]{:S(2)}) %collective-permute-start.13) | collective-permute-done | bytes 131104 | tf_op jit(solution)/shard_map/ppermute | solution.py:39
  57.6 1.7 %shard_map.156 = (bf16[64,8192]{1,0:T(8,128)(2,1)}, bf16[64,2048]{1,0:T(8,128)(2,1)}) custom-call(bf16[64,1024]{1,0:T(8,128)(2,1)S(1)} %get-tuple-element.61.refs_0_, bf16[64,1024]{1,0:T(8,128)(2,1)S(1)} %collective-permute-done.7.refs_1_, bf16[64,1024]{1,0:T(8,128)(2,1)S(1)} %collective-permute-done.8.refs_2_, ...), custom_call_target="tpu_custom_call" | custom-call | bytes 3145728 | tf_op jit(solution)/shard_map/pallas_call | solution.py:761
  (32 shorter events, 0.1 us)
Async XLA Ops:
  3.7 8.7 %collective-permute-start.1 = (bf16[64,1408]{1,0:T(8,128)(2,1)}, bf16[64,1408]{1,0:T(8,128)(2,1)S(1)}, u32[]{:S(2)}, u32[]{:S(2)}) collective-permute-start(bf16[64,1408]{1,0:T(8,128)(2,1)} %get-tuple-element.41), channel_id=1, source_target_pairs={{0,2},{1,3},{2,0},{3,1},{4,6},{5,7},{6,4},{7,5},{8,10},{9,11},{10,... | collective-permute-start | bytes 540680 | tf_op jit(solution)/shard_map/ppermute | solution.py:39
  6.8 9.9 %collective-permute-start = (bf16[64,1408]{1,0:T(8,128)(2,1)}, bf16[64,1408]{1,0:T(8,128)(2,1)S(1)}, u32[]{:S(2)}, u32[]{:S(2)}) collective-permute-start(bf16[64,1408]{1,0:T(8,128)(2,1)} %get-tuple-element.39), channel_id=1, source_target_pairs={{0,1},{1,0},{2,3},{3,2},{4,5},{5,4},{6,7},{7,6},{8,9},{9,8},{10,11... | collective-permute-start | bytes 540680 | tf_op jit(solution)/shard_map/ppermute | solution.py:39
  6.8 10.1 %collective-permute-start.2 = (bf16[64,1408]{1,0:T(8,128)(2,1)}, bf16[64,1408]{1,0:T(8,128)(2,1)S(1)}, u32[]{:S(2)}, u32[]{:S(2)}) collective-permute-start(bf16[64,1408]{1,0:T(8,128)(2,1)} %get-tuple-element.43), channel_id=1, source_target_pairs={{0,3},{1,2},{2,1},{3,0},{4,7},{5,6},{6,5},{7,4},{8,11},{9,10},{10,... | collective-permute-start | bytes 540680 | tf_op jit(solution)/shard_map/ppermute | solution.py:39
  7.0 13.9 %collective-permute-start.4 = (bf16[96,512]{1,0:T(8,128)(2,1)}, bf16[96,512]{1,0:T(8,128)(2,1)S(1)}, u32[]{:S(2)}, u32[]{:S(2)}) collective-permute-start(bf16[96,512]{1,0:T(8,128)(2,1)} %get-tuple-element.52), channel_id=1, source_target_pairs={{0,2},{1,3},{2,4},{3,5},{4,6},{5,7},{6,0},{7,1},{8,10},{9,11},{10,... | collective-permute-start | bytes 294920 | tf_op jit(solution)/shard_map/ppermute | solution.py:34
  9.0 11.9 %collective-permute-start.5 = (bf16[96,512]{1,0:T(8,128)(2,1)}, bf16[96,512]{1,0:T(8,128)(2,1)S(1)}, u32[]{:S(2)}, u32[]{:S(2)}) collective-permute-start(bf16[96,512]{1,0:T(8,128)(2,1)} %get-tuple-element.53), channel_id=1, source_target_pairs={{0,4},{1,5},{2,6},{3,7},{4,0},{5,1},{6,2},{7,3},{8,12},{9,13},{10,... | collective-permute-start | bytes 294920 | tf_op jit(solution)/shard_map/ppermute | solution.py:34
  12.4 3.6 %copy-start.6 = (bf16[80,512]{1,0:T(8,128)(2,1)S(1)}, bf16[80,512]{1,0:T(8,128)(2,1)}, u32[]{:S(2)}) copy-start(bf16[80,512]{1,0:T(8,128)(2,1)} %get-tuple-element.51) | copy-start | bytes 245764
  12.4 4.5 %copy-start.1 = (bf16[64,1408]{1,0:T(8,128)(2,1)S(1)}, bf16[64,1408]{1,0:T(8,128)(2,1)}, u32[]{:S(2)}) copy-start(bf16[64,1408]{1,0:T(8,128)(2,1)} %get-tuple-element.38.refs_0_) | copy-start | bytes 540676
  12.4 14.6 %all-to-all-start = ((bf16[4,64,1024]{2,1,0:T(8,128)(2,1)}), bf16[4,64,1024]{2,1,0:T(8,128)(2,1)S(1)}, u32[]{:S(2)}, u32[]{:S(2)}) async-start(bf16[4,64,1024]{2,1,0:T(8,128)(2,1)} %get-tuple-element.45), calls=%async_computation | async-start | bytes 1048576 | tf_op jit(solution)/shard_map/all_to_all | solution.py:663
  16.1 0.7 %copy-start.7 = (f32[1,128]{1,0:T(1,128)S(1)}, f32[1,128]{1,0:T(1,128)}, u32[]{:S(2)}) copy-start(f32[1,128]{1,0:T(1,128)} %param.20) | copy-start | bytes 1540
  16.1 0.7 %copy-start.8 = (f32[1,128]{1,0:T(1,128)S(1)}, f32[1,128]{1,0:T(1,128)}, u32[]{:S(2)}) copy-start(f32[1,128]{1,0:T(1,128)} %param.18) | copy-start | bytes 1540
  16.1 0.7 %copy-start.9 = (f32[1,128]{1,0:T(1,128)S(1)}, f32[1,128]{1,0:T(1,128)}, u32[]{:S(2)}) copy-start(f32[1,128]{1,0:T(1,128)} %param.19) | copy-start | bytes 1540
  16.1 0.9 %copy-start.2 = (bf16[1,4,8192]{2,1,0:T(4,128)(2,1)S(1)}, bf16[1,4,8192]{2,1,0:T(4,128)(2,1)}, u32[]{:S(2)}) copy-start(bf16[1,4,8192]{2,1,0:T(4,128)(2,1)} %param.21) | copy-start | bytes 196612
  16.7 0.7 %copy-start.4 = (bf16[1,4,1024]{2,1,0:T(4,128)(2,1)S(1)}, bf16[1,4,1024]{2,1,0:T(4,128)(2,1)}, u32[]{:S(2)}) copy-start(bf16[1,4,1024]{2,1,0:T(4,128)(2,1)} %param.22) | copy-start | bytes 24580
  19.8 5.2 %copy-start.5 = (bf16[1,64,2048]{2,1,0:T(8,128)(2,1)S(1)}, bf16[1,64,2048]{2,1,0:T(8,128)(2,1)}, u32[]{:S(2)}) copy-start(bf16[1,64,2048]{2,1,0:T(8,128)(2,1)} %param.25) | copy-start | bytes 786436
  20.9 4.0 %collective-permute-start.6 = (bf16[272,512]{1,0:T(8,128)(2,1)S(1)}, bf16[272,512]{1,0:T(8,128)(2,1)S(1)}, u32[]{:S(2)}, u32[]{:S(2)}) collective-permute-start(bf16[272,512]{1,0:T(8,128)(2,1)S(1)} %constant_dynamic-update-slice_fusion.refs_7_.mine), channel_id=1, source_target_pairs={{0,1},{1,0},{2,3},{3,2},{4,5},{5,4},{6,7},{7,6},{8,9},{9,8},{10,11... | collective-permute-start | bytes 835592 | tf_op jit(solution)/shard_map/ppermute | solution.py:39
  21.0 16.1 %collective-permute-start.3 = (bf16[128,1024]{1,0:T(8,128)(2,1)S(1)}, bf16[128,1024]{1,0:T(8,128)(2,1)S(1)}, u32[]{:S(2)}, u32[]{:S(2)}) collective-permute-start(bf16[128,1024]{1,0:T(8,128)(2,1)S(1)} %get-tuple-element.44), channel_id=1, source_target_pairs={{0,4},{1,5},{2,6},{3,7},{4,0},{5,1},{6,2},{7,3},{8,12},{9,13},{10,... | collective-permute-start | bytes 786440 | tf_op jit(solution)/shard_map/ppermute | solution.py:34
  28.8 17.1 %collective-permute-start.10 = (bf16[128,1024]{1,0:T(8,128)(2,1)S(1)}, bf16[128,1024]{1,0:T(8,128)(2,1)S(1)}, u32[]{:S(2)}, u32[]{:S(2)}) collective-permute-start(bf16[128,1024]{1,0:T(8,128)(2,1)S(1)} %get-tuple-element.65), channel_id=1, source_target_pairs={{0,4},{1,5},{2,6},{3,7},{8,12},{9,13},{10,14},{11,15},{16,20},{17,... | collective-permute-start | bytes 786440 | tf_op jit(solution)/shard_map/ppermute | solution.py:29
  37.6 20.0 %copy-start = (bf16[1,64,8192]{2,1,0:T(8,128)(2,1)S(1)}, bf16[1,64,8192]{2,1,0:T(8,128)(2,1)}, u32[]{:S(2)}) copy-start(bf16[1,64,8192]{2,1,0:T(8,128)(2,1)} %param.15) | copy-start | bytes 3145732
  37.6 8.9 %collective-permute-start.7 = (bf16[64,1024]{1,0:T(8,128)(2,1)S(1)}, bf16[64,1024]{1,0:T(8,128)(2,1)S(1)}, u32[]{:S(2)}, u32[]{:S(2)}) collective-permute-start(bf16[64,1024]{1,0:T(8,128)(2,1)S(1)} %get-tuple-element.62), channel_id=1, source_target_pairs={{0,1},{1,0},{2,3},{3,2},{4,5},{5,4},{6,7},{7,6},{8,9},{9,8},{10,11... | collective-permute-start | bytes 393224 | tf_op jit(solution)/shard_map/ppermute | solution.py:39
  37.7 14.8 %collective-permute-start.14 = (bf16[64,2048]{1,0:T(8,128)(2,1)S(1)}, bf16[64,2048]{1,0:T(8,128)(2,1)S(1)}, u32[]{:S(2)}, u32[]{:S(2)}) collective-permute-start(bf16[64,2048]{1,0:T(8,128)(2,1)S(1)} %shard_map.153), channel_id=1, source_target_pairs={{0,8},{8,16},{16,24},{24,0},{1,9},{9,17},{17,25},{25,1},{2,10},{10... | collective-permute-start | bytes 786440 | tf_op jit(solution)/shard_map/ppermute | solution.py:34
  40.0 10.1 %collective-permute-start.8 = (bf16[64,1024]{1,0:T(8,128)(2,1)S(1)}, bf16[64,1024]{1,0:T(8,128)(2,1)S(1)}, u32[]{:S(2)}, u32[]{:S(2)}) collective-permute-start(bf16[64,1024]{1,0:T(8,128)(2,1)S(1)} %get-tuple-element.63), channel_id=1, source_target_pairs={{0,2},{1,3},{2,0},{3,1},{4,6},{5,7},{6,4},{7,5},{8,10},{9,11},{10,... | collective-permute-start | bytes 393224 | tf_op jit(solution)/shard_map/ppermute | solution.py:39
  45.8 6.7 %collective-permute-start.9 = (bf16[64,1024]{1,0:T(8,128)(2,1)S(1)}, bf16[64,1024]{1,0:T(8,128)(2,1)S(1)}, u32[]{:S(2)}, u32[]{:S(2)}) collective-permute-start(bf16[64,1024]{1,0:T(8,128)(2,1)S(1)} %get-tuple-element.64), channel_id=1, source_target_pairs={{0,3},{1,2},{2,1},{3,0},{4,7},{5,6},{6,5},{7,4},{8,11},{9,10},{10,... | collective-permute-start | bytes 393224 | tf_op jit(solution)/shard_map/ppermute | solution.py:39
  45.8 11.8 %copy-start.3 = (f32[1,8192]{1,0:T(1,128)S(1)}, f32[1,8192]{1,0:T(1,128)}, u32[]{:S(2)}) copy-start(f32[1,8192]{1,0:T(1,128)} %refs_9_.1) | copy-start | bytes 98308
  46.3 6.2 %collective-permute-start.11 = (bf16[64,1024]{1,0:T(8,128)(2,1)S(1)}, bf16[64,1024]{1,0:T(8,128)(2,1)S(1)}, u32[]{:S(2)}, u32[]{:S(2)}) collective-permute-start(bf16[64,1024]{1,0:T(8,128)(2,1)S(1)} %get-tuple-element.68), channel_id=1, source_target_pairs={{0,1},{1,0},{2,3},{3,2},{4,5},{5,4},{6,7},{7,6},{8,9},{9,8},{10,11... | collective-permute-start | bytes 393224 | tf_op jit(solution)/shard_map/ppermute | solution.py:39
  46.6 9.2 %collective-permute-start.12 = (bf16[64,1024]{1,0:T(8,128)(2,1)S(1)}, bf16[64,1024]{1,0:T(8,128)(2,1)S(1)}, u32[]{:S(2)}, u32[]{:S(2)}) collective-permute-start(bf16[64,1024]{1,0:T(8,128)(2,1)S(1)} %get-tuple-element.69), channel_id=1, source_target_pairs={{0,2},{1,3},{2,0},{3,1},{4,6},{5,7},{6,4},{7,5},{8,10},{9,11},{10,... | collective-permute-start | bytes 393224 | tf_op jit(solution)/shard_map/ppermute | solution.py:39
  50.1 7.5 %collective-permute-start.13 = (bf16[64,1024]{1,0:T(8,128)(2,1)S(1)}, bf16[64,1024]{1,0:T(8,128)(2,1)S(1)}, u32[]{:S(2)}, u32[]{:S(2)}) collective-permute-start(bf16[64,1024]{1,0:T(8,128)(2,1)S(1)} %get-tuple-element.70), channel_id=1, source_target_pairs={{0,3},{1,2},{2,1},{3,0},{4,7},{5,6},{6,5},{7,4},{8,11},{9,10},{10,... | collective-permute-start | bytes 393224 | tf_op jit(solution)/shard_map/ppermute | solution.py:39
